TPU v7x, 512 devices: a whole 4x8x8 slice. The times are simulated.
512 devices in a mesh: slab: 64 (over y, z_hi, x), field: 8 (over z_lo, core).
Axes of the slice: x: 4, y: 8, z: 8 (z_hi: 2, z_lo: 4; z = z_hi * 4 + z_lo), core: 2. Of those that a mesh axis runs over, the one named last changes fastest.
Arguments:
- conform: float32 [3, 256, 1024, 128], P(None, 'field', 'slab'), may hold values from -6 to 6
- velocity: float32 [2, 1024, 128], P(None, 'slab'), may hold values from -0.9 to 2.1
- solid_mask: int32 [1024, 128], P('slab'), may hold values from 0 to 1, as said below
- upwind: int32 [2, 1024, 128], P(None, 'slab'), may hold values from 0 to 1
- relax_time: float32 [256], P('field'), may hold values from 0.5 to 5
- wiener: bfloat16 [6, 3, 256, 1024, 128], P(None, None, 'field', 'slab'), may hold values from -6 to 6
Outputs:
- fields_out: float32 [3, 256, 1024, 128], P(None, 'field', 'slab')
- velocity_out: float32 [2, 1024, 128], P(None, 'slab')
Inputs may be any that keep to these rules, and one draw needn't show every extreme that they name: `solid_mask`: each aligned 32 by 32 tile of cells holds one disc of radius 3 to 9; at least 70 percent of cells are fluid. `upwind`: 1 takes the difference toward the lower neighbour, 0 toward the higher.
All inputs are finite; a program needn't handle non-finite values.
Results may differ from a plain program's by a relative error of at most 0.0003.
Values may be sent and summed in bfloat16 or wider, within the bound.
No kernel may reach another device: no remote copies, remote signals or barrier semaphores. Data moves between devices by JAX's collectives and lax.ppermute only.
A program may use at most 64 MiB of HBM per device.

v0:
```python
import jax
import jax.numpy as jnp
from jax import lax
from jax.sharding import PartitionSpec as P

FIELDS = 256
STEPS = 2
SUBS = 3


sub_step = 0.1
macro_step = 0.3
viscosity = 0.5
modulus = 4.0
target_flow = 0.8


def extended_2(array, sides, width):
    for axis, dim in sides:
        count, length = (lax.axis_size(axis), array.shape[dim])
        up = [(i, (i + 1) % count) for i in range(count)]
        down = [(j, i) for i, j in up]
        last = lax.slice_in_dim(array, length - width, length, axis=dim)
        leading = lax.slice_in_dim(array, 0, width, axis=dim)
        before = lax.ppermute(last, axis, up)
        after = lax.ppermute(leading, axis, down)
        array = jnp.concatenate([before, array, after], axis=dim)
    return array


def advance(extended, speed, flags, kicks, decay, spread):
    center = extended[:, :, 1:-1]
    back_x = center - extended[:, :, :-2]
    ahead_x = extended[:, :, 2:] - center
    slope_x = jnp.where(flags[0] == 1, back_x, ahead_x)
    back_y = center - jnp.roll(center, 1, 3)
    ahead_y = jnp.roll(center, -1, 3) - center
    slope_y = jnp.where(flags[1] == 1, back_y, ahead_y)
    middle = speed[:, 1:-1]
    grad_x = (speed[:, 2:] - speed[:, :-2]) * 0.5
    grad_y = (jnp.roll(middle, -1, 2) - jnp.roll(middle, 1, 2)) * 0.5
    transport = middle[0] * slope_x + middle[1] * slope_y
    comp_x = center[0]
    comp_y = center[1]
    stretch = jnp.stack(
        [
            grad_x[0] * comp_x + grad_y[0] * comp_y,
            grad_x[1] * comp_x + grad_y[1] * comp_y,
            jnp.zeros_like(comp_x),
        ]
    )
    return center + sub_step * (stretch - transport - decay * center) + spread * kicks


def update(speed_wide, stress_wide, fluid, mean_flow):
    middle = speed_wide[:, 1:-1]
    laplace = (
        speed_wide[:, 2:]
        + speed_wide[:, :-2]
        + jnp.roll(middle, 1, 2)
        + jnp.roll(middle, -1, 2)
        - 4.0 * middle
    )
    inner = stress_wide[:, 1:-1]
    div_x = (stress_wide[0, 2:] - stress_wide[0, :-2]) * 0.5 + (
        jnp.roll(inner[1], -1, 1) - jnp.roll(inner[1], 1, 1)
    ) * 0.5
    div_y = (stress_wide[1, 2:] - stress_wide[1, :-2]) * 0.5 + (
        jnp.roll(inner[2], -1, 1) - jnp.roll(inner[2], 1, 1)
    ) * 0.5
    new_x = middle[0] + macro_step * (div_x + viscosity * laplace[0]) + (target_flow - mean_flow)
    new_y = middle[1] + macro_step * (div_y + viscosity * laplace[1])
    return fluid * jnp.stack([new_x, new_y])


def per_device(conform, velocity, solid_mask, upwind, relax_time, wiener):
    fluid = (1 - solid_mask).astype(jnp.float32)
    decay = (0.5 / relax_time)[:, None, None]
    spread = jnp.sqrt(sub_step / relax_time)[:, None, None]
    fields = conform
    speed = velocity
    for step_index in range(STEPS):
        first = step_index * SUBS
        speed_wide = extended_2(speed, (("slab", 1),), 1)
        for sub_index in range(SUBS):
            extended = extended_2(fields, (("slab", 2),), 1)
            kicks = wiener[first + sub_index].astype(jnp.float32)
            fields = advance(extended, speed_wide, upwind, kicks, decay, spread)
        comp_x = fields[0]
        comp_y = fields[1]
        partial_value = jnp.stack(
            [
                jnp.sum(comp_x * comp_x, axis=0),
                jnp.sum(comp_x * comp_y, axis=0),
                jnp.sum(comp_y * comp_y, axis=0),
            ]
        )
        summed = lax.psum(partial_value, "field")
        stress = (
            modulus / FIELDS * summed
            - jnp.array([modulus, 0.0, modulus], jnp.float32)[:, None, None]
        )
        stress_wide = extended_2(stress, (("slab", 1),), 1)
        flow_sum, fluid_count = lax.psum((jnp.sum(fluid * speed[0]), jnp.sum(fluid)), "slab")
        mean_flow = flow_sum / fluid_count
        speed = update(speed_wide, stress_wide, fluid, mean_flow)
    return (fields, speed)


def solution(mesh):
    placed = (
        P(None, "field", "slab", None),
        P(None, "slab", None),
        P("slab", None),
        P(None, "slab", None),
        P("field"),
        P(None, None, "field", "slab", None),
    )
    return jax.shard_map(
        per_device,
        mesh=mesh,
        in_specs=placed,
        out_specs=(P(None, "field", "slab", None), P(None, "slab", None)),
        check_vma=False,
    )
```

profile of v0, /device:TPU:1, one launch (start us, length us, event | category | flops | bytes accessed | tf_op | source)
XLA Modules:
  0.0 674.8 jit_solution(6821522083587706207)
XLA Ops:
  1.4 3.9 collective-permute-start.1
  5.4 14.5 %collective-permute-start = (f32[2,1,128]{2,1,0:T(1,128)S(1)}, f32[2,1,128]{2,1,0:T(1,128)S(1)}, u32[]{:S(2)}, u32[]{:S(2)}) collective-permute-start(f32[2,1,128]{2,1,0:T(1,128)S(1)} %get-tuple-element.95), channel_id=1, source_target_pairs={{8,0},{16,8},{24,16},{32,24},{40,32},{48,40},{56,48},{64,56},{72,6... | collective-permute-start | bytes 3080 | tf_op jit(solution)/shard_map/ppermute | solution.py:26
  21.1 1.9 collective-permute-start.2
  23.0 11.5 %collective-permute-start.3 = (f32[3,32,1,128]{3,2,1,0:T(1,128)S(1)}, f32[3,32,1,128]{3,2,1,0:T(1,128)S(1)}, u32[]{:S(2)}, u32[]{:S(2)}) collective-permute-start(f32[3,32,1,128]{3,2,1,0:T(1,128)S(1)} %get-tuple-element.59), channel_id=1, source_target_pairs={{8,0},{16,8},{24,16},{32,24},{40,32},{48,40},{56,48},{64,56},{72,6... | collective-permute-start | bytes 147464 | tf_op jit(solution)/shard_map/ppermute | solution.py:26
  37.0 1.8 fusion.106
  40.7 188.3 %all-reduce = (f32[]{:T(128)}, f32[]{:T(128)}) all-reduce(f32[]{:T(128)} %get-tuple-element.9, f32[]{:T(128)} %get-tuple-element.8), channel_id=1, replica_groups=mesh['slab'=64,'field'=8] {'slab'}, use_global_device_ids=true, to_apply=%region_5.6 | all-reduce | flops 2 | bytes 16 | tf_op jit(solution)/shard_map/psum | solution.py:104
  230.6 2.2 fusion.58
  233.5 3.3 collective-permute-start.4
  236.8 10.1 %collective-permute-start.5 = (f32[3,32,1,128]{3,2,1,0:T(1,128)S(1)}, f32[3,32,1,128]{3,2,1,0:T(1,128)S(1)}, u32[]{:S(2)}, u32[]{:S(2)}) collective-permute-start(f32[3,32,1,128]{3,2,1,0:T(1,128)S(1)} %get-tuple-element.51), channel_id=1, source_target_pairs={{8,0},{16,8},{24,16},{32,24},{40,32},{48,40},{56,48},{64,56},{72,6... | collective-permute-start | bytes 147464 | tf_op jit(solution)/shard_map/ppermute | solution.py:26
  248.1 2.0 fusion.48
  250.7 1.9 collective-permute-start.6
  252.6 12.2 %collective-permute-start.7 = (f32[3,32,1,128]{3,2,1,0:T(1,128)S(1)}, f32[3,32,1,128]{3,2,1,0:T(1,128)S(1)}, u32[]{:S(2)}, u32[]{:S(2)}) collective-permute-start(f32[3,32,1,128]{3,2,1,0:T(1,128)S(1)} %get-tuple-element.43), channel_id=1, source_target_pairs={{8,0},{16,8},{24,16},{32,24},{40,32},{48,40},{56,48},{64,56},{72,6... | collective-permute-start | bytes 147464 | tf_op jit(solution)/shard_map/ppermute | solution.py:26
  266.0 2.0 fusion.38
  268.0 53.8 %psum.38 = f32[3,16,128]{2,1,0:T(8,128)S(1)} all-reduce(f32[3,16,128]{2,1,0:T(8,128)S(1)} %pad_maximum_fusion.12), channel_id=1, replica_groups=mesh['slab'=64,'field'=8] {'field'}, use_global_device_ids=true, to_apply=%region_3.4 | all-reduce | flops 6144 | bytes 49152 | tf_op jit(solution)/shard_map/psum | solution.py:98
  323.5 12.1 %collective-permute-start.8 = (f32[3,1,128]{2,1,0:T(1,128)S(1)}, f32[3,1,128]{2,1,0:T(1,128)S(1)}, u32[]{:S(2)}, u32[]{:S(2)}) collective-permute-start(f32[3,1,128]{2,1,0:T(1,128)S(1)} %get-tuple-element.70), channel_id=1, source_target_pairs={{8,0},{16,8},{24,16},{32,24},{40,32},{48,40},{56,48},{64,56},{72,6... | collective-permute-start | bytes 4616 | tf_op jit(solution)/shard_map/ppermute | solution.py:26
  335.6 1.9 collective-permute-start.9
  337.6 1.9 collective-permute-start.12
  339.6 11.5 %collective-permute-start.13 = (f32[3,32,1,128]{3,2,1,0:T(1,128)S(1)}, f32[3,32,1,128]{3,2,1,0:T(1,128)S(1)}, u32[]{:S(2)}, u32[]{:S(2)}) collective-permute-start(f32[3,32,1,128]{3,2,1,0:T(1,128)S(1)} %get-tuple-element.35), channel_id=1, source_target_pairs={{8,0},{16,8},{24,16},{32,24},{40,32},{48,40},{56,48},{64,56},{72,6... | collective-permute-start | bytes 147464 | tf_op jit(solution)/shard_map/ppermute | solution.py:26
  352.2 1.9 collective-permute-start.11
  354.1 11.5 %collective-permute-start.10 = (f32[2,1,128]{2,1,0:T(1,128)S(1)}, f32[2,1,128]{2,1,0:T(1,128)S(1)}, u32[]{:S(2)}, u32[]{:S(2)}) collective-permute-start(f32[2,1,128]{2,1,0:T(1,128)S(1)} %get-tuple-element.81), channel_id=1, source_target_pairs={{8,0},{16,8},{24,16},{32,24},{40,32},{48,40},{56,48},{64,56},{72,6... | collective-permute-start | bytes 3080 | tf_op jit(solution)/shard_map/ppermute | solution.py:26
  365.6 188.0 %psum.42 = f32[]{:T(128)} all-reduce(f32[]{:T(128)} %multiply_reduce_fusion.6), channel_id=1, replica_groups=mesh['slab'=64,'field'=8] {'slab'}, use_global_device_ids=true, to_apply=%region_13.14 | all-reduce | flops 1 | bytes 8 | tf_op jit(solution)/shard_map/psum | solution.py:104
  555.1 2.2 fusion.28
  557.9 3.0 collective-permute-start.14
  561.0 10.4 %collective-permute-start.15 = (f32[3,32,1,128]{3,2,1,0:T(1,128)S(1)}, f32[3,32,1,128]{3,2,1,0:T(1,128)S(1)}, u32[]{:S(2)}, u32[]{:S(2)}) collective-permute-start(f32[3,32,1,128]{3,2,1,0:T(1,128)S(1)} %get-tuple-element.27), channel_id=1, source_target_pairs={{8,0},{16,8},{24,16},{32,24},{40,32},{48,40},{56,48},{64,56},{72,6... | collective-permute-start | bytes 147464 | tf_op jit(solution)/shard_map/ppermute | solution.py:26
  572.5 2.0 fusion.18
  575.1 1.9 collective-permute-start.16
  577.1 11.8 %collective-permute-start.17 = (f32[3,32,1,128]{3,2,1,0:T(1,128)S(1)}, f32[3,32,1,128]{3,2,1,0:T(1,128)S(1)}, u32[]{:S(2)}, u32[]{:S(2)}) collective-permute-start(f32[3,32,1,128]{3,2,1,0:T(1,128)S(1)} %get-tuple-element.19), channel_id=1, source_target_pairs={{8,0},{16,8},{24,16},{32,24},{40,32},{48,40},{56,48},{64,56},{72,6... | collective-permute-start | bytes 147464 | tf_op jit(solution)/shard_map/ppermute | solution.py:26
  590.0 2.0 fusion.8
  592.1 57.1 %psum.41 = f32[3,16,128]{2,1,0:T(8,128)S(1)} all-reduce(f32[3,16,128]{2,1,0:T(8,128)S(1)} %pad_maximum_fusion.13), channel_id=1, replica_groups=mesh['slab'=64,'field'=8] {'field'}, use_global_device_ids=true, to_apply=%region_11.12 | all-reduce | flops 6144 | bytes 49152 | tf_op jit(solution)/shard_map/psum | solution.py:98
  649.3 12.1 %collective-permute-start.18 = (f32[3,1,128]{2,1,0:T(1,128)S(1)}, f32[3,1,128]{2,1,0:T(1,128)S(1)}, u32[]{:S(2)}, u32[]{:S(2)}) collective-permute-start(f32[3,1,128]{2,1,0:T(1,128)S(1)} %get-tuple-element.66), channel_id=1, source_target_pairs={{8,0},{16,8},{24,16},{32,24},{40,32},{48,40},{56,48},{64,56},{72,6... | collective-permute-start | bytes 4616 | tf_op jit(solution)/shard_map/ppermute | solution.py:26
  661.4 1.9 collective-permute-start.19
  663.5 10.4 %collective-permute-done.19 = f32[3,1,128]{2,1,0:T(1,128)S(1)} collective-permute-done((f32[3,1,128]{2,1,0:T(1,128)S(1)}, f32[3,1,128]{2,1,0:T(1,128)S(1)}, u32[]{:S(2)}, u32[]{:S(2)}) %collective-permute-start.19) | collective-permute-done | bytes 1568 | tf_op jit(solution)/shard_map/ppermute | solution.py:25
  (99 shorter events, 17.9 us)
Async XLA Ops:
  0.6 38.2 %copy-start = (f32[3,32,16,128]{3,2,1,0:T(8,128)S(1)}, f32[3,32,16,128]{3,2,1,0:T(8,128)}, u32[]{:S(2)}) copy-start(f32[3,32,16,128]{3,2,1,0:T(8,128)} %param.8) | copy-start | bytes 2359300
  1.4 229.0 %collective-permute-start.1 = (f32[2,1,128]{2,1,0:T(1,128)S(1)}, f32[2,1,128]{2,1,0:T(1,128)S(1)}, u32[]{:S(2)}, u32[]{:S(2)}) collective-permute-start(f32[2,1,128]{2,1,0:T(1,128)S(1)} %get-tuple-element.94), channel_id=1, source_target_pairs={{0,8},{8,16},{16,24},{24,32},{32,40},{40,48},{48,56},{56,64},{64,7... | collective-permute-start | bytes 3080 | tf_op jit(solution)/shard_map/ppermute | solution.py:25
  5.4 225.1 %collective-permute-start = (f32[2,1,128]{2,1,0:T(1,128)S(1)}, f32[2,1,128]{2,1,0:T(1,128)S(1)}, u32[]{:S(2)}, u32[]{:S(2)}) collective-permute-start(f32[2,1,128]{2,1,0:T(1,128)S(1)} %get-tuple-element.95), channel_id=1, source_target_pairs={{8,0},{16,8},{24,16},{32,24},{40,32},{48,40},{56,48},{64,56},{72,6... | collective-permute-start | bytes 3080 | tf_op jit(solution)/shard_map/ppermute | solution.py:26
  21.1 209.5 %collective-permute-start.2 = (f32[3,32,1,128]{3,2,1,0:T(1,128)S(1)}, f32[3,32,1,128]{3,2,1,0:T(1,128)S(1)}, u32[]{:S(2)}, u32[]{:S(2)}) collective-permute-start(f32[3,32,1,128]{3,2,1,0:T(1,128)S(1)} %get-tuple-element.58), channel_id=1, source_target_pairs={{0,8},{8,16},{16,24},{24,32},{32,40},{40,48},{48,56},{56,64},{64,7... | collective-permute-start | bytes 147464 | tf_op jit(solution)/shard_map/ppermute | solution.py:25
  23.0 207.6 %collective-permute-start.3 = (f32[3,32,1,128]{3,2,1,0:T(1,128)S(1)}, f32[3,32,1,128]{3,2,1,0:T(1,128)S(1)}, u32[]{:S(2)}, u32[]{:S(2)}) collective-permute-start(f32[3,32,1,128]{3,2,1,0:T(1,128)S(1)} %get-tuple-element.59), channel_id=1, source_target_pairs={{8,0},{16,8},{24,16},{32,24},{40,32},{48,40},{56,48},{64,56},{72,6... | collective-permute-start | bytes 147464 | tf_op jit(solution)/shard_map/ppermute | solution.py:26
  37.0 3.0 copy-start.6
  38.8 1.2 copy-start.4
  38.8 1.2 copy-start.3
  38.9 1.2 copy-start.2
  233.5 13.5 %collective-permute-start.4 = (f32[3,32,1,128]{3,2,1,0:T(1,128)S(1)}, f32[3,32,1,128]{3,2,1,0:T(1,128)S(1)}, u32[]{:S(2)}, u32[]{:S(2)}) collective-permute-start(f32[3,32,1,128]{3,2,1,0:T(1,128)S(1)} %get-tuple-element.50), channel_id=1, source_target_pairs={{0,8},{8,16},{16,24},{24,32},{32,40},{40,48},{48,56},{56,64},{64,7... | collective-permute-start | bytes 147464 | tf_op jit(solution)/shard_map/ppermute | solution.py:25
  236.8 11.3 %collective-permute-start.5 = (f32[3,32,1,128]{3,2,1,0:T(1,128)S(1)}, f32[3,32,1,128]{3,2,1,0:T(1,128)S(1)}, u32[]{:S(2)}, u32[]{:S(2)}) collective-permute-start(f32[3,32,1,128]{3,2,1,0:T(1,128)S(1)} %get-tuple-element.51), channel_id=1, source_target_pairs={{8,0},{16,8},{24,16},{32,24},{40,32},{48,40},{56,48},{64,56},{72,6... | collective-permute-start | bytes 147464 | tf_op jit(solution)/shard_map/ppermute | solution.py:26
  250.7 14.2 %collective-permute-start.6 = (f32[3,32,1,128]{3,2,1,0:T(1,128)S(1)}, f32[3,32,1,128]{3,2,1,0:T(1,128)S(1)}, u32[]{:S(2)}, u32[]{:S(2)}) collective-permute-start(f32[3,32,1,128]{3,2,1,0:T(1,128)S(1)} %get-tuple-element.42), channel_id=1, source_target_pairs={{0,8},{8,16},{16,24},{24,32},{32,40},{40,48},{48,56},{56,64},{64,7... | collective-permute-start | bytes 147464 | tf_op jit(solution)/shard_map/ppermute | solution.py:25
  252.6 13.4 %collective-permute-start.7 = (f32[3,32,1,128]{3,2,1,0:T(1,128)S(1)}, f32[3,32,1,128]{3,2,1,0:T(1,128)S(1)}, u32[]{:S(2)}, u32[]{:S(2)}) collective-permute-start(f32[3,32,1,128]{3,2,1,0:T(1,128)S(1)} %get-tuple-element.43), channel_id=1, source_target_pairs={{8,0},{16,8},{24,16},{32,24},{40,32},{48,40},{56,48},{64,56},{72,6... | collective-permute-start | bytes 147464 | tf_op jit(solution)/shard_map/ppermute | solution.py:26
  266.0 55.9 %copy-start.5 = (f32[3]{0:T(128)S(1)}, f32[3]{0:T(128)}, u32[]{:S(2)}) copy-start(f32[3]{0:T(128)} %constant.32) | copy-start | bytes 40
  323.5 27.6 %collective-permute-start.8 = (f32[3,1,128]{2,1,0:T(1,128)S(1)}, f32[3,1,128]{2,1,0:T(1,128)S(1)}, u32[]{:S(2)}, u32[]{:S(2)}) collective-permute-start(f32[3,1,128]{2,1,0:T(1,128)S(1)} %get-tuple-element.70), channel_id=1, source_target_pairs={{8,0},{16,8},{24,16},{32,24},{40,32},{48,40},{56,48},{64,56},{72,6... | collective-permute-start | bytes 4616 | tf_op jit(solution)/shard_map/ppermute | solution.py:26
  335.6 15.5 %collective-permute-start.9 = (f32[3,1,128]{2,1,0:T(1,128)S(1)}, f32[3,1,128]{2,1,0:T(1,128)S(1)}, u32[]{:S(2)}, u32[]{:S(2)}) collective-permute-start(f32[3,1,128]{2,1,0:T(1,128)S(1)} %get-tuple-element.71), channel_id=1, source_target_pairs={{0,8},{8,16},{16,24},{24,32},{32,40},{40,48},{48,56},{56,64},{64,7... | collective-permute-start | bytes 4616 | tf_op jit(solution)/shard_map/ppermute | solution.py:25
  337.6 217.5 %collective-permute-start.12 = (f32[3,32,1,128]{3,2,1,0:T(1,128)S(1)}, f32[3,32,1,128]{3,2,1,0:T(1,128)S(1)}, u32[]{:S(2)}, u32[]{:S(2)}) collective-permute-start(f32[3,32,1,128]{3,2,1,0:T(1,128)S(1)} %get-tuple-element.34), channel_id=1, source_target_pairs={{0,8},{8,16},{16,24},{24,32},{32,40},{40,48},{48,56},{56,64},{64,7... | collective-permute-start | bytes 147464 | tf_op jit(solution)/shard_map/ppermute | solution.py:25
  339.6 215.6 %collective-permute-start.13 = (f32[3,32,1,128]{3,2,1,0:T(1,128)S(1)}, f32[3,32,1,128]{3,2,1,0:T(1,128)S(1)}, u32[]{:S(2)}, u32[]{:S(2)}) collective-permute-start(f32[3,32,1,128]{3,2,1,0:T(1,128)S(1)} %get-tuple-element.35), channel_id=1, source_target_pairs={{8,0},{16,8},{24,16},{32,24},{40,32},{48,40},{56,48},{64,56},{72,6... | collective-permute-start | bytes 147464 | tf_op jit(solution)/shard_map/ppermute | solution.py:26
  352.2 202.7 %collective-permute-start.11 = (f32[2,1,128]{2,1,0:T(1,128)S(1)}, f32[2,1,128]{2,1,0:T(1,128)S(1)}, u32[]{:S(2)}, u32[]{:S(2)}) collective-permute-start(f32[2,1,128]{2,1,0:T(1,128)S(1)} %get-tuple-element.80), channel_id=1, source_target_pairs={{0,8},{8,16},{16,24},{24,32},{32,40},{40,48},{48,56},{56,64},{64,7... | collective-permute-start | bytes 3080 | tf_op jit(solution)/shard_map/ppermute | solution.py:25
  354.1 200.8 %collective-permute-start.10 = (f32[2,1,128]{2,1,0:T(1,128)S(1)}, f32[2,1,128]{2,1,0:T(1,128)S(1)}, u32[]{:S(2)}, u32[]{:S(2)}) collective-permute-start(f32[2,1,128]{2,1,0:T(1,128)S(1)} %get-tuple-element.81), channel_id=1, source_target_pairs={{8,0},{16,8},{24,16},{32,24},{40,32},{48,40},{56,48},{64,56},{72,6... | collective-permute-start | bytes 3080 | tf_op jit(solution)/shard_map/ppermute | solution.py:26
  557.9 13.5 %collective-permute-start.14 = (f32[3,32,1,128]{3,2,1,0:T(1,128)S(1)}, f32[3,32,1,128]{3,2,1,0:T(1,128)S(1)}, u32[]{:S(2)}, u32[]{:S(2)}) collective-permute-start(f32[3,32,1,128]{3,2,1,0:T(1,128)S(1)} %get-tuple-element.26), channel_id=1, source_target_pairs={{0,8},{8,16},{16,24},{24,32},{32,40},{40,48},{48,56},{56,64},{64,7... | collective-permute-start | bytes 147464 | tf_op jit(solution)/shard_map/ppermute | solution.py:25
  561.0 11.5 %collective-permute-start.15 = (f32[3,32,1,128]{3,2,1,0:T(1,128)S(1)}, f32[3,32,1,128]{3,2,1,0:T(1,128)S(1)}, u32[]{:S(2)}, u32[]{:S(2)}) collective-permute-start(f32[3,32,1,128]{3,2,1,0:T(1,128)S(1)} %get-tuple-element.27), channel_id=1, source_target_pairs={{8,0},{16,8},{24,16},{32,24},{40,32},{48,40},{56,48},{64,56},{72,6... | collective-permute-start | bytes 147464 | tf_op jit(solution)/shard_map/ppermute | solution.py:26
  575.1 13.8 %collective-permute-start.16 = (f32[3,32,1,128]{3,2,1,0:T(1,128)S(1)}, f32[3,32,1,128]{3,2,1,0:T(1,128)S(1)}, u32[]{:S(2)}, u32[]{:S(2)}) collective-permute-start(f32[3,32,1,128]{3,2,1,0:T(1,128)S(1)} %get-tuple-element.18), channel_id=1, source_target_pairs={{0,8},{8,16},{16,24},{24,32},{32,40},{40,48},{48,56},{56,64},{64,7... | collective-permute-start | bytes 147464 | tf_op jit(solution)/shard_map/ppermute | solution.py:25
  577.1 13.0 %collective-permute-start.17 = (f32[3,32,1,128]{3,2,1,0:T(1,128)S(1)}, f32[3,32,1,128]{3,2,1,0:T(1,128)S(1)}, u32[]{:S(2)}, u32[]{:S(2)}) collective-permute-start(f32[3,32,1,128]{3,2,1,0:T(1,128)S(1)} %get-tuple-element.19), channel_id=1, source_target_pairs={{8,0},{16,8},{24,16},{32,24},{40,32},{48,40},{56,48},{64,56},{72,6... | collective-permute-start | bytes 147464 | tf_op jit(solution)/shard_map/ppermute | solution.py:26
  592.0 82.8 %copy-start.1 = (f32[3,32,16,128]{3,2,1,0:T(8,128)}, f32[3,32,16,128]{3,2,1,0:T(8,128)S(1)}, u32[]{:S(2)}) copy-start(f32[3,32,16,128]{3,2,1,0:T(8,128)S(1)} %fusion.8) | copy-start | bytes 2359300
  649.3 14.2 %collective-permute-start.18 = (f32[3,1,128]{2,1,0:T(1,128)S(1)}, f32[3,1,128]{2,1,0:T(1,128)S(1)}, u32[]{:S(2)}, u32[]{:S(2)}) collective-permute-start(f32[3,1,128]{2,1,0:T(1,128)S(1)} %get-tuple-element.66), channel_id=1, source_target_pairs={{8,0},{16,8},{24,16},{32,24},{40,32},{48,40},{56,48},{64,56},{72,6... | collective-permute-start | bytes 4616 | tf_op jit(solution)/shard_map/ppermute | solution.py:26
  661.4 12.4 %collective-permute-start.19 = (f32[3,1,128]{2,1,0:T(1,128)S(1)}, f32[3,1,128]{2,1,0:T(1,128)S(1)}, u32[]{:S(2)}, u32[]{:S(2)}) collective-permute-start(f32[3,1,128]{2,1,0:T(1,128)S(1)} %get-tuple-element.67), channel_id=1, source_target_pairs={{0,8},{8,16},{16,24},{24,32},{32,40},{40,48},{48,56},{56,64},{64,7... | collective-permute-start | bytes 4616 | tf_op jit(solution)/shard_map/ppermute | solution.py:25
where the time goes:
time: 677 us; the launch traced here: 675 us
  blocking collectives  487 us (72%)
  starting transfers between devices  141 us (21%)
  other arithmetic  15.3 us (2%)
  waiting for transfers between devices  14.7 us (2%)
  local copies, waits for them, and re-layouts  12.3 us (2%)
    psum x2, blocking collectives, per_device(): lax.psum((jnp.sum(fluid * speed[0]), jnp.sum(fluid)), 'slab')  376 us
    ppermute x10, starting transfers between devices, extended_2(): after = lax.ppermute(leading, axis, down)  118 us
    psum x2, blocking collectives, per_device(): summed = lax.psum(partial_value, 'field')  111 us
    ppermute x10, starting transfers between devices, extended_2(): before = lax.ppermute(last, axis, up)  23.7 us
  transfers between devices with their start and end apart: 20, of which 5 were waited for; matrix products, arithmetic and copies ran while one was open for 1% of the time, Pallas kernels for 0%

commit v1 on v0

v1 whole, which is shorter than its diff:
```python
import functools
import jax
import jax.numpy as jnp
from jax import lax
from jax.experimental import pallas as pl
from jax.experimental.pallas import tpu as pltpu
from jax.sharding import PartitionSpec as P

STEPS = 2
SUBS = 3
ROWS = 16
LANES = 128

sub_step = 0.1
macro_step = 0.3
viscosity = 0.5
modulus = 4.0
target_flow = 0.8

TRACKS = 3 * SUBS + 2
SENT = 3 * SUBS + 3 + 4
KEPT = 0.85
EXTRA = 16
TOP_ROW = ROWS + 3
BOTTOM_ROW = ROWS + 4
VMEM_LIMIT = 40 * 1024 * 1024


def left(v):
    return pltpu.roll(v, 1, 1)


def right(v):
    return pltpu.roll(v, LANES - 1, 1)


def above(v):
    return pltpu.roll(v, 1, 0)


def below(v):
    return pltpu.roll(v, v.shape[0] - 1, 0)


def row_index(rows):
    return lax.broadcasted_iota(jnp.int32, (rows, LANES), 0)


def neighbour_weights(speed, flag):
    step = sub_step * speed
    zero = jnp.zeros_like(step)
    return jnp.where(flag == 1, step, zero), jnp.where(flag == 1, zero, -step)


def split(v):
    first = v.astype(jnp.bfloat16).astype(jnp.float32)
    rest = v - first
    second = rest.astype(jnp.bfloat16).astype(jnp.float32)
    third = (rest - second).astype(jnp.bfloat16).astype(jnp.float32)
    return first, second, third


def updated_speed(fields_total, speed_ref, halo_ref, stress_ref, fluid):
    row = row_index(ROWS)
    scale = modulus / fields_total
    main = [scale * stress_ref[c, 0:ROWS, :] - (modulus if c != 1 else 0.0) for c in range(3)]
    before = [scale * stress_ref[c, TOP_ROW : TOP_ROW + 1, :] - (modulus if c != 1 else 0.0) for c in range(3)]
    after = [scale * stress_ref[c, BOTTOM_ROW : BOTTOM_ROW + 1, :] - (modulus if c != 1 else 0.0) for c in range(3)]
    mean_flow = stress_ref[0, ROWS : ROWS + 1, 0:1] / stress_ref[0, ROWS : ROWS + 1, 1:2]

    def up(v, edge):
        return jnp.where(row == 0, edge, above(v))

    def down(v, edge):
        return jnp.where(row == ROWS - 1, edge, below(v))

    new = []
    for c in range(2):
        v = speed_ref[c]
        laplace = up(v, halo_ref[c : c + 1, :]) + down(v, halo_ref[2 + c : 3 + c, :]) + left(v) + right(v) - 4.0 * v
        along_x = down(main[c], after[c]) - up(main[c], before[c])
        along_y = right(main[c + 1]) - left(main[c + 1])
        divergence = along_x * 0.5 + along_y * 0.5
        v = v + macro_step * (divergence + viscosity * laplace)
        if c == 0:
            v = v + (target_flow - mean_flow)
        new.append(fluid * v)
    return new


def own_kernel(nf, fields_total, first, *refs):
    refs = list(refs)
    delta_ref, spread_ref, odd_ref, speed_ref, solid_ref, upwind_ref, fields_ref, wiener_ref = refs[:8]
    rest = refs[8:]
    fluid = (1 - solid_ref[...]).astype(jnp.float32)
    if first:
        sx, sy = speed_ref[0], speed_ref[1]
    else:
        halo_ref, stress_ref = rest[:2]
        rest = rest[2:]
        sx, sy = updated_speed(fields_total, speed_ref, halo_ref, stress_ref, fluid)
    out_ref, top_ref, bottom_ref, send1_ref, send2_ref, sums_ref = rest[:6]
    rest = rest[6:]
    if not first:
        new_speed_ref = rest[0]
        rest = rest[1:]
        new_speed_ref[0] = sx
        new_speed_ref[1] = sy
    top_extra, bottom_extra = rest

    row = row_index(ROWS)
    zero = jnp.zeros((ROWS, LANES), jnp.float32)

    def grad_x(v):
        return (jnp.where(row == ROWS - 1, zero, below(v)) - jnp.where(row == 0, zero, above(v))) * 0.5

    def grad_y(v):
        return (right(v) - left(v)) * 0.5

    gxx, gxy = sub_step * grad_x(sx), sub_step * grad_x(sy)
    gyx, gyy = sub_step * grad_y(sx), sub_step * grad_y(sy)
    flag_x, flag_y = upwind_ref[0], upwind_ref[1]
    wa, wb = neighbour_weights(sx, flag_x)
    wl, wr = neighbour_weights(sy, flag_y)
    centre = 1.0 - wa - wb - wl - wr
    wa = jnp.where(row == 0, zero, wa)
    wb = jnp.where(row == ROWS - 1, zero, wb)

    def body(f, carry):
        base = centre - delta_ref[f]
        spread = spread_ref[f]
        diagonal = (base + gxx, base + gyy, base)
        q = [fields_ref[c, f] for c in range(3)]
        for k in range(SUBS):
            new = []
            for c in range(3):
                v = q[c]
                top_ref[3 * k + c, pl.ds(f, 1), :] = v[0:1, :]
                bottom_ref[3 * k + c, pl.ds(f, 1), :] = v[ROWS - 1 : ROWS, :]
                acc = diagonal[c] * v + spread * wiener_ref[k, c, f].astype(jnp.float32)
                acc = acc + (wl * left(v) + wr * right(v))
                acc = acc + (wa * above(v) + wb * below(v))
                if c == 0:
                    acc = acc + gyx * q[1]
                elif c == 1:
                    acc = acc + gxy * q[0]
                new.append(acc)
            q = new
        for c in range(3):
            out_ref[c, f] = q[c]
        for c in range(2):
            top_ref[3 * SUBS + c, pl.ds(f, 1), :] = q[c][0:1, :]
            bottom_ref[3 * SUBS + c, pl.ds(f, 1), :] = q[c][ROWS - 1 : ROWS, :]
        return carry

    lax.fori_loop(0, nf, body, 0, unroll=2)

    flow = jnp.sum(jnp.sum(fluid * sx, axis=0, keepdims=True), axis=1, keepdims=True)
    cells = jnp.sum(jnp.sum(fluid, axis=0, keepdims=True), axis=1, keepdims=True)
    lane = lax.broadcasted_iota(jnp.int32, (8, LANES), 1)
    flow = flow + jnp.zeros((8, LANES), jnp.float32)
    cells = cells + jnp.zeros((8, LANES), jnp.float32)
    sums_ref[...] = jnp.where(lane == 0, flow, jnp.where(lane == 1, cells, 0.0))
    packed = jnp.zeros((8, LANES), jnp.float32)
    for i, term in enumerate(split(flow) + split(cells)):
        packed = jnp.where(lane == i, term, packed)
    terms = (split(sx), split(sy))
    flags = (flag_x.astype(jnp.float32), flag_y.astype(jnp.float32))
    for extra, near, far in ((top_extra, 0, 1), (bottom_extra, ROWS - 1, ROWS - 2)):
        for c in range(2):
            for i in range(3):
                extra[3 * c + i : 3 * c + i + 1, :] = terms[c][i][near : near + 1, :]
                extra[6 + 3 * c + i : 7 + 3 * c + i, :] = terms[c][i][far : far + 1, :]
        extra[12:13, :] = flags[0][near : near + 1, :]
        extra[13:14, :] = flags[1][near : near + 1, :]
        extra[14:15, :] = flags[0][far : far + 1, :]
        extra[15:16, :] = packed[0:1, :]

    odd = jnp.full((nf, LANES), odd_ref[0], jnp.int32) == 1
    for send_ref, one_ref, other_ref in ((send1_ref, top_ref, bottom_ref), (send2_ref, bottom_ref, top_ref)):

        def put(t, v):
            rounded = v.astype(jnp.bfloat16)
            send_ref[nf * t : nf * t + nf, :] = rounded
            return v - rounded.astype(jnp.float32)

        for c in range(3):
            error = jnp.zeros((nf, LANES), jnp.float32)
            for k in range(SUBS):
                error = put(3 * k + c, jnp.where(odd, one_ref[3 * k + c], other_ref[3 * k + c]) + KEPT * error)
            put(3 * SUBS + c, error)
            if c < 2:
                error = put(3 * SUBS + 3 + c, jnp.where(odd, one_ref[3 * SUBS + c], other_ref[3 * SUBS + c]))
                put(3 * SUBS + 5 + c, error)
    odd = jnp.full((EXTRA, LANES), odd_ref[0], jnp.int32) == 1
    top, bottom = top_extra[...], bottom_extra[...]
    tail = nf * SENT
    send1_ref[tail : tail + EXTRA, :] = jnp.where(odd, top, bottom).astype(jnp.bfloat16)
    send2_ref[tail : tail + EXTRA, :] = jnp.where(odd, bottom, top).astype(jnp.bfloat16)


def join_kernel(nf, delta_ref, odd_ref, speed_ref, upwind_ref, own_ref, top_ref, bottom_ref, recv1_ref, recv2_ref,
                out_ref, stress_ref, halo_ref, before_ref, after_ref):
    tail = nf * SENT
    odd = jnp.full((nf, LANES), odd_ref[0], jnp.int32) == 1

    def track(ref, t):
        last = 3 * (SUBS - 1)
        if t < last:
            places = (t,)
        elif t < 3 * SUBS:
            places = (t, t + 3)
        else:
            places = (t + 3, t + 5)
        terms = [ref[nf * p : nf * p + nf, :].astype(jnp.float32) for p in places]
        return sum(terms[1:], terms[0])

    for t in range(TRACKS):
        one = track(recv1_ref, t)
        two = track(recv2_ref, t)
        before_ref[t] = jnp.where(odd, one, two)
        after_ref[t] = jnp.where(odd, two, one)
    odd = jnp.full((EXTRA, LANES), odd_ref[0], jnp.int32) == 1
    one = recv1_ref[tail : tail + EXTRA, :].astype(jnp.float32)
    two = recv2_ref[tail : tail + EXTRA, :].astype(jnp.float32)
    extras = (jnp.where(odd, one, two), jnp.where(odd, two, one))

    row = row_index(8)
    zero = jnp.zeros((8, LANES), jnp.float32)

    def joined(extra, i):
        return extra[i : i + 1, :] + extra[i + 1 : i + 2, :] + extra[i + 2 : i + 3, :]

    def strips(values, near, far):
        own_top = pltpu.roll(values[0:8], 4, 0)
        own_bottom = pltpu.roll(values[8:16], 4, 0)
        top = jnp.where(row >= 4, own_top, jnp.where(row == 3, near[0], jnp.where(row == 2, far[0], zero)))
        bottom = jnp.where(row < 4, own_bottom, jnp.where(row == 4, near[1], jnp.where(row == 5, far[1], zero)))
        return jnp.concatenate([top, bottom], axis=0)

    near_x = [joined(e, 0) for e in extras]
    near_y = [joined(e, 3) for e in extras]
    far_x = [joined(e, 6) for e in extras]
    far_y = [joined(e, 9) for e in extras]
    halo_ref[0:1, :] = near_x[0]
    halo_ref[1:2, :] = near_y[0]
    halo_ref[2:3, :] = near_x[1]
    halo_ref[3:4, :] = near_y[1]
    halo_ref[4:8, :] = jnp.zeros((4, LANES), jnp.float32)
    sx = strips(speed_ref[0], near_x, far_x)
    sy = strips(speed_ref[1], near_y, far_y)
    flag_x = strips(upwind_ref[0].astype(jnp.float32), [e[12:13, :] for e in extras], [e[14:15, :] for e in extras])
    flag_y = strips(upwind_ref[1].astype(jnp.float32), [e[13:14, :] for e in extras], [zero[0:1, :]] * 2)

    row2 = row_index(16)
    upper = (row2 == 3) | (row2 == 11)
    lower = (row2 == 4) | (row2 == 12)
    zero2 = jnp.zeros((16, LANES), jnp.float32)
    gxx = (0.5 * sub_step) * (below(sx) - above(sx))
    gxy = (0.5 * sub_step) * (below(sy) - above(sy))
    gyx = (0.5 * sub_step) * (right(sx) - left(sx))
    gyy = (0.5 * sub_step) * (right(sy) - left(sy))
    wa, wb = neighbour_weights(sx, flag_x)
    wl, wr = neighbour_weights(sy, flag_y)
    centre = 1.0 - wa - wb - wl - wr
    from_upper = jnp.where(lower, wa, zero2)
    from_lower = jnp.where(upper, wb, zero2)
    upper_x = jnp.where(upper, (0.5 * sub_step) * below(sx), zero2)
    upper_y = jnp.where(upper, (0.5 * sub_step) * below(sy), zero2)
    lower_x = jnp.where(lower, (-0.5 * sub_step) * above(sx), zero2)
    lower_y = jnp.where(lower, (-0.5 * sub_step) * above(sy), zero2)
    from_upper_x = from_upper + upper_x
    from_lower_x = from_lower + lower_x

    def spread_rows(first_ref, second_ref, t, f):
        return jnp.concatenate(
            [
                jnp.broadcast_to(first_ref[t, pl.ds(f, 1), :], (8, LANES)),
                jnp.broadcast_to(second_ref[t, pl.ds(f, 1), :], (8, LANES)),
            ],
            axis=0,
        )

    def body(f, sums):
        base = centre - delta_ref[f]
        diagonal = (base + gxx, base + gyy, base)
        d = None
        for k in range(SUBS):
            hu = [spread_rows(before_ref, bottom_ref, 3 * k + c, f) for c in range(3)]
            hl = [spread_rows(top_ref, after_ref, 3 * k + c, f) for c in range(3)]
            new = [
                from_upper_x * hu[0] + from_lower_x * hl[0],
                from_upper * hu[1] + from_lower * hl[1] + (upper_y * hu[0] + lower_y * hl[0]),
                from_upper * hu[2] + from_lower * hl[2],
            ]
            if d is not None:
                for c in range(3):
                    v = d[c]
                    acc = new[c] + diagonal[c] * v
                    acc = acc + (wl * left(v) + wr * right(v))
                    acc = acc + (wa * above(v) + wb * below(v))
                    if c == 0:
                        acc = acc + gyx * d[1]
                    elif c == 1:
                        acc = acc + gxy * d[0]
                    new[c] = acc
            d = new
        full = []
        edge = []
        for c in range(3):
            own = own_ref[c, f]
            top = own[0:8] + jnp.where(row < 4, pltpu.roll(d[c][0:8], 4, 0), zero)
            bottom = own[8:16] + jnp.where(row >= 4, pltpu.roll(d[c][8:16], 4, 0), zero)
            v = jnp.concatenate([top, bottom], axis=0)
            out_ref[c, f] = v
            if c < 2:
                t = 3 * SUBS + c
                full.append(v)
                edge.append(
                    jnp.where(
                        row < 4,
                        d[c][0:8] + jnp.broadcast_to(before_ref[t, pl.ds(f, 1), :], (8, LANES)),
                        d[c][8:16] + jnp.broadcast_to(after_ref[t, pl.ds(f, 1), :], (8, LANES)),
                    )
                )
        pairs = ((0, 0), (0, 1), (1, 1))
        return tuple(s + full[i] * full[j] for s, (i, j) in zip(sums[:3], pairs)) + tuple(
            s + edge[i] * edge[j] for s, (i, j) in zip(sums[3:], pairs)
        )

    sums = lax.fori_loop(0, nf, body, (zero2,) * 3 + (zero,) * 3, unroll=2)
    keep = (row == 3) | (row == 4)
    for c in range(3):
        stress_ref[c, 0:ROWS, :] = sums[c]
        stress_ref[c, ROWS : ROWS + 8, :] = jnp.where(keep, sums[3 + c], zero)


def last_kernel(fields_total, speed_ref, solid_ref, halo_ref, stress_ref, out_ref):
    fluid = (1 - solid_ref[...]).astype(jnp.float32)
    sx, sy = updated_speed(fields_total, speed_ref, halo_ref, stress_ref, fluid)
    out_ref[0] = sx
    out_ref[1] = sy


def vmem():
    return pl.BlockSpec(memory_space=pltpu.VMEM)


def smem():
    return pl.BlockSpec(memory_space=pltpu.SMEM)


def shaped(shape, dtype=jnp.float32):
    return jax.ShapeDtypeStruct(shape, dtype)


def whole(shape):
    return pl.BlockSpec(shape, lambda i: (0,) * len(shape))


def own_steps(step, fields_total, delta, spread, odd, speed, solid, upwind, fields, wiener, halo, stress):
    nf = fields.shape[1]
    first = step == 0
    size = nf * SENT + EXTRA
    extra = [] if first else [halo, stress]
    outs = [
        shaped(fields.shape),
        shaped((TRACKS, nf, LANES)),
        shaped((TRACKS, nf, LANES)),
        shaped((size, LANES), jnp.bfloat16),
        shaped((size, LANES), jnp.bfloat16),
        shaped((8, LANES)),
    ]
    if not first:
        outs.append(shaped(speed.shape))
    got = pl.pallas_call(
        functools.partial(own_kernel, nf, fields_total, first),
        grid=(1,),
        out_shape=outs,
        in_specs=[smem(), smem(), smem()]
        + [whole(v.shape) for v in (speed, solid, upwind, fields)]
        + [pl.BlockSpec((SUBS,) + wiener.shape[1:], lambda i: (step, 0, 0, 0, 0))]
        + [whole(v.shape) for v in extra],
        out_specs=[whole(o.shape) for o in outs],
        scratch_shapes=[pltpu.VMEM((EXTRA, LANES), jnp.float32)] * 2,
        compiler_params=pltpu.CompilerParams(vmem_limit_bytes=VMEM_LIMIT),
        name="own_steps",
    )(delta, spread, odd, speed, solid, upwind, fields, wiener, *extra)
    return got if not first else list(got) + [speed]


def join(delta, odd, speed, upwind, own, top, bottom, recv1, recv2):
    nf = own.shape[1]
    return pl.pallas_call(
        functools.partial(join_kernel, nf),
        out_shape=[shaped(own.shape), shaped((3, ROWS + 8, LANES)), shaped((8, LANES))],
        in_specs=[smem(), smem()] + [vmem()] * 7,
        out_specs=[vmem()] * 3,
        scratch_shapes=[pltpu.VMEM((TRACKS, nf, LANES), jnp.float32)] * 2,
        compiler_params=pltpu.CompilerParams(vmem_limit_bytes=VMEM_LIMIT),
        name="join",
    )(delta, odd, speed, upwind, own, top, bottom, recv1, recv2)


def last_speed(fields_total, speed, solid, halo, stress):
    return pl.pallas_call(
        functools.partial(last_kernel, fields_total),
        out_shape=shaped(speed.shape),
        in_specs=[vmem()] * 4,
        out_specs=vmem(),
        name="last_speed",
    )(speed, solid, halo, stress)


def swapped(value, axis, bit):
    count = lax.axis_size(axis)
    return lax.ppermute(value, axis, [(i, i ^ bit) for i in range(count)])


def flow_sums(sums, recv1, recv2):
    terms = recv1[recv1.shape[0] - 1, 0:6].astype(jnp.float32)
    value = sums[0, 0:2] + jnp.stack([terms[0] + terms[1] + terms[2], terms[3] + terms[4] + terms[5]])
    value = value + swapped(value, "slab", 2)
    value = value + swapped(value, "slab", 4)
    value, recv2 = lax.optimization_barrier((value, recv2))
    slabs, parts = lax.axis_size("slab"), lax.axis_size("field")
    assert slabs == 8 * parts
    pairs = [(((s + 8 * f) % slabs) * parts + f, s * parts + f) for s in range(slabs) for f in range(parts)]
    return lax.ppermute(value, ("slab", "field"), pairs), recv2


def field_sum(value):
    bit = 1
    while bit < lax.axis_size("field"):
        value = value + swapped(value, "field", bit)
        bit *= 2
    return value


def per_device(conform, velocity, solid_mask, upwind, relax_time, wiener):
    slabs = lax.axis_size("slab")
    fields_total = conform.shape[1] * lax.axis_size("field")
    odd = (lax.axis_index("slab") % 2).astype(jnp.int32).reshape(1)
    delta = sub_step * (0.5 / relax_time)
    spread = jnp.sqrt(sub_step / relax_time)
    near_pairs = [(i, i ^ 1) for i in range(slabs)]
    far_pairs = [(i, (i + 1) % slabs if i % 2 else (i - 1) % slabs) for i in range(slabs)]
    fields, speed, halo, stress = conform, velocity, None, None
    for step in range(STEPS):
        own, top, bottom, send1, send2, sums, speed = own_steps(
            step, fields_total, delta, spread, odd, speed, solid_mask, upwind, fields, wiener, halo, stress
        )
        recv1 = lax.ppermute(send1, "slab", near_pairs)
        recv2 = lax.ppermute(send2, "slab", far_pairs)
        flow, recv2 = flow_sums(sums, recv1, recv2)
        fields, stress, halo = join(delta, odd, speed, upwind, own, top, bottom, recv1, recv2)
        stress = stress.at[0, ROWS, 0:2].set(flow)
        stress = field_sum(stress)
    speed = last_speed(fields_total, speed, solid_mask, halo, stress)
    return (fields, speed)


def solution(mesh):
    placed = (
        P(None, "field", "slab", None),
        P(None, "slab", None),
        P("slab", None),
        P(None, "slab", None),
        P("field"),
        P(None, None, "field", "slab", None),
    )
    return jax.shard_map(
        per_device,
        mesh=mesh,
        in_specs=placed,
        out_specs=(P(None, "field", "slab", None), P(None, "slab", None)),
        check_vma=False,
    )
```

time: 677 us -> 138 us (0.20)
  blocking collectives: 487 us -> 0 us
  starting transfers between devices: 141 us -> 73.1 us
  Pallas kernels: 0 us -> 20.7 us
  other arithmetic: 15.3 us -> 1.64 us
  waiting for transfers between devices: 14.7 us -> 25.4 us
    psum x4 -> x0, blocking collectives: 487 us -> none  [the longest x2 376 us: per_device(): lax.psum((jnp.sum(fluid * speed[0]), jnp.sum(fluid)), 'slab')]
    ppermute x20 -> x16, starting transfers between devices: 141 us -> 73.1 us  [the longest x10 41.5 us: swapped(): return lax.ppermute(value, axis, [(i, i ^ bit) for i in range(count)])]
    pallas_call x0 -> x5, Pallas kernels: none -> 20.7 us  [the longest x2 10.5 us: own_steps(): pl.pallas_call(functools.partial(own_kernel, nf, fields_total, first), gr...]
    add x16 -> x12, other arithmetic: 13 us -> 0.97 us  [the longest x6 0.65 us: field_sum(): value = value + swapped(value, 'field', bit)]
    ppermute x20 -> x16, waiting for transfers between devices: 14.7 us -> 25.4 us  [the longest x10 25.4 us: swapped(): return lax.ppermute(value, axis, [(i, i ^ bit) for i in range(count)])]
    slice x26 -> x2, local copies, waits for them, and re-layouts: 10.9 us -> 1.33 us  [flow_sums(): terms[2]]
  transfers between devices with their start and end apart: 20 -> 16, of which waited for: 5 -> 10; matrix products, arithmetic and copies ran while one was open for 1% -> 1% of each run, Pallas kernels for 0% -> 6%
where the time goes in v1:
time: 138 us; the launch traced here: 136 us
  starting transfers between devices  73.1 us (53%)
  waiting for transfers between devices  25.4 us (18%)
  Pallas kernels  20.7 us (15%)
  between operations  8.39 us (6%)
  local copies, waits for them, and re-layouts  7.15 us (5%)
  other arithmetic  1.64 us (1%)
    ppermute x10, starting transfers between devices, swapped(): return lax.ppermute(value, axis, [(i, i ^ bit) for i in range(count)])  41.5 us
    ppermute x10, waiting for transfers between devices, swapped(): return lax.ppermute(value, axis, [(i, i ^ bit) for i in range(count)])  25.4 us
    ppermute x2, starting transfers between devices, per_device(): recv2 = lax.ppermute(send2, 'slab', far_pairs)  19.8 us
    pallas_call x2, Pallas kernels, own_steps(): pl.pallas_call(functools.partial(own_kernel, nf, fields_total, first), gr...  10.5 us
    pallas_call x2, Pallas kernels, join(): pl.pallas_call(functools.partial(join_kernel, nf), out_shape=[shaped(own....  8.64 us
    ppermute x2, starting transfers between devices, flow_sums(): return (lax.ppermute(value, ('slab', 'field'), pairs), recv2)  5.89 us
    ppermute x2, starting transfers between devices, per_device(): recv1 = lax.ppermute(send1, 'slab', near_pairs)  5.87 us
    unnamed x22, local copies, waits for them, and re-layouts  5.53 us
  transfers between devices with their start and end apart: 16, of which 10 were waited for; matrix products, arithmetic and copies ran while one was open for 1% of the time, Pallas kernels for 6%

profile of v1, /device:TPU:1, one launch (start us, length us, event | category | flops | bytes accessed | tf_op | source)
XLA Modules:
  0.0 136.3 jit_solution(11566441920831106660)
XLA Ops:
  1.3 1.7 %copy-done = bf16[6,3,32,16,128]{4,3,2,1,0:T(8,128)(2,1)S(1)} copy-done((bf16[6,3,32,16,128]{4,3,2,1,0:T(8,128)(2,1)S(1)}, bf16[6,3,32,16,128]{4,3,2,1,0:T(8,128)(2,1)}, u32[]{:S(2)}) %copy-start) | copy-done | bytes 2359320
  3.0 1.1 copy-done.2
  6.3 5.2 %own_steps.2 = (f32[3,32,16,128]{3,2,1,0:T(8,128)S(1)}, f32[11,32,128]{2,1,0:T(8,128)S(1)}, f32[11,32,128]{2,1,0:T(8,128)S(1)}, bf16[528,128]{1,0:T(8,128)(2,1)S...) custom-call(f32[32]{0:T(128)S(1)} %get-tuple-element.85.refs_0_.delta_ref, f32[32]{0:T(128)S(1)} %get-tuple-element.84.refs_1_, ...), custom_call_target="tpu_custom_call" | custom-call | tf_op jit(solution)/shard_map/own_steps/pallas_call | solution.py:376
  11.4 3.9 %collective-permute-start = (bf16[528,128]{1,0:T(8,128)(2,1)S(1)}, bf16[528,128]{1,0:T(8,128)(2,1)S(1)}, u32[]{:S(2)}, u32[]{:S(2)}) collective-permute-start(bf16[528,128]{1,0:T(8,128)(2,1)S(1)} %get-tuple-element.52), channel_id=1, source_target_pairs={{0,8},{8,0},{16,24},{24,16},{32,40},{40,32},{48,56},{56,48},{64,72... | collective-permute-start | bytes 405512 | tf_op jit(solution)/shard_map/ppermute | solution.py:453
  15.4 15.1 %collective-permute-start.3 = (bf16[528,128]{1,0:T(8,128)(2,1)S(1)}, bf16[528,128]{1,0:T(8,128)(2,1)S(1)}, u32[]{:S(2)}, u32[]{:S(2)}) collective-permute-start(bf16[528,128]{1,0:T(8,128)(2,1)S(1)} %get-tuple-element.54), channel_id=1, source_target_pairs={{0,504},{8,16},{16,8},{24,32},{32,24},{40,48},{48,40},{56,64},{64,... | collective-permute-start | bytes 405512 | tf_op jit(solution)/shard_map/ppermute | solution.py:454
  35.1 1.9 %collective-permute-start.1 = (f32[2]{0:T(128)S(1)}, f32[2]{0:T(128)S(1)}, u32[]{:S(2)}, u32[]{:S(2)}) collective-permute-start(f32[2]{0:T(128)S(1)} %maximum_add_fusion), channel_id=1, source_target_pairs={{0,16},{8,24},{16,0},{24,8},{32,48},{40,56},{48,32},{56,40},{64,80... | collective-permute-start | bytes 32 | tf_op jit(solution)/shard_map/ppermute | solution.py:417
  37.0 3.9 %collective-permute-done.1 = f32[2]{0:T(128)S(1)} collective-permute-done((f32[2]{0:T(128)S(1)}, f32[2]{0:T(128)S(1)}, u32[]{:S(2)}, u32[]{:S(2)}) %collective-permute-start.1) | collective-permute-done | bytes 40 | tf_op jit(solution)/shard_map/ppermute | solution.py:417
  40.9 1.9 %collective-permute-start.2 = (f32[2]{0:T(128)S(1)}, f32[2]{0:T(128)S(1)}, u32[]{:S(2)}, u32[]{:S(2)}) collective-permute-start(f32[2]{0:T(128)S(1)} %fusion.3), channel_id=1, source_target_pairs={{0,32},{8,40},{16,48},{24,56},{32,0},{40,8},{48,16},{56,24},{64,96... | collective-permute-start | bytes 32 | tf_op jit(solution)/shard_map/ppermute | solution.py:417
  42.8 6.3 %collective-permute-done.2 = f32[2]{0:T(128)S(1)} collective-permute-done((f32[2]{0:T(128)S(1)}, f32[2]{0:T(128)S(1)}, u32[]{:S(2)}, u32[]{:S(2)}) %collective-permute-start.2) | collective-permute-done | bytes 40 | tf_op jit(solution)/shard_map/ppermute | solution.py:417
  49.1 3.0 %collective-permute-start.4 = (f32[2]{0:T(128)S(1)}, f32[2]{0:T(128)S(1)}, u32[]{:S(2)}, u32[]{:S(2)}) collective-permute-start(f32[2]{0:T(128)S(1)} %add.87), channel_id=1, source_target_pairs={{0,0},{65,1},{130,2},{195,3},{260,4},{325,5},{390,6},{455,7},{8,8}... | collective-permute-start | bytes 32 | tf_op jit(solution)/shard_map/ppermute | solution.py:429
  52.1 3.9 %join.2 = (f32[3,32,16,128]{3,2,1,0:T(8,128)S(1)}, f32[3,24,128]{2,1,0:T(8,128)S(1)}, f32[8,128]{1,0:T(8,128)S(1)}) custom-call(f32[32]{0:T(128)S(1)} %get-tuple-element.85.refs_0_.delta_ref, s32[1]{0:T(128)} %bitcast.refs_2_.odd_ref, f32[2,16,128]{2,1,0:T(8,128)S(1)} %copy-done.5, s32[2,16,128]{2,1,0:T(8,128)S(1)} %copy-done.3, ...), custom_call_target="tpu_custom_call" | custom-call | tf_op jit(solution)/shard_map/join/pallas_call | solution.py:394
  56.2 3.1 %collective-permute-start.5 = (f32[3,24,128]{2,1,0:T(8,128)S(1)}, f32[3,24,128]{2,1,0:T(8,128)S(1)}, u32[]{:S(2)}, u32[]{:S(2)}) collective-permute-start(f32[3,24,128]{2,1,0:T(8,128)S(1)} %scatter.6), channel_id=1, source_target_pairs={{0,1},{1,0},{2,3},{3,2},{4,5},{5,4},{6,7},{7,6},{8,9},{9,8},{10,11... | collective-permute-start | bytes 110600 | tf_op jit(solution)/shard_map/ppermute | solution.py:417
  59.3 0.8 collective-permute-done.5
  60.2 6.5 %collective-permute-start.6 = (f32[3,24,128]{2,1,0:T(8,128)S(1)}, f32[3,24,128]{2,1,0:T(8,128)S(1)}, u32[]{:S(2)}, u32[]{:S(2)}) collective-permute-start(f32[3,24,128]{2,1,0:T(8,128)S(1)} %add.88), channel_id=1, source_target_pairs={{0,2},{1,3},{2,0},{3,1},{4,6},{5,7},{6,4},{7,5},{8,10},{9,11},{10,... | collective-permute-start | bytes 110600 | tf_op jit(solution)/shard_map/ppermute | solution.py:417
  66.6 1.3 collective-permute-done.6
  68.0 5.5 %collective-permute-start.7 = (f32[3,24,128]{2,1,0:T(8,128)S(1)}, f32[3,24,128]{2,1,0:T(8,128)S(1)}, u32[]{:S(2)}, u32[]{:S(2)}) collective-permute-start(f32[3,24,128]{2,1,0:T(8,128)S(1)} %add.89), channel_id=1, source_target_pairs={{0,4},{1,5},{2,6},{3,7},{4,0},{5,1},{6,2},{7,3},{8,12},{9,13},{10,... | collective-permute-start | bytes 110600 | tf_op jit(solution)/shard_map/ppermute | solution.py:417
  73.5 1.6 %collective-permute-done.7 = f32[3,24,128]{2,1,0:T(8,128)S(1)} collective-permute-done((f32[3,24,128]{2,1,0:T(8,128)S(1)}, f32[3,24,128]{2,1,0:T(8,128)S(1)}, u32[]{:S(2)}, u32[]{:S(2)}) %collective-permute-start.7) | collective-permute-done | bytes 36896 | tf_op jit(solution)/shard_map/ppermute | solution.py:417
  75.2 5.3 %own_steps.3 = (f32[3,32,16,128]{3,2,1,0:T(8,128)S(1)}, f32[11,32,128]{2,1,0:T(8,128)S(1)}, f32[11,32,128]{2,1,0:T(8,128)S(1)}, bf16[528,128]{1,0:T(8,128)(2,1)S...) custom-call(f32[32]{0:T(128)S(1)} %get-tuple-element.85.refs_0_.delta_ref, ...), custom_call_target="tpu_custom_call" | custom-call | tf_op jit(solution)/shard_map/own_steps/pallas_call | solution.py:376
  80.5 1.9 %collective-permute-start.8 = (bf16[528,128]{1,0:T(8,128)(2,1)S(1)}, bf16[528,128]{1,0:T(8,128)(2,1)S(1)}, u32[]{:S(2)}, u32[]{:S(2)}) collective-permute-start(bf16[528,128]{1,0:T(8,128)(2,1)S(1)} %get-tuple-element.64), channel_id=1, source_target_pairs={{0,8},{8,0},{16,24},{24,16},{32,40},{40,32},{48,56},{56,48},{64,72... | collective-permute-start | bytes 405512 | tf_op jit(solution)/shard_map/ppermute | solution.py:453
  82.4 4.7 %collective-permute-start.11 = (bf16[528,128]{1,0:T(8,128)(2,1)S(1)}, bf16[528,128]{1,0:T(8,128)(2,1)S(1)}, u32[]{:S(2)}, u32[]{:S(2)}) collective-permute-start(bf16[528,128]{1,0:T(8,128)(2,1)S(1)} %get-tuple-element.66), channel_id=1, source_target_pairs={{0,504},{8,16},{16,8},{24,32},{32,24},{40,48},{48,40},{56,64},{64,... | collective-permute-start | bytes 405512 | tf_op jit(solution)/shard_map/ppermute | solution.py:454
  91.6 2.3 %collective-permute-start.9 = (f32[2]{0:T(128)S(1)}, f32[2]{0:T(128)S(1)}, u32[]{:S(2)}, u32[]{:S(2)}) collective-permute-start(f32[2]{0:T(128)S(1)} %maximum_add_fusion.1), channel_id=1, source_target_pairs={{0,16},{8,24},{16,0},{24,8},{32,48},{40,56},{48,32},{56,40},{64,80... | collective-permute-start | bytes 32 | tf_op jit(solution)/shard_map/ppermute | solution.py:417
  94.0 3.8 %collective-permute-done.9 = f32[2]{0:T(128)S(1)} collective-permute-done((f32[2]{0:T(128)S(1)}, f32[2]{0:T(128)S(1)}, u32[]{:S(2)}, u32[]{:S(2)}) %collective-permute-start.9) | collective-permute-done | bytes 40 | tf_op jit(solution)/shard_map/ppermute | solution.py:417
  97.8 4.1 %collective-permute-start.10 = (f32[2]{0:T(128)S(1)}, f32[2]{0:T(128)S(1)}, u32[]{:S(2)}, u32[]{:S(2)}) collective-permute-start(f32[2]{0:T(128)S(1)} %fusion.2), channel_id=1, source_target_pairs={{0,32},{8,40},{16,48},{24,56},{32,0},{40,8},{48,16},{56,24},{64,96... | collective-permute-start | bytes 32 | tf_op jit(solution)/shard_map/ppermute | solution.py:417
  101.9 4.1 %collective-permute-done.10 = f32[2]{0:T(128)S(1)} collective-permute-done((f32[2]{0:T(128)S(1)}, f32[2]{0:T(128)S(1)}, u32[]{:S(2)}, u32[]{:S(2)}) %collective-permute-start.10) | collective-permute-done | bytes 40 | tf_op jit(solution)/shard_map/ppermute | solution.py:417
  106.0 2.9 %collective-permute-start.12 = (f32[2]{0:T(128)S(1)}, f32[2]{0:T(128)S(1)}, u32[]{:S(2)}, u32[]{:S(2)}) collective-permute-start(f32[2]{0:T(128)S(1)} %add.97), channel_id=1, source_target_pairs={{0,0},{65,1},{130,2},{195,3},{260,4},{325,5},{390,6},{455,7},{8,8}... | collective-permute-start | bytes 32 | tf_op jit(solution)/shard_map/ppermute | solution.py:429
  108.9 4.8 %join.3 = (f32[3,32,16,128]{3,2,1,0:T(8,128)}, f32[3,24,128]{2,1,0:T(8,128)S(1)}, f32[8,128]{1,0:T(8,128)S(1)}) custom-call(f32[32]{0:T(128)S(1)} %get-tuple-element.85.refs_0_.delta_ref, s32[1]{0:T(128)} %bitcast.refs_2_.odd_ref, f32[2,16,128]{2,1,0:T(8,128)S(1)} %get-tuple-element.60.speed_ref, s32[2,16,128]{2,1,0:T(8,128)S(1)} %copy-done.4, ...), custom_call_target="tpu_custom_call" | custom-call | tf_op jit(solution)/shard_map/join/pallas_call | solution.py:394
  114.3 4.6 %collective-permute-start.13 = (f32[3,24,128]{2,1,0:T(8,128)S(1)}, f32[3,24,128]{2,1,0:T(8,128)S(1)}, u32[]{:S(2)}, u32[]{:S(2)}) collective-permute-start(f32[3,24,128]{2,1,0:T(8,128)S(1)} %scatter.9), channel_id=1, source_target_pairs={{0,1},{1,0},{2,3},{3,2},{4,5},{5,4},{6,7},{7,6},{8,9},{9,8},{10,11... | collective-permute-start | bytes 110600 | tf_op jit(solution)/shard_map/ppermute | solution.py:417
  119.8 4.6 %collective-permute-start.14 = (f32[3,24,128]{2,1,0:T(8,128)S(1)}, f32[3,24,128]{2,1,0:T(8,128)S(1)}, u32[]{:S(2)}, u32[]{:S(2)}) collective-permute-start(f32[3,24,128]{2,1,0:T(8,128)S(1)} %add.98), channel_id=1, source_target_pairs={{0,2},{1,3},{2,0},{3,1},{4,6},{5,7},{6,4},{7,5},{8,10},{9,11},{10,... | collective-permute-start | bytes 110600 | tf_op jit(solution)/shard_map/ppermute | solution.py:417
  124.5 1.3 collective-permute-done.14
  125.8 6.9 %collective-permute-start.15 = (f32[3,24,128]{2,1,0:T(8,128)S(1)}, f32[3,24,128]{2,1,0:T(8,128)S(1)}, u32[]{:S(2)}, u32[]{:S(2)}) collective-permute-start(f32[3,24,128]{2,1,0:T(8,128)S(1)} %add.99), channel_id=1, source_target_pairs={{0,4},{1,5},{2,6},{3,7},{4,0},{5,1},{6,2},{7,3},{8,12},{9,13},{10,... | collective-permute-start | bytes 110600 | tf_op jit(solution)/shard_map/ppermute | solution.py:417
  132.7 1.5 %collective-permute-done.15 = f32[3,24,128]{2,1,0:T(8,128)S(1)} collective-permute-done((f32[3,24,128]{2,1,0:T(8,128)S(1)}, f32[3,24,128]{2,1,0:T(8,128)S(1)}, u32[]{:S(2)}, u32[]{:S(2)}) %collective-permute-start.15) | collective-permute-done | bytes 36896 | tf_op jit(solution)/shard_map/ppermute | solution.py:417
  134.8 1.5 %last_speed.1 = f32[2,16,128]{2,1,0:T(8,128)} custom-call(f32[2,16,128]{2,1,0:T(8,128)} %copy-done.9, s32[16,128]{1,0:T(8,128)} %solid_ref.1, f32[8,128]{1,0:T(8,128)} %copy-done.10, f32[3,24,128]{2,1,0:T(8,128)} %add.100.stress_ref), custom_call_target="tpu_custom_call" | custom-call | tf_op jit(solution)/shard_map/last_speed/pallas_call | solution.py:406
  (46 shorter events, 6.9 us)
Async XLA Ops:
  1.3 1.7 %copy-start = (bf16[6,3,32,16,128]{4,3,2,1,0:T(8,128)(2,1)S(1)}, bf16[6,3,32,16,128]{4,3,2,1,0:T(8,128)(2,1)}, u32[]{:S(2)}) copy-start(bf16[6,3,32,16,128]{4,3,2,1,0:T(8,128)(2,1)} %refs_7_.3) | copy-start | bytes 7077892
  3.0 1.1 copy-start.2
  4.1 0.7 copy-start.3
  4.8 0.7 copy-start.5
  5.5 0.7 copy-start.7
  6.2 68.9 %copy-start.1 = (bf16[6,3,32,16,128]{4,3,2,1,0:T(8,128)(2,1)S(1)}, bf16[6,3,32,16,128]{4,3,2,1,0:T(8,128)(2,1)}, u32[]{:S(2)}) copy-start(bf16[6,3,32,16,128]{4,3,2,1,0:T(8,128)(2,1)} %refs_7_.3) | copy-start | bytes 7077892
  6.2 68.9 %copy-start.4 = (s32[2,16,128]{2,1,0:T(8,128)S(1)}, s32[2,16,128]{2,1,0:T(8,128)}, u32[]{:S(2)}) copy-start(s32[2,16,128]{2,1,0:T(8,128)} %upwind_ref.3) | copy-start | bytes 49156
  6.2 68.9 %copy-start.6 = (f32[2,16,128]{2,1,0:T(8,128)S(1)}, f32[2,16,128]{2,1,0:T(8,128)}, u32[]{:S(2)}) copy-start(f32[2,16,128]{2,1,0:T(8,128)} %refs_3_.3) | copy-start | bytes 49156
  6.2 68.9 %copy-start.8 = (s32[16,128]{1,0:T(8,128)S(1)}, s32[16,128]{1,0:T(8,128)}, u32[]{:S(2)}) copy-start(s32[16,128]{1,0:T(8,128)} %solid_ref.1) | copy-start | bytes 24580
  11.4 19.0 %collective-permute-start = (bf16[528,128]{1,0:T(8,128)(2,1)S(1)}, bf16[528,128]{1,0:T(8,128)(2,1)S(1)}, u32[]{:S(2)}, u32[]{:S(2)}) collective-permute-start(bf16[528,128]{1,0:T(8,128)(2,1)S(1)} %get-tuple-element.52), channel_id=1, source_target_pairs={{0,8},{8,0},{16,24},{24,16},{32,40},{40,32},{48,56},{56,48},{64,72... | collective-permute-start | bytes 405512 | tf_op jit(solution)/shard_map/ppermute | solution.py:453
  15.4 33.7 %collective-permute-start.3 = (bf16[528,128]{1,0:T(8,128)(2,1)S(1)}, bf16[528,128]{1,0:T(8,128)(2,1)S(1)}, u32[]{:S(2)}, u32[]{:S(2)}) collective-permute-start(bf16[528,128]{1,0:T(8,128)(2,1)S(1)} %get-tuple-element.54), channel_id=1, source_target_pairs={{0,504},{8,16},{16,8},{24,32},{32,24},{40,48},{48,40},{56,64},{64,... | collective-permute-start | bytes 405512 | tf_op jit(solution)/shard_map/ppermute | solution.py:454
  35.1 5.8 %collective-permute-start.1 = (f32[2]{0:T(128)S(1)}, f32[2]{0:T(128)S(1)}, u32[]{:S(2)}, u32[]{:S(2)}) collective-permute-start(f32[2]{0:T(128)S(1)} %maximum_add_fusion), channel_id=1, source_target_pairs={{0,16},{8,24},{16,0},{24,8},{32,48},{40,56},{48,32},{56,40},{64,80... | collective-permute-start | bytes 32 | tf_op jit(solution)/shard_map/ppermute | solution.py:417
  40.9 8.2 %collective-permute-start.2 = (f32[2]{0:T(128)S(1)}, f32[2]{0:T(128)S(1)}, u32[]{:S(2)}, u32[]{:S(2)}) collective-permute-start(f32[2]{0:T(128)S(1)} %fusion.3), channel_id=1, source_target_pairs={{0,32},{8,40},{16,48},{24,56},{32,0},{40,8},{48,16},{56,24},{64,96... | collective-permute-start | bytes 32 | tf_op jit(solution)/shard_map/ppermute | solution.py:417
  49.1 6.9 %collective-permute-start.4 = (f32[2]{0:T(128)S(1)}, f32[2]{0:T(128)S(1)}, u32[]{:S(2)}, u32[]{:S(2)}) collective-permute-start(f32[2]{0:T(128)S(1)} %add.87), channel_id=1, source_target_pairs={{0,0},{65,1},{130,2},{195,3},{260,4},{325,5},{390,6},{455,7},{8,8}... | collective-permute-start | bytes 32 | tf_op jit(solution)/shard_map/ppermute | solution.py:429
  56.2 4.0 %collective-permute-start.5 = (f32[3,24,128]{2,1,0:T(8,128)S(1)}, f32[3,24,128]{2,1,0:T(8,128)S(1)}, u32[]{:S(2)}, u32[]{:S(2)}) collective-permute-start(f32[3,24,128]{2,1,0:T(8,128)S(1)} %scatter.6), channel_id=1, source_target_pairs={{0,1},{1,0},{2,3},{3,2},{4,5},{5,4},{6,7},{7,6},{8,9},{9,8},{10,11... | collective-permute-start | bytes 110600 | tf_op jit(solution)/shard_map/ppermute | solution.py:417
  60.2 7.8 %collective-permute-start.6 = (f32[3,24,128]{2,1,0:T(8,128)S(1)}, f32[3,24,128]{2,1,0:T(8,128)S(1)}, u32[]{:S(2)}, u32[]{:S(2)}) collective-permute-start(f32[3,24,128]{2,1,0:T(8,128)S(1)} %add.88), channel_id=1, source_target_pairs={{0,2},{1,3},{2,0},{3,1},{4,6},{5,7},{6,4},{7,5},{8,10},{9,11},{10,... | collective-permute-start | bytes 110600 | tf_op jit(solution)/shard_map/ppermute | solution.py:417
  68.0 7.2 %collective-permute-start.7 = (f32[3,24,128]{2,1,0:T(8,128)S(1)}, f32[3,24,128]{2,1,0:T(8,128)S(1)}, u32[]{:S(2)}, u32[]{:S(2)}) collective-permute-start(f32[3,24,128]{2,1,0:T(8,128)S(1)} %add.89), channel_id=1, source_target_pairs={{0,4},{1,5},{2,6},{3,7},{4,0},{5,1},{6,2},{7,3},{8,12},{9,13},{10,... | collective-permute-start | bytes 110600 | tf_op jit(solution)/shard_map/ppermute | solution.py:417
  80.5 54.3 %copy-start.9 = (f32[2,16,128]{2,1,0:T(8,128)}, f32[2,16,128]{2,1,0:T(8,128)S(1)}, u32[]{:S(2)}) copy-start(f32[2,16,128]{2,1,0:T(8,128)S(1)} %get-tuple-element.60.speed_ref) | copy-start | bytes 49156
  80.5 6.6 %collective-permute-start.8 = (bf16[528,128]{1,0:T(8,128)(2,1)S(1)}, bf16[528,128]{1,0:T(8,128)(2,1)S(1)}, u32[]{:S(2)}, u32[]{:S(2)}) collective-permute-start(bf16[528,128]{1,0:T(8,128)(2,1)S(1)} %get-tuple-element.64), channel_id=1, source_target_pairs={{0,8},{8,0},{16,24},{24,16},{32,40},{40,32},{48,56},{56,48},{64,72... | collective-permute-start | bytes 405512 | tf_op jit(solution)/shard_map/ppermute | solution.py:453
  82.4 23.6 %collective-permute-start.11 = (bf16[528,128]{1,0:T(8,128)(2,1)S(1)}, bf16[528,128]{1,0:T(8,128)(2,1)S(1)}, u32[]{:S(2)}, u32[]{:S(2)}) collective-permute-start(bf16[528,128]{1,0:T(8,128)(2,1)S(1)} %get-tuple-element.66), channel_id=1, source_target_pairs={{0,504},{8,16},{16,8},{24,32},{32,24},{40,48},{48,40},{56,64},{64,... | collective-permute-start | bytes 405512 | tf_op jit(solution)/shard_map/ppermute | solution.py:454
  91.6 6.1 %collective-permute-start.9 = (f32[2]{0:T(128)S(1)}, f32[2]{0:T(128)S(1)}, u32[]{:S(2)}, u32[]{:S(2)}) collective-permute-start(f32[2]{0:T(128)S(1)} %maximum_add_fusion.1), channel_id=1, source_target_pairs={{0,16},{8,24},{16,0},{24,8},{32,48},{40,56},{48,32},{56,40},{64,80... | collective-permute-start | bytes 32 | tf_op jit(solution)/shard_map/ppermute | solution.py:417
  97.8 8.2 %collective-permute-start.10 = (f32[2]{0:T(128)S(1)}, f32[2]{0:T(128)S(1)}, u32[]{:S(2)}, u32[]{:S(2)}) collective-permute-start(f32[2]{0:T(128)S(1)} %fusion.2), channel_id=1, source_target_pairs={{0,32},{8,40},{16,48},{24,56},{32,0},{40,8},{48,16},{56,24},{64,96... | collective-permute-start | bytes 32 | tf_op jit(solution)/shard_map/ppermute | solution.py:417
  106.0 8.3 %collective-permute-start.12 = (f32[2]{0:T(128)S(1)}, f32[2]{0:T(128)S(1)}, u32[]{:S(2)}, u32[]{:S(2)}) collective-permute-start(f32[2]{0:T(128)S(1)} %add.97), channel_id=1, source_target_pairs={{0,0},{65,1},{130,2},{195,3},{260,4},{325,5},{390,6},{455,7},{8,8}... | collective-permute-start | bytes 32 | tf_op jit(solution)/shard_map/ppermute | solution.py:429
  113.7 0.6 copy-start.10
  114.3 5.5 %collective-permute-start.13 = (f32[3,24,128]{2,1,0:T(8,128)S(1)}, f32[3,24,128]{2,1,0:T(8,128)S(1)}, u32[]{:S(2)}, u32[]{:S(2)}) collective-permute-start(f32[3,24,128]{2,1,0:T(8,128)S(1)} %scatter.9), channel_id=1, source_target_pairs={{0,1},{1,0},{2,3},{3,2},{4,5},{5,4},{6,7},{7,6},{8,9},{9,8},{10,11... | collective-permute-start | bytes 110600 | tf_op jit(solution)/shard_map/ppermute | solution.py:417
  119.8 6.0 %collective-permute-start.14 = (f32[3,24,128]{2,1,0:T(8,128)S(1)}, f32[3,24,128]{2,1,0:T(8,128)S(1)}, u32[]{:S(2)}, u32[]{:S(2)}) collective-permute-start(f32[3,24,128]{2,1,0:T(8,128)S(1)} %add.98), channel_id=1, source_target_pairs={{0,2},{1,3},{2,0},{3,1},{4,6},{5,7},{6,4},{7,5},{8,10},{9,11},{10,... | collective-permute-start | bytes 110600 | tf_op jit(solution)/shard_map/ppermute | solution.py:417
  125.8 8.4 %collective-permute-start.15 = (f32[3,24,128]{2,1,0:T(8,128)S(1)}, f32[3,24,128]{2,1,0:T(8,128)S(1)}, u32[]{:S(2)}, u32[]{:S(2)}) collective-permute-start(f32[3,24,128]{2,1,0:T(8,128)S(1)} %add.99), channel_id=1, source_target_pairs={{0,4},{1,5},{2,6},{3,7},{4,0},{5,1},{6,2},{7,3},{8,12},{9,13},{10,... | collective-permute-start | bytes 110600 | tf_op jit(solution)/shard_map/ppermute | solution.py:417

commit v2 on v1

v2 whole, which is shorter than its diff:
```python
import functools
import jax
import jax.numpy as jnp
from jax import lax
from jax.experimental import pallas as pl
from jax.experimental.pallas import tpu as pltpu
from jax.sharding import PartitionSpec as P

STEPS = 2
SUBS = 3
ROWS = 16
LANES = 128

sub_step = 0.1
macro_step = 0.3
viscosity = 0.5
modulus = 4.0
target_flow = 0.8

TRACKS = 3 * SUBS + 2
SENT = 3 * SUBS + 3 + 4
KEPT = 0.85
EXTRA = 16
TOP_ROW = ROWS + 3
BOTTOM_ROW = ROWS + 4
UNROLL = 4
VMEM_LIMIT = 32 * 1024 * 1024


def left(v):
    return pltpu.roll(v, 1, 1)


def right(v):
    return pltpu.roll(v, LANES - 1, 1)


def above(v):
    return pltpu.roll(v, 1, 0)


def below(v):
    return pltpu.roll(v, v.shape[0] - 1, 0)


def row_index(rows):
    return lax.broadcasted_iota(jnp.int32, (rows, LANES), 0)


def neighbour_weights(speed, flag):
    step = sub_step * speed
    zero = jnp.zeros_like(step)
    return jnp.where(flag == 1, step, zero), jnp.where(flag == 1, zero, -step)


def split(v):
    first = v.astype(jnp.bfloat16).astype(jnp.float32)
    rest = v - first
    second = rest.astype(jnp.bfloat16).astype(jnp.float32)
    third = (rest - second).astype(jnp.bfloat16).astype(jnp.float32)
    return first, second, third


def total(flow_ref, which):
    flow = jnp.sum(flow_ref[...], axis=0, keepdims=True)
    return flow[:, which : which + 1] + flow[:, which + 2 : which + 3] + flow[:, which + 4 : which + 5]


def updated_speed(fields_total, speed, halo_ref, stress_refs, flow_ref, fluid):
    row = row_index(ROWS)
    scale = modulus / fields_total

    def stress(c, rows):
        return scale * (stress_refs[0][c, rows, :] + stress_refs[1][c, rows, :]) - (modulus if c != 1 else 0.0)

    main = [stress(c, slice(0, ROWS)) for c in range(3)]
    before = [stress(c, slice(TOP_ROW, TOP_ROW + 1)) for c in range(3)]
    after = [stress(c, slice(BOTTOM_ROW, BOTTOM_ROW + 1)) for c in range(3)]
    mean_flow = total(flow_ref, 0) / total(flow_ref, 1)

    def up(v, edge):
        return jnp.where(row == 0, edge, above(v))

    def down(v, edge):
        return jnp.where(row == ROWS - 1, edge, below(v))

    new = []
    for c in range(2):
        v = speed[c]
        laplace = up(v, halo_ref[c : c + 1, :]) + down(v, halo_ref[2 + c : 3 + c, :]) + left(v) + right(v) - 4.0 * v
        along_x = down(main[c], after[c]) - up(main[c], before[c])
        along_y = right(main[c + 1]) - left(main[c + 1])
        divergence = along_x * 0.5 + along_y * 0.5
        v = v + macro_step * (divergence + viscosity * laplace)
        if c == 0:
            v = v + (target_flow - mean_flow)
        new.append(fluid * v)
    return new


def relaxation(relax_ref, f):
    relax = jnp.full((8, LANES), relax_ref[f], jnp.float32)
    return sub_step * (0.5 / relax), jnp.sqrt(sub_step / relax)


def doubled(v):
    return jnp.concatenate([v, v], axis=0)


def slab_weights(sx, sy, flag_x, flag_y):
    row = row_index(ROWS)
    zero = jnp.zeros((ROWS, LANES), jnp.float32)

    def grad_x(v):
        return (jnp.where(row == ROWS - 1, zero, below(v)) - jnp.where(row == 0, zero, above(v))) * 0.5

    def grad_y(v):
        return (right(v) - left(v)) * 0.5

    gxx, gxy = sub_step * grad_x(sx), sub_step * grad_x(sy)
    gyx, gyy = sub_step * grad_y(sx), sub_step * grad_y(sy)
    wa, wb = neighbour_weights(sx, flag_x)
    wl, wr = neighbour_weights(sy, flag_y)
    centre = 1.0 - wa - wb - wl - wr
    wa = jnp.where(row == 0, zero, wa)
    wb = jnp.where(row == ROWS - 1, zero, wb)
    return centre, wa, wb, wl, wr, gxx, gxy, gyx, gyy


def substep(q, diagonal, weights, extra):
    _, wa, wb, wl, wr, _, gxy, gyx, _ = weights
    new = []
    for c in range(3):
        v = q[c]
        acc = diagonal[c] * v + extra[c]
        acc = acc + (wl * left(v) + wr * right(v))
        acc = acc + (wa * above(v) + wb * below(v))
        if c == 0:
            acc = acc + gyx * q[1]
        elif c == 1:
            acc = acc + gxy * q[0]
        new.append(acc)
    return new


def edge_kernel(nf, fields_total, first, *refs):
    refs = list(refs)

    def take(count):
        taken = refs[:count]
        del refs[:count]
        return taken

    relax_ref, odd_ref, speed_ref, solid_ref, upwind_ref, fields_ref, wiener_ref = take(7)
    if not first:
        halo_ref, stress_ref, other_ref, flow_ref = take(4)
    top_ref, bottom_ref, send1_ref, send2_ref, sums_ref = take(5)
    if not first:
        (new_speed_ref,) = take(1)
    top_extra, bottom_extra = refs

    fluid = (1 - solid_ref[...]).astype(jnp.float32)
    sx, sy = speed_ref[0], speed_ref[1]
    if not first:
        sx, sy = updated_speed(fields_total, (sx, sy), halo_ref, (stress_ref, other_ref), flow_ref, fluid)
        new_speed_ref[0] = sx
        new_speed_ref[1] = sy
    flow = jnp.sum(jnp.sum(fluid * sx, axis=0, keepdims=True), axis=1, keepdims=True)
    cells = jnp.sum(jnp.sum(fluid, axis=0, keepdims=True), axis=1, keepdims=True)
    lane = lax.broadcasted_iota(jnp.int32, (1, LANES), 1)
    sums = jnp.where(lane == 0, flow, jnp.where(lane == 1, cells, 0.0))
    sums_ref[...] = sums

    row = row_index(8)
    flag_x, flag_y = upwind_ref[0], upwind_ref[1]

    def packed(v):
        return jnp.where(row < 4, v[0:8], v[8:16])

    weights = [packed(w) for w in slab_weights(sx, sy, flag_x, flag_y)]
    centre, gxx, gyy = weights[0], weights[5], weights[8]

    def body(f):
        delta, spread = relaxation(relax_ref, f)
        base = centre - delta
        diagonal = (base + gxx, base + gyy, base)
        q = [packed(fields_ref[c, f]) for c in range(3)]
        for k in range(SUBS + 1):
            for c in range(3 if k < SUBS else 2):
                top_ref[3 * k + c, pl.ds(f, 1), :] = q[c][0:1, :]
                bottom_ref[3 * k + c, pl.ds(f, 1), :] = q[c][7:8, :]
            if k < SUBS:
                kicks = [spread * packed(wiener_ref[k, c, f].astype(jnp.float32)) for c in range(3)]
                q = substep(q, diagonal, weights, kicks)

    def some(j, carry):
        for u in range(UNROLL):
            body(j * UNROLL + u)
        return carry

    lax.fori_loop(0, nf // UNROLL, some, 0)

    first_term, second_term, third_term = split(jnp.broadcast_to(sums, (8, LANES)))
    packed_sums = (first_term + pltpu.roll(second_term, 2, 1) + pltpu.roll(third_term, 4, 1))[0:1]
    terms = (split(sx), split(sy))
    flags = (flag_x.astype(jnp.float32), flag_y.astype(jnp.float32))
    for extra, near, far in ((top_extra, 0, 1), (bottom_extra, ROWS - 1, ROWS - 2)):
        for c in range(2):
            for i in range(3):
                extra[3 * c + i : 3 * c + i + 1, :] = terms[c][i][near : near + 1, :]
                extra[6 + 3 * c + i : 7 + 3 * c + i, :] = terms[c][i][far : far + 1, :]
        extra[12:13, :] = flags[0][near : near + 1, :]
        extra[13:14, :] = flags[1][near : near + 1, :]
        extra[14:15, :] = flags[0][far : far + 1, :]
        extra[15:16, :] = packed_sums

    odd = jnp.full((nf, LANES), odd_ref[0], jnp.int32) == 1
    for send_ref, one_ref, two_ref in ((send1_ref, top_ref, bottom_ref), (send2_ref, bottom_ref, top_ref)):

        def put(t, v):
            rounded = v.astype(jnp.bfloat16)
            send_ref[nf * t : nf * t + nf, :] = rounded
            return v - rounded.astype(jnp.float32)

        for c in range(3):
            error = jnp.zeros((nf, LANES), jnp.float32)
            for k in range(SUBS):
                error = put(3 * k + c, jnp.where(odd, one_ref[3 * k + c], two_ref[3 * k + c]) + KEPT * error)
            put(3 * SUBS + c, error)
            if c < 2:
                error = put(3 * SUBS + 3 + c, jnp.where(odd, one_ref[3 * SUBS + c], two_ref[3 * SUBS + c]))
                put(3 * SUBS + 5 + c, error)
    odd = jnp.full((EXTRA, LANES), odd_ref[0], jnp.int32) == 1
    top, bottom = top_extra[...], bottom_extra[...]
    tail = nf * SENT
    send1_ref[tail : tail + EXTRA, :] = jnp.where(odd, top, bottom).astype(jnp.bfloat16)
    send2_ref[tail : tail + EXTRA, :] = jnp.where(odd, bottom, top).astype(jnp.bfloat16)


def own_kernel(nf, relax_ref, speed_ref, upwind_ref, fields_ref, wiener_ref, out_ref):
    weights = slab_weights(speed_ref[0], speed_ref[1], upwind_ref[0], upwind_ref[1])
    centre, gxx, gyy = weights[0], weights[5], weights[8]

    def body(f):
        delta, spread = [doubled(v) for v in relaxation(relax_ref, f)]
        base = centre - delta
        diagonal = (base + gxx, base + gyy, base)
        q = [fields_ref[c, f] for c in range(3)]
        for k in range(SUBS):
            kicks = [spread * wiener_ref[k, c, f].astype(jnp.float32) for c in range(3)]
            q = substep(q, diagonal, weights, kicks)
        for c in range(3):
            out_ref[c, f] = q[c]

    def some(j, carry):
        for u in range(UNROLL):
            body(j * UNROLL + u)
        return carry

    lax.fori_loop(0, nf // UNROLL, some, 0)


def join_kernel(nf, first, *refs):
    refs = list(refs)
    relax_ref, side_ref, speed_ref, upwind_ref, own_ref, top_ref, bottom_ref, recv_ref = refs[:8]
    refs = refs[8:]
    if not first:
        stress_in, halo_in = refs[:2]
        refs = refs[2:]
    out_ref, stress_ref, halo_ref, upper_ref, lower_ref = refs
    side = side_ref[0]
    top = jnp.full((nf, LANES), side, jnp.int32) == 1
    last = 3 * (SUBS - 1)
    for t in range(TRACKS):
        if t < last:
            places = (t,)
        elif t < 3 * SUBS:
            places = (t, t + 3)
        else:
            places = (t + 3, t + 5)
        terms = [recv_ref[nf * p : nf * p + nf, :].astype(jnp.float32) for p in places]
        got = sum(terms[1:], terms[0])
        upper_ref[t] = jnp.where(top, got, bottom_ref[t])
        lower_ref[t] = jnp.where(top, top_ref[t], got)
    tail = nf * SENT
    extra = recv_ref[tail : tail + EXTRA, :].astype(jnp.float32)

    row = row_index(8)
    top = jnp.full((8, LANES), side, jnp.int32) == 1
    zero = jnp.zeros((8, LANES), jnp.float32)
    own_rows = (top & (row >= 4)) | (~top & (row < 4))
    near_row = (top & (row == 3)) | (~top & (row == 4))
    far_row = (top & (row == 2)) | (~top & (row == 5))

    def strip(values, near, far):
        own = pltpu.roll(jnp.where(top, values[0:8], values[8:16]), 4, 0)
        return jnp.where(own_rows, own, jnp.where(near_row, near, jnp.where(far_row, far, zero)))

    def joined(i):
        return extra[i : i + 1, :] + extra[i + 1 : i + 2, :] + extra[i + 2 : i + 3, :]

    near_x, near_y = joined(0), joined(3)
    halo = jnp.where(row % 2 == 0, near_x, near_y)
    mine = (top & (row < 2)) | (~top & (row >= 2) & (row < 4))
    halo = jnp.where(mine, halo, zero)
    halo_ref[...] = halo if first else halo + halo_in[...]
    sx = strip(speed_ref[0], near_x, joined(6))
    sy = strip(speed_ref[1], near_y, joined(9))
    flag_x = strip(upwind_ref[0].astype(jnp.float32), extra[12:13, :], extra[14:15, :])
    flag_y = strip(upwind_ref[1].astype(jnp.float32), extra[13:14, :], zero)

    upper = row == 3
    lower = row == 4
    half = 0.5 * sub_step
    gxx = half * (below(sx) - above(sx))
    gxy = half * (below(sy) - above(sy))
    gyx = half * (right(sx) - left(sx))
    gyy = half * (right(sy) - left(sy))
    wa, wb = neighbour_weights(sx, flag_x)
    wl, wr = neighbour_weights(sy, flag_y)
    centre = 1.0 - wa - wb - wl - wr
    weights = (centre, wa, wb, wl, wr, gxx, gxy, gyx, gyy)
    from_upper = jnp.where(lower, wa, zero)
    from_lower = jnp.where(upper, wb, zero)
    upper_y = jnp.where(upper, half * below(sy), zero)
    lower_y = jnp.where(lower, -half * above(sy), zero)
    from_upper_x = from_upper + jnp.where(upper, half * below(sx), zero)
    from_lower_x = from_lower + jnp.where(lower, -half * above(sx), zero)
    start = pl.multiple_of((1 - side) * 8, 8)

    def body(f, sums):
        delta, _ = relaxation(relax_ref, f)
        base = centre - delta
        diagonal = (base + gxx, base + gyy, base)

        def spread_row(ref, t):
            return jnp.broadcast_to(ref[t, pl.ds(f, 1), :], (8, LANES))

        d = None
        for k in range(SUBS):
            hu = [spread_row(upper_ref, 3 * k + c) for c in range(3)]
            hl = [spread_row(lower_ref, 3 * k + c) for c in range(3)]
            new = [
                from_upper_x * hu[0] + from_lower_x * hl[0],
                from_upper * hu[1] + from_lower * hl[1] + (upper_y * hu[0] + lower_y * hl[0]),
                from_upper * hu[2] + from_lower * hl[2],
            ]
            d = new if d is None else substep(d, diagonal, weights, new)
        full = []
        edge = []
        for c in range(3):
            half_rows = own_ref[c, f, pl.ds(start, 8), :]
            v = half_rows + pltpu.roll(jnp.where(own_rows, d[c], zero), 4, 0)
            out_ref[c, f, pl.ds(start, 8), :] = v
            rest = pl.multiple_of(8 - start, 8)
            out_ref[c, f, pl.ds(rest, 8), :] = own_ref[c, f, pl.ds(rest, 8), :]
            if c < 2:
                t = 3 * SUBS + c
                full.append(v)
                edge.append(d[c] + jnp.where(upper, spread_row(upper_ref, t), spread_row(lower_ref, t)))
        pairs = ((0, 0), (0, 1), (1, 1))
        return tuple(s + full[i] * full[j] for s, (i, j) in zip(sums[:3], pairs)) + tuple(
            s + edge[i] * edge[j] for s, (i, j) in zip(sums[3:], pairs)
        )

    def some(j, sums):
        for u in range(UNROLL):
            sums = body(j * UNROLL + u, sums)
        return sums

    sums = lax.fori_loop(0, nf // UNROLL, some, (zero,) * 6)
    for c in range(3):
        edge = jnp.where(near_row, sums[3 + c], zero)
        if first:
            stress_ref[c, 0:ROWS, :] = jnp.zeros((ROWS, LANES), jnp.float32)
        else:
            stress_ref[c, 0:ROWS, :] = stress_in[c, 0:ROWS, :]
            edge = edge + stress_in[c, ROWS : ROWS + 8, :]
        stress_ref[c, pl.ds(start, 8), :] = sums[c]
        stress_ref[c, ROWS : ROWS + 8, :] = edge


def last_kernel(fields_total, speed_ref, solid_ref, halo_ref, stress_ref, other_ref, flow_ref, out_ref):
    fluid = (1 - solid_ref[...]).astype(jnp.float32)
    speed = (speed_ref[0], speed_ref[1])
    sx, sy = updated_speed(fields_total, speed, halo_ref, (stress_ref, other_ref), flow_ref, fluid)
    out_ref[0] = sx
    out_ref[1] = sy


def vmem():
    return pl.BlockSpec(memory_space=pltpu.VMEM)


def smem():
    return pl.BlockSpec(memory_space=pltpu.SMEM)


def shaped(shape, dtype=jnp.float32):
    return jax.ShapeDtypeStruct(shape, dtype)


def whole(shape):
    return pl.BlockSpec(shape, lambda i: (0,) * len(shape))


def step_block(step, shape):
    return pl.BlockSpec((SUBS,) + shape[1:], lambda i: (step,) + (0,) * (len(shape) - 1))


def cost(flops, *arrays):
    size = sum(v.size * v.dtype.itemsize for v in arrays)
    return pl.CostEstimate(flops=flops, bytes_accessed=size, transcendentals=0)


def params():
    return pltpu.CompilerParams(vmem_limit_bytes=VMEM_LIMIT)


def edge_steps(step, fields_total, relax, odd, speed, solid, upwind, fields, wiener, extra):
    nf = fields.shape[1]
    first = step == 0
    size = nf * SENT + EXTRA
    outs = [
        shaped((TRACKS, nf, LANES)),
        shaped((TRACKS, nf, LANES)),
        shaped((size, LANES), jnp.bfloat16),
        shaped((size, LANES), jnp.bfloat16),
        shaped((1, LANES)),
    ]
    if not first:
        outs.append(shaped(speed.shape))
    got = pl.pallas_call(
        functools.partial(edge_kernel, nf, fields_total, first),
        grid=(1,),
        out_shape=outs,
        in_specs=[smem(), smem()]
        + [whole(v.shape) for v in (speed, solid, upwind, fields)]
        + [step_block(step, wiener.shape)]
        + [whole(v.shape) for v in extra],
        out_specs=[whole(o.shape) for o in outs],
        scratch_shapes=[pltpu.VMEM((EXTRA, LANES), jnp.float32)] * 2,
        compiler_params=params(),
        name="edge_steps",
    )(relax, odd, speed, solid, upwind, fields, wiener, *extra)
    return list(got) + ([speed] if first else [])


def own_steps(step, relax, speed, upwind, fields, wiener):
    return pl.pallas_call(
        functools.partial(own_kernel, fields.shape[1]),
        grid=(1,),
        out_shape=shaped(fields.shape),
        in_specs=[smem()] + [whole(v.shape) for v in (speed, upwind, fields)] + [step_block(step, wiener.shape)],
        out_specs=whole(fields.shape),
        compiler_params=params(),
        cost_estimate=cost(60 * fields.size, fields, fields, fields),
        name="own_steps",
    )(relax, speed, upwind, fields, wiener)


def join(relax, side, speed, upwind, own, top, bottom, recv, before=()):
    nf = own.shape[1]
    return pl.pallas_call(
        functools.partial(join_kernel, nf, not before),
        out_shape=[shaped(own.shape), shaped((3, ROWS + 8, LANES)), shaped((8, LANES))],
        in_specs=[smem(), smem()] + [vmem()] * (6 + len(before)),
        out_specs=[vmem()] * 3,
        scratch_shapes=[pltpu.VMEM((TRACKS, nf, LANES), jnp.float32)] * 2,
        compiler_params=params(),
        cost_estimate=cost(20 * own.size, own, own),
        name="join",
    )(relax, side, speed, upwind, own, top, bottom, recv, *before)


def last_speed(fields_total, speed, solid, halo, stress, other, flow):
    return pl.pallas_call(
        functools.partial(last_kernel, fields_total),
        out_shape=shaped(speed.shape),
        in_specs=[vmem()] * 6,
        out_specs=vmem(),
        name="last_speed",
    )(speed, solid, halo, stress, other, flow)


def swapped(value, axis, bit):
    count = lax.axis_size(axis)
    return lax.ppermute(value, axis, [(i, i ^ bit) for i in range(count)])


def field_sum(value):
    bit = 1
    while 2 * bit < lax.axis_size("field"):
        value = value + swapped(value, "field", bit)
        bit *= 2
    return value, swapped(value, "field", bit)


def flow_sums(sums, recv1, recv2):
    value = sums + recv1[recv1.shape[0] - 1 :].astype(jnp.float32)
    value = value + swapped(value, "slab", 2)
    value = value + swapped(value, "slab", 4)
    value, recv2 = lax.optimization_barrier((value, recv2))
    slabs, parts = lax.axis_size("slab"), lax.axis_size("field")
    assert slabs == 8 * parts
    pairs = [(((s + 8 * f) % slabs) * parts + f, s * parts + f) for s in range(slabs) for f in range(parts)]
    return lax.ppermute(value, ("slab", "field"), pairs), recv2


def per_device(conform, velocity, solid_mask, upwind, relax_time, wiener):
    slabs = lax.axis_size("slab")
    fields_total = conform.shape[1] * lax.axis_size("field")
    odd = (lax.axis_index("slab") % 2).astype(jnp.int32).reshape(1)
    near_pairs = [(i, i ^ 1) for i in range(slabs)]
    far_pairs = [(i, (i + 1) % slabs if i % 2 else (i - 1) % slabs) for i in range(slabs)]
    fields, speed, extra = conform, velocity, ()
    for step in range(STEPS):
        top, bottom, send1, send2, sums, speed = edge_steps(
            step, fields_total, relax_time, odd, speed, solid_mask, upwind, fields, wiener, extra
        )
        recv1 = lax.ppermute(send1, "slab", near_pairs)
        recv2 = lax.ppermute(send2, "slab", far_pairs)
        if step == 0:
            flow = lax.all_gather(sums, "slab", axis=0, tiled=True)
            recv1, flow = lax.optimization_barrier((recv1, flow))
        else:
            flow, recv2 = flow_sums(sums, recv1, recv2)
        own = own_steps(step, relax_time, speed, upwind, fields, wiener)
        fields, stress, halo = join(relax_time, odd, speed, upwind, own, top, bottom, recv1)
        fields, stress, halo = join(relax_time, 1 - odd, speed, upwind, fields, top, bottom, recv2, (stress, halo))
        if step > 0:
            stress = lax.dynamic_update_slice(stress, flow[None], (0, ROWS, 0))
        stress, other = field_sum(stress)
        if step > 0:
            flow = stress[0, ROWS : ROWS + 1] + other[0, ROWS : ROWS + 1]
        extra = (halo, stress, other, flow)
    speed = last_speed(fields_total, speed, solid_mask, *extra)
    return (fields, speed)


def solution(mesh):
    placed = (
        P(None, "field", "slab", None),
        P(None, "slab", None),
        P("slab", None),
        P(None, "slab", None),
        P("field"),
        P(None, None, "field", "slab", None),
    )
    return jax.shard_map(
        per_device,
        mesh=mesh,
        in_specs=placed,
        out_specs=(P(None, "field", "slab", None), P(None, "slab", None)),
        check_vma=False,
    )
```

time: 138 us -> 319 us (2.31)
  blocking collectives: 0 us -> 186 us
  starting transfers between devices: 73.1 us -> 88.9 us
  waiting for transfers between devices: 25.4 us -> 12.6 us
  between operations: 8.39 us -> 0.89 us
    all_gather x0 -> x1, blocking collectives: none -> 186 us  [per_device(): flow = lax.all_gather(sums, 'slab', axis=0, tiled=True)]
    ppermute x10 -> x8, starting transfers between devices: 41.5 us -> 63.1 us  [swapped(): return lax.ppermute(value, axis, [(i, i ^ bit) for i in range(count)])]
    ppermute x10 -> x8, waiting for transfers between devices: 25.4 us -> 11.8 us  [swapped(): return lax.ppermute(value, axis, [(i, i ^ bit) for i in range(count)])]
    ppermute x2 -> x1, starting transfers between devices: 5.89 us -> 1.91 us  [flow_sums(): return (lax.ppermute(value, ('slab', 'field'), pairs), recv2)]
    pallas_call x4 -> x8, Pallas kernels: 19.1 us -> 21.2 us  [the longest x4 9.44 us: join(): pl.pallas_call(functools.partial(join_kernel, nf, not before), out_shape=...]
  transfers between devices with their start and end apart: 16 -> 13, of which waited for: 10 -> 8; matrix products, arithmetic and copies ran while one was open for 1% -> 0% of each run, Pallas kernels for 6% -> 4%
where the time goes in v2:
time: 319 us; the launch traced here: 318 us
  blocking collectives  186 us (58%)
  starting transfers between devices  88.9 us (28%)
  Pallas kernels  22.9 us (7%)
  waiting for transfers between devices  12.6 us (4%)
  local copies, waits for them, and re-layouts  6.3 us (2%)
    all_gather x1, blocking collectives, per_device(): flow = lax.all_gather(sums, 'slab', axis=0, tiled=True)  186 us
    ppermute x8, starting transfers between devices, swapped(): return lax.ppermute(value, axis, [(i, i ^ bit) for i in range(count)])  63.1 us
    ppermute x2, starting transfers between devices, per_device(): recv2 = lax.ppermute(send2, 'slab', far_pairs)  17.4 us
    ppermute x8, waiting for transfers between devices, swapped(): return lax.ppermute(value, axis, [(i, i ^ bit) for i in range(count)])  11.8 us
    pallas_call x4, Pallas kernels, join(): pl.pallas_call(functools.partial(join_kernel, nf, not before), out_shape=...  9.44 us
    ppermute x2, starting transfers between devices, per_device(): recv1 = lax.ppermute(send1, 'slab', near_pairs)  6.51 us
  transfers between devices with their start and end apart: 13, of which 8 were waited for; matrix products, arithmetic and copies ran while one was open for 0% of the time, Pallas kernels for 4%

profile of v2, /device:TPU:1, one launch (start us, length us, event | category | flops | bytes accessed | tf_op | source)
XLA Modules:
  0.0 317.8 jit_solution(9880823348516522379)
XLA Ops:
  0.7 1.7 copy-done
  2.3 1.1 copy-done.2
  6.2 2.6 edge_steps.2
  8.9 3.9 %collective-permute-start = (bf16[528,128]{1,0:T(8,128)(2,1)S(1)}, bf16[528,128]{1,0:T(8,128)(2,1)S(1)}, u32[]{:S(2)}, u32[]{:S(2)}) collective-permute-start(bf16[528,128]{1,0:T(8,128)(2,1)S(1)} %get-tuple-element.31), channel_id=1, source_target_pairs={{0,8},{8,0},{16,24},{24,16},{32,40},{40,32},{48,56},{56,48},{64,72... | collective-permute-start | bytes 405512 | tf_op jit(solution)/shard_map/ppermute | solution.py:521
  12.8 15.1 %collective-permute-start.1 = (bf16[528,128]{1,0:T(8,128)(2,1)S(1)}, bf16[528,128]{1,0:T(8,128)(2,1)S(1)}, u32[]{:S(2)}, u32[]{:S(2)}) collective-permute-start(bf16[528,128]{1,0:T(8,128)(2,1)S(1)} %get-tuple-element.35), channel_id=1, source_target_pairs={{0,504},{8,16},{16,8},{24,32},{32,24},{40,48},{48,40},{56,64},{64,... | collective-permute-start | bytes 405512 | tf_op jit(solution)/shard_map/ppermute | solution.py:522
  27.9 3.1 own_steps.2.refs_4_
  31.1 185.7 %all-gather = f32[64,1,128]{2,1,0:T(1,128)S(1)} all-gather(f32[1,1,128]{2,1,0:T(1,128)S(1)} %bitcast.7), channel_id=1, replica_groups=mesh['slab'=64,'field'=8] {'slab'}, dimensions={0}, use_global_device_ids=true | all-gather | bytes 33280 | tf_op jit(solution)/shard_map/all_gather | solution.py:524
  216.8 2.2 join.4
  219.0 2.1 join.5
  221.1 29.7 %collective-permute-start.2 = (f32[3,24,128]{2,1,0:T(8,128)S(1)}, f32[3,24,128]{2,1,0:T(8,128)S(1)}, u32[]{:S(2)}, u32[]{:S(2)}) collective-permute-start(f32[3,24,128]{2,1,0:T(8,128)S(1)} %get-tuple-element.40), channel_id=1, source_target_pairs={{0,1},{1,0},{2,3},{3,2},{4,5},{5,4},{6,7},{7,6},{8,9},{9,8},{10,11... | collective-permute-start | bytes 110600 | tf_op jit(solution)/shard_map/ppermute | solution.py:488
  250.8 0.8 collective-permute-done.2
  251.7 2.9 collective-permute-start.3
  254.6 1.9 collective-permute-done.3
  256.5 4.7 %collective-permute-start.4 = (f32[3,24,128]{2,1,0:T(8,128)S(1)}, f32[3,24,128]{2,1,0:T(8,128)S(1)}, u32[]{:S(2)}, u32[]{:S(2)}) collective-permute-start(f32[3,24,128]{2,1,0:T(8,128)S(1)} %add.32.refs_8_), channel_id=1, source_target_pairs={{0,4},{1,5},{2,6},{3,7},{4,0},{5,1},{6,2},{7,3},{8,12},{9,13},{10,... | collective-permute-start | bytes 110600 | tf_op jit(solution)/shard_map/ppermute | solution.py:488
  261.1 1.3 collective-permute-done.4.refs_9_
  262.5 2.8 edge_steps.3
  265.3 2.6 collective-permute-start.5
  267.9 2.3 collective-permute-start.8
  270.2 0.9 collective-permute-done.5.refs_7_
  271.1 3.3 %collective-permute-start.6 = (f32[1,128]{1,0:T(1,128)S(1)}, f32[1,128]{1,0:T(1,128)S(1)}, u32[]{:S(2)}, u32[]{:S(2)}) collective-permute-start(f32[1,128]{1,0:T(1,128)S(1)} %fusion.1), channel_id=1, source_target_pairs={{0,16},{8,24},{16,0},{24,8},{32,48},{40,56},{48,32},{56,40},{64,80... | collective-permute-start | bytes 1544 | tf_op jit(solution)/shard_map/ppermute | solution.py:488
  274.4 3.1 own_steps.3.refs_4_
  277.5 1.9 collective-permute-start.7
  279.5 2.1 join.6
  281.6 4.1 %collective-permute-done.7 = f32[1,128]{1,0:T(1,128)S(1)} collective-permute-done((f32[1,128]{1,0:T(1,128)S(1)}, f32[1,128]{1,0:T(1,128)S(1)}, u32[]{:S(2)}, u32[]{:S(2)}) %collective-permute-start.7) | collective-permute-done | bytes 544 | tf_op jit(solution)/shard_map/ppermute | solution.py:488
  285.7 1.9 collective-permute-start.9
  287.7 3.0 join.7
  291.3 9.8 %collective-permute-start.10 = (f32[3,24,128]{2,1,0:T(8,128)S(1)}, f32[3,24,128]{2,1,0:T(8,128)S(1)}, u32[]{:S(2)}, u32[]{:S(2)}) collective-permute-start(f32[3,24,128]{2,1,0:T(8,128)S(1)} %dynamic_update_slice.3), channel_id=1, source_target_pairs={{0,1},{1,0},{2,3},{3,2},{4,5},{5,4},{6,7},{7,6},{8,9},{9,8},{10,11... | collective-permute-start | bytes 110600 | tf_op jit(solution)/shard_map/ppermute | solution.py:488
  302.0 3.5 %collective-permute-start.11 = (f32[3,24,128]{2,1,0:T(8,128)S(1)}, f32[3,24,128]{2,1,0:T(8,128)S(1)}, u32[]{:S(2)}, u32[]{:S(2)}) collective-permute-start(f32[3,24,128]{2,1,0:T(8,128)S(1)} %add.36), channel_id=1, source_target_pairs={{0,2},{1,3},{2,0},{3,1},{4,6},{5,7},{6,4},{7,5},{8,10},{9,11},{10,... | collective-permute-start | bytes 110600 | tf_op jit(solution)/shard_map/ppermute | solution.py:488
  305.4 1.3 collective-permute-done.11
  306.8 7.3 %collective-permute-start.12 = (f32[3,24,128]{2,1,0:T(8,128)S(1)}, f32[3,24,128]{2,1,0:T(8,128)S(1)}, u32[]{:S(2)}, u32[]{:S(2)}) collective-permute-start(f32[3,24,128]{2,1,0:T(8,128)S(1)} %add.37.stress_ref), channel_id=1, source_target_pairs={{0,4},{1,5},{2,6},{3,7},{4,0},{5,1},{6,2},{7,3},{8,12},{9,13},{10,... | collective-permute-start | bytes 110600 | tf_op jit(solution)/shard_map/ppermute | solution.py:488
  314.1 1.5 collective-permute-done.12.other_ref
  316.2 1.6 last_speed.1
  (39 shorter events, 4.9 us)
Async XLA Ops:
  0.6 1.7 copy-start
  2.3 1.1 copy-start.2
  3.4 0.7 copy-start.3
  4.2 0.7 copy-start.5
  4.9 0.7 copy-start.7
  5.6 0.7 copy-start.9
  8.9 207.9 %collective-permute-start = (bf16[528,128]{1,0:T(8,128)(2,1)S(1)}, bf16[528,128]{1,0:T(8,128)(2,1)S(1)}, u32[]{:S(2)}, u32[]{:S(2)}) collective-permute-start(bf16[528,128]{1,0:T(8,128)(2,1)S(1)} %get-tuple-element.31), channel_id=1, source_target_pairs={{0,8},{8,0},{16,24},{24,16},{32,40},{40,32},{48,56},{56,48},{64,72... | collective-permute-start | bytes 405512 | tf_op jit(solution)/shard_map/ppermute | solution.py:521
  12.8 206.1 %collective-permute-start.1 = (bf16[528,128]{1,0:T(8,128)(2,1)S(1)}, bf16[528,128]{1,0:T(8,128)(2,1)S(1)}, u32[]{:S(2)}, u32[]{:S(2)}) collective-permute-start(bf16[528,128]{1,0:T(8,128)(2,1)S(1)} %get-tuple-element.35), channel_id=1, source_target_pairs={{0,504},{8,16},{16,8},{24,32},{32,24},{40,48},{48,40},{56,64},{64,... | collective-permute-start | bytes 405512 | tf_op jit(solution)/shard_map/ppermute | solution.py:522
  31.1 231.4 %copy-start.1 = (bf16[6,3,32,16,128]{4,3,2,1,0:T(8,128)(2,1)S(1)}, bf16[6,3,32,16,128]{4,3,2,1,0:T(8,128)(2,1)}, u32[]{:S(2)}) copy-start(bf16[6,3,32,16,128]{4,3,2,1,0:T(8,128)(2,1)} %wiener_ref.3) | copy-start | bytes 7077892
  31.1 231.4 %copy-start.8 = (s32[16,128]{1,0:T(8,128)S(1)}, s32[16,128]{1,0:T(8,128)}, u32[]{:S(2)}) copy-start(s32[16,128]{1,0:T(8,128)} %solid_ref.1) | copy-start | bytes 24580
  221.1 30.6 %collective-permute-start.2 = (f32[3,24,128]{2,1,0:T(8,128)S(1)}, f32[3,24,128]{2,1,0:T(8,128)S(1)}, u32[]{:S(2)}, u32[]{:S(2)}) collective-permute-start(f32[3,24,128]{2,1,0:T(8,128)S(1)} %get-tuple-element.40), channel_id=1, source_target_pairs={{0,1},{1,0},{2,3},{3,2},{4,5},{5,4},{6,7},{7,6},{8,9},{9,8},{10,11... | collective-permute-start | bytes 110600 | tf_op jit(solution)/shard_map/ppermute | solution.py:488
  251.7 4.8 %collective-permute-start.3 = (f32[3,24,128]{2,1,0:T(8,128)S(1)}, f32[3,24,128]{2,1,0:T(8,128)S(1)}, u32[]{:S(2)}, u32[]{:S(2)}) collective-permute-start(f32[3,24,128]{2,1,0:T(8,128)S(1)} %add.31), channel_id=1, source_target_pairs={{0,2},{1,3},{2,0},{3,1},{4,6},{5,7},{6,4},{7,5},{8,10},{9,11},{10,... | collective-permute-start | bytes 110600 | tf_op jit(solution)/shard_map/ppermute | solution.py:488
  256.5 6.0 %collective-permute-start.4 = (f32[3,24,128]{2,1,0:T(8,128)S(1)}, f32[3,24,128]{2,1,0:T(8,128)S(1)}, u32[]{:S(2)}, u32[]{:S(2)}) collective-permute-start(f32[3,24,128]{2,1,0:T(8,128)S(1)} %add.32.refs_8_), channel_id=1, source_target_pairs={{0,4},{1,5},{2,6},{3,7},{4,0},{5,1},{6,2},{7,3},{8,12},{9,13},{10,... | collective-permute-start | bytes 110600 | tf_op jit(solution)/shard_map/ppermute | solution.py:488
  265.3 22.4 %copy-start.6 = (f32[2,16,128]{2,1,0:T(8,128)}, f32[2,16,128]{2,1,0:T(8,128)S(1)}, u32[]{:S(2)}) copy-start(f32[2,16,128]{2,1,0:T(8,128)S(1)} %get-tuple-element.42.speed_ref.refs_2_) | copy-start | bytes 49156
  265.3 14.1 %copy-start.4 = (s32[2,16,128]{2,1,0:T(8,128)S(1)}, s32[2,16,128]{2,1,0:T(8,128)}, u32[]{:S(2)}) copy-start(s32[2,16,128]{2,1,0:T(8,128)} %refs_3_.11) | copy-start | bytes 49156
  265.3 5.8 %collective-permute-start.5 = (bf16[528,128]{1,0:T(8,128)(2,1)S(1)}, bf16[528,128]{1,0:T(8,128)(2,1)S(1)}, u32[]{:S(2)}, u32[]{:S(2)}) collective-permute-start(bf16[528,128]{1,0:T(8,128)(2,1)S(1)} %get-tuple-element.45), channel_id=1, source_target_pairs={{0,8},{8,0},{16,24},{24,16},{32,40},{40,32},{48,56},{56,48},{64,72... | collective-permute-start | bytes 405512 | tf_op jit(solution)/shard_map/ppermute | solution.py:521
  267.9 17.8 %collective-permute-start.8 = (bf16[528,128]{1,0:T(8,128)(2,1)S(1)}, bf16[528,128]{1,0:T(8,128)(2,1)S(1)}, u32[]{:S(2)}, u32[]{:S(2)}) collective-permute-start(bf16[528,128]{1,0:T(8,128)(2,1)S(1)} %get-tuple-element.48), channel_id=1, source_target_pairs={{0,504},{8,16},{16,8},{24,32},{32,24},{40,48},{48,40},{56,64},{64,... | collective-permute-start | bytes 405512 | tf_op jit(solution)/shard_map/ppermute | solution.py:522
  271.1 6.4 %collective-permute-start.6 = (f32[1,128]{1,0:T(1,128)S(1)}, f32[1,128]{1,0:T(1,128)S(1)}, u32[]{:S(2)}, u32[]{:S(2)}) collective-permute-start(f32[1,128]{1,0:T(1,128)S(1)} %fusion.1), channel_id=1, source_target_pairs={{0,16},{8,24},{16,0},{24,8},{32,48},{40,56},{48,32},{56,40},{64,80... | collective-permute-start | bytes 1544 | tf_op jit(solution)/shard_map/ppermute | solution.py:488
  277.5 8.2 %collective-permute-start.7 = (f32[1,128]{1,0:T(1,128)S(1)}, f32[1,128]{1,0:T(1,128)S(1)}, u32[]{:S(2)}, u32[]{:S(2)}) collective-permute-start(f32[1,128]{1,0:T(1,128)S(1)} %add.34), channel_id=1, source_target_pairs={{0,32},{8,40},{16,48},{24,56},{32,0},{40,8},{48,16},{56,24},{64,96... | collective-permute-start | bytes 1544 | tf_op jit(solution)/shard_map/ppermute | solution.py:488
  285.7 5.5 %collective-permute-start.9 = (f32[1,128]{1,0:T(1,128)S(1)}, f32[1,128]{1,0:T(1,128)S(1)}, u32[]{:S(2)}, u32[]{:S(2)}) collective-permute-start(f32[1,128]{1,0:T(1,128)S(1)} %add.35), channel_id=1, source_target_pairs={{0,0},{65,1},{130,2},{195,3},{260,4},{325,5},{390,6},{455,7},{8,8}... | collective-permute-start | bytes 1544 | tf_op jit(solution)/shard_map/ppermute | solution.py:507
  290.7 0.6 copy-start.10
  291.3 10.7 %collective-permute-start.10 = (f32[3,24,128]{2,1,0:T(8,128)S(1)}, f32[3,24,128]{2,1,0:T(8,128)S(1)}, u32[]{:S(2)}, u32[]{:S(2)}) collective-permute-start(f32[3,24,128]{2,1,0:T(8,128)S(1)} %dynamic_update_slice.3), channel_id=1, source_target_pairs={{0,1},{1,0},{2,3},{3,2},{4,5},{5,4},{6,7},{7,6},{8,9},{9,8},{10,11... | collective-permute-start | bytes 110600 | tf_op jit(solution)/shard_map/ppermute | solution.py:488
  302.0 4.8 %collective-permute-start.11 = (f32[3,24,128]{2,1,0:T(8,128)S(1)}, f32[3,24,128]{2,1,0:T(8,128)S(1)}, u32[]{:S(2)}, u32[]{:S(2)}) collective-permute-start(f32[3,24,128]{2,1,0:T(8,128)S(1)} %add.36), channel_id=1, source_target_pairs={{0,2},{1,3},{2,0},{3,1},{4,6},{5,7},{6,4},{7,5},{8,10},{9,11},{10,... | collective-permute-start | bytes 110600 | tf_op jit(solution)/shard_map/ppermute | solution.py:488
  306.8 9.3 %copy-start.11 = (f32[3,24,128]{2,1,0:T(8,128)}, f32[3,24,128]{2,1,0:T(8,128)S(1)}, u32[]{:S(2)}) copy-start(f32[3,24,128]{2,1,0:T(8,128)S(1)} %add.37.stress_ref) | copy-start | bytes 110596
  306.8 8.8 %collective-permute-start.12 = (f32[3,24,128]{2,1,0:T(8,128)S(1)}, f32[3,24,128]{2,1,0:T(8,128)S(1)}, u32[]{:S(2)}, u32[]{:S(2)}) collective-permute-start(f32[3,24,128]{2,1,0:T(8,128)S(1)} %add.37.stress_ref), channel_id=1, source_target_pairs={{0,4},{1,5},{2,6},{3,7},{4,0},{5,1},{6,2},{7,3},{8,12},{9,13},{10,... | collective-permute-start | bytes 110600 | tf_op jit(solution)/shard_map/ppermute | solution.py:488
  315.6 0.6 copy-start.12

commit v3 on v2

--- a/solution.py
+++ b/solution.py
@@ -61,12 +61,11 @@
     return first, second, third
 
 
-def total(flow_ref, which):
-    flow = jnp.sum(flow_ref[...], axis=0, keepdims=True)
+def total(flow, which):
     return flow[:, which : which + 1] + flow[:, which + 2 : which + 3] + flow[:, which + 4 : which + 5]
 
 
-def updated_speed(fields_total, speed, halo_ref, stress_refs, flow_ref, fluid):
+def updated_speed(fields_total, speed, halo_ref, stress_refs, fluid):
     row = row_index(ROWS)
     scale = modulus / fields_total
 
@@ -76,7 +75,8 @@
     main = [stress(c, slice(0, ROWS)) for c in range(3)]
     before = [stress(c, slice(TOP_ROW, TOP_ROW + 1)) for c in range(3)]
     after = [stress(c, slice(BOTTOM_ROW, BOTTOM_ROW + 1)) for c in range(3)]
-    mean_flow = total(flow_ref, 0) / total(flow_ref, 1)
+    flow = sum(ref[0, ROWS : ROWS + 1, :] for ref in stress_refs)
+    mean_flow = total(flow, 0) / total(flow, 1)
 
     def up(v, edge):
         return jnp.where(row == 0, edge, above(v))
@@ -153,7 +153,7 @@
 
     relax_ref, odd_ref, speed_ref, solid_ref, upwind_ref, fields_ref, wiener_ref = take(7)
     if not first:
-        halo_ref, stress_ref, other_ref, flow_ref = take(4)
+        halo_ref, stress_ref, other_ref = take(3)
     top_ref, bottom_ref, send1_ref, send2_ref, sums_ref = take(5)
     if not first:
         (new_speed_ref,) = take(1)
@@ -162,7 +162,7 @@
     fluid = (1 - solid_ref[...]).astype(jnp.float32)
     sx, sy = speed_ref[0], speed_ref[1]
     if not first:
-        sx, sy = updated_speed(fields_total, (sx, sy), halo_ref, (stress_ref, other_ref), flow_ref, fluid)
+        sx, sy = updated_speed(fields_total, (sx, sy), halo_ref, (stress_ref, other_ref), fluid)
         new_speed_ref[0] = sx
         new_speed_ref[1] = sy
     flow = jnp.sum(jnp.sum(fluid * sx, axis=0, keepdims=True), axis=1, keepdims=True)
@@ -380,10 +380,10 @@
         stress_ref[c, ROWS : ROWS + 8, :] = edge
 
 
-def last_kernel(fields_total, speed_ref, solid_ref, halo_ref, stress_ref, other_ref, flow_ref, out_ref):
+def last_kernel(fields_total, speed_ref, solid_ref, halo_ref, stress_ref, other_ref, out_ref):
     fluid = (1 - solid_ref[...]).astype(jnp.float32)
     speed = (speed_ref[0], speed_ref[1])
-    sx, sy = updated_speed(fields_total, speed, halo_ref, (stress_ref, other_ref), flow_ref, fluid)
+    sx, sy = updated_speed(fields_total, speed, halo_ref, (stress_ref, other_ref), fluid)
     out_ref[0] = sx
     out_ref[1] = sy
 
@@ -473,14 +473,15 @@
     )(relax, side, speed, upwind, own, top, bottom, recv, *before)
 
 
-def last_speed(fields_total, speed, solid, halo, stress, other, flow):
+def last_speed(fields_total, speed, solid, halo, stress, other):
     return pl.pallas_call(
         functools.partial(last_kernel, fields_total),
         out_shape=shaped(speed.shape),
-        in_specs=[vmem()] * 6,
+        in_specs=[vmem()] * 5,
         out_specs=vmem(),
+        compiler_params=params(),
         name="last_speed",
-    )(speed, solid, halo, stress, other, flow)
+    )(speed, solid, halo, stress, other)
 
 
 def swapped(value, axis, bit):
@@ -498,8 +499,8 @@
 
 def flow_sums(sums, recv1, recv2):
     value = sums + recv1[recv1.shape[0] - 1 :].astype(jnp.float32)
+    value = value + swapped(value, "slab", 4)
     value = value + swapped(value, "slab", 2)
-    value = value + swapped(value, "slab", 4)
     value, recv2 = lax.optimization_barrier((value, recv2))
     slabs, parts = lax.axis_size("slab"), lax.axis_size("field")
     assert slabs == 8 * parts
@@ -520,20 +521,12 @@
         )
         recv1 = lax.ppermute(send1, "slab", near_pairs)
         recv2 = lax.ppermute(send2, "slab", far_pairs)
-        if step == 0:
-            flow = lax.all_gather(sums, "slab", axis=0, tiled=True)
-            recv1, flow = lax.optimization_barrier((recv1, flow))
-        else:
-            flow, recv2 = flow_sums(sums, recv1, recv2)
+        flow, recv2 = flow_sums(sums, recv1, recv2)
         own = own_steps(step, relax_time, speed, upwind, fields, wiener)
         fields, stress, halo = join(relax_time, odd, speed, upwind, own, top, bottom, recv1)
         fields, stress, halo = join(relax_time, 1 - odd, speed, upwind, fields, top, bottom, recv2, (stress, halo))
-        if step > 0:
-            stress = lax.dynamic_update_slice(stress, flow[None], (0, ROWS, 0))
-        stress, other = field_sum(stress)
-        if step > 0:
-            flow = stress[0, ROWS : ROWS + 1] + other[0, ROWS : ROWS + 1]
-        extra = (halo, stress, other, flow)
+        stress = lax.dynamic_update_slice(stress, flow[None], (0, ROWS, 0))
+        extra = (halo,) + field_sum(stress)
     speed = last_speed(fields_total, speed, solid_mask, *extra)
     return (fields, speed)
 

time: 319 us -> 121 us (0.38)
  blocking collectives: 186 us -> 0 us
  starting transfers between devices: 88.9 us -> 77.4 us
    all_gather x1 -> x0, blocking collectives: 186 us -> none  [per_device(): flow = lax.all_gather(sums, 'slab', axis=0, tiled=True)]
    ppermute x8 -> x10, starting transfers between devices: 63.1 us -> 45.9 us  [swapped(): return lax.ppermute(value, axis, [(i, i ^ bit) for i in range(count)])]
    ppermute x1 -> x2, starting transfers between devices: 1.91 us -> 5.83 us  [flow_sums(): return (lax.ppermute(value, ('slab', 'field'), pairs), recv2)]
    ppermute x8 -> x10, waiting for transfers between devices: 11.8 us -> 13.9 us  [swapped(): return lax.ppermute(value, axis, [(i, i ^ bit) for i in range(count)])]
  transfers between devices with their start and end apart: 13 -> 16, of which waited for: 8 -> 10; matrix products, arithmetic and copies ran while one was open for 0% -> 0% of each run, Pallas kernels for 4% -> 13%
where the time goes in v3:
time: 121 us; the launch traced here: 120 us
  starting transfers between devices  77.4 us (64%)
  Pallas kernels  22 us (18%)
  waiting for transfers between devices  13.9 us (11%)
  local copies, waits for them, and re-layouts  5.67 us (5%)
    ppermute x10, starting transfers between devices, swapped(): return lax.ppermute(value, axis, [(i, i ^ bit) for i in range(count)])  45.9 us
    ppermute x2, starting transfers between devices, per_device(): recv2 = lax.ppermute(send2, 'slab', far_pairs)  19.8 us
    ppermute x10, waiting for transfers between devices, swapped(): return lax.ppermute(value, axis, [(i, i ^ bit) for i in range(count)])  13.9 us
    pallas_call x4, Pallas kernels, join(): pl.pallas_call(functools.partial(join_kernel, nf, not before), out_shape=...  9.45 us
    pallas_call x2, Pallas kernels, own_steps(): pl.pallas_call(functools.partial(own_kernel, fields.shape[1]), grid=(1,),...  6.29 us
    ppermute x2, starting transfers between devices, per_device(): recv1 = lax.ppermute(send1, 'slab', near_pairs)  5.87 us
    ppermute x2, starting transfers between devices, flow_sums(): return (lax.ppermute(value, ('slab', 'field'), pairs), recv2)  5.83 us
    unnamed x22, local copies, waits for them, and re-layouts  5.61 us
  transfers between devices with their start and end apart: 16, of which 10 were waited for; matrix products, arithmetic and copies ran while one was open for 0% of the time, Pallas kernels for 13%

profile of v3, /device:TPU:1, one launch (start us, length us, event | category | flops | bytes accessed | tf_op | source)
XLA Modules:
  0.0 119.9 jit_solution(2328800711681997867)
XLA Ops:
  0.7 1.7 %copy-done = bf16[6,3,32,16,128]{4,3,2,1,0:T(8,128)(2,1)S(1)} copy-done((bf16[6,3,32,16,128]{4,3,2,1,0:T(8,128)(2,1)S(1)}, bf16[6,3,32,16,128]{4,3,2,1,0:T(8,128)(2,1)}, u32[]{:S(2)}) %copy-start) | copy-done | bytes 2359320
  6.2 2.6 %edge_steps.2 = (f32[11,32,128]{2,1,0:T(8,128)S(1)}, f32[11,32,128]{2,1,0:T(8,128)S(1)}, bf16[528,128]{1,0:T(8,128)(2,1)S(1)}, bf16[528,128]{1,0:T(8,128)(2,1)S(1)}, f32[1,128]{1,0:T(1,128)S(1)}) custom-call(f32[32]{0:T(128)S(1)} %copy-done.9, s32[1]{0:T(128)} %bitcast.refs_1_, f32[2,16,128]{2,1,0:T(8,128)S(1)} %copy-done.5, s32[16,128]{1,0:T(8,128)S(1)} %copy-done.7, ...), custom_call_target="tpu_custom_call" | custom-call | tf_op jit(solution)/shard_map/edge_steps/pallas_call | solution.py:433
  8.9 3.9 %collective-permute-start = (bf16[528,128]{1,0:T(8,128)(2,1)S(1)}, bf16[528,128]{1,0:T(8,128)(2,1)S(1)}, u32[]{:S(2)}, u32[]{:S(2)}) collective-permute-start(bf16[528,128]{1,0:T(8,128)(2,1)S(1)} %get-tuple-element.31), channel_id=1, source_target_pairs={{0,8},{8,0},{16,24},{24,16},{32,40},{40,32},{48,56},{56,48},{64,72... | collective-permute-start | bytes 405512 | tf_op jit(solution)/shard_map/ppermute | solution.py:522
  12.8 15.1 %collective-permute-start.3 = (bf16[528,128]{1,0:T(8,128)(2,1)S(1)}, bf16[528,128]{1,0:T(8,128)(2,1)S(1)}, u32[]{:S(2)}, u32[]{:S(2)}) collective-permute-start(bf16[528,128]{1,0:T(8,128)(2,1)S(1)} %get-tuple-element.34), channel_id=1, source_target_pairs={{0,504},{8,16},{16,8},{24,32},{32,24},{40,48},{48,40},{56,64},{64,... | collective-permute-start | bytes 405512 | tf_op jit(solution)/shard_map/ppermute | solution.py:523
  27.9 1.9 %collective-permute-start.1 = (f32[1,128]{1,0:T(1,128)S(1)}, f32[1,128]{1,0:T(1,128)S(1)}, u32[]{:S(2)}, u32[]{:S(2)}) collective-permute-start(f32[1,128]{1,0:T(1,128)S(1)} %fusion.1), channel_id=1, source_target_pairs={{0,32},{8,40},{16,48},{24,56},{32,0},{40,8},{48,16},{56,24},{64,96... | collective-permute-start | bytes 1544 | tf_op jit(solution)/shard_map/ppermute | solution.py:489
  29.9 3.1 %own_steps.2.refs_4_ = f32[3,32,16,128]{3,2,1,0:T(8,128)S(1)} custom-call(f32[32]{0:T(128)S(1)} %copy-done.9, f32[2,16,128]{2,1,0:T(8,128)S(1)} %copy-done.5, s32[2,16,128]{2,1,0:T(8,128)S(1)} %copy-done.3, f32[3,32,16,128]{3,2,1,0:T(8,128)S(1)} %copy-done.2, bf16[6,3,32,16,128]{4,3,2,1,0:T(8,128)(2,1)S(1)} %copy-done), custom_call_target="tpu_custom_call" | custom-call | flops 11796480 | bytes 2359296 | tf_op jit(solution)/shard_map/own_steps/pallas_call | solution.py:450
  33.1 3.1 %collective-permute-done.1 = f32[1,128]{1,0:T(1,128)S(1)} collective-permute-done((f32[1,128]{1,0:T(1,128)S(1)}, f32[1,128]{1,0:T(1,128)S(1)}, u32[]{:S(2)}, u32[]{:S(2)}) %collective-permute-start.1) | collective-permute-done | bytes 544 | tf_op jit(solution)/shard_map/ppermute | solution.py:489
  36.2 1.9 %collective-permute-start.2 = (f32[1,128]{1,0:T(1,128)S(1)}, f32[1,128]{1,0:T(1,128)S(1)}, u32[]{:S(2)}, u32[]{:S(2)}) collective-permute-start(f32[1,128]{1,0:T(1,128)S(1)} %add.36), channel_id=1, source_target_pairs={{0,16},{8,24},{16,0},{24,8},{32,48},{40,56},{48,32},{56,40},{64,80... | collective-permute-start | bytes 1544 | tf_op jit(solution)/shard_map/ppermute | solution.py:489
  38.1 2.2 %join.4 = (f32[3,32,16,128]{3,2,1,0:T(8,128)S(1)}, f32[3,24,128]{2,1,0:T(8,128)S(1)}, f32[8,128]{1,0:T(8,128)S(1)}) custom-call(f32[32]{0:T(128)S(1)} %copy-done.9, s32[1]{0:T(128)} %bitcast.refs_1_, f32[2,16,128]{2,1,0:T(8,128)S(1)} %copy-done.5, s32[2,16,128]{2,1,0:T(8,128)S(1)} %copy-done.3, f32[3,32,16,128]{3,2,1,0:T(8,128)S(1)} %own_steps.2.refs_4_, ...), custom_call_target="tpu_custom_call" | custom-call | flops 3932160 | bytes 1572864 | tf_op jit(solution)/shard_map/join/pallas_call | solution.py:464
  40.3 1.7 %collective-permute-done.2 = f32[1,128]{1,0:T(1,128)S(1)} collective-permute-done((f32[1,128]{1,0:T(1,128)S(1)}, f32[1,128]{1,0:T(1,128)S(1)}, u32[]{:S(2)}, u32[]{:S(2)}) %collective-permute-start.2) | collective-permute-done | bytes 544 | tf_op jit(solution)/shard_map/ppermute | solution.py:489
  42.0 3.0 %collective-permute-start.4 = (f32[1,128]{1,0:T(1,128)S(1)}, f32[1,128]{1,0:T(1,128)S(1)}, u32[]{:S(2)}, u32[]{:S(2)}) collective-permute-start(f32[1,128]{1,0:T(1,128)S(1)} %add.37), channel_id=1, source_target_pairs={{0,0},{65,1},{130,2},{195,3},{260,4},{325,5},{390,6},{455,7},{8,8}... | collective-permute-start | bytes 1544 | tf_op jit(solution)/shard_map/ppermute | solution.py:508
  44.9 2.1 %join.5 = (f32[3,32,16,128]{3,2,1,0:T(8,128)S(1)}, f32[3,24,128]{2,1,0:T(8,128)S(1)}, f32[8,128]{1,0:T(8,128)S(1)}) custom-call(f32[32]{0:T(128)S(1)} %copy-done.9, s32[1]{0:T(128)S(6)} %sub.4.refs_1_, f32[2,16,128]{2,1,0:T(8,128)S(1)} %copy-done.5, s32[2,16,128]{2,1,0:T(8,128)S(1)} %copy-done.3, f32[3,32,16,128]{3,2,1,0:T(8,128)S(1)} %get-tuple-element.32.refs_4_, ...), custom_call_target="tpu_custom_call" | custom-call | flops 3932160 | bytes 1572864 | tf_op jit(solution)/shard_map/join/pallas_call | solution.py:464
  47.1 3.1 %collective-permute-start.5 = (f32[3,24,128]{2,1,0:T(8,128)S(1)}, f32[3,24,128]{2,1,0:T(8,128)S(1)}, u32[]{:S(2)}, u32[]{:S(2)}) collective-permute-start(f32[3,24,128]{2,1,0:T(8,128)S(1)} %dynamic_update_slice.6), channel_id=1, source_target_pairs={{0,1},{1,0},{2,3},{3,2},{4,5},{5,4},{6,7},{7,6},{8,9},{9,8},{10,11... | collective-permute-start | bytes 110600 | tf_op jit(solution)/shard_map/ppermute | solution.py:489
  51.1 6.6 %collective-permute-start.6 = (f32[3,24,128]{2,1,0:T(8,128)S(1)}, f32[3,24,128]{2,1,0:T(8,128)S(1)}, u32[]{:S(2)}, u32[]{:S(2)}) collective-permute-start(f32[3,24,128]{2,1,0:T(8,128)S(1)} %add.38), channel_id=1, source_target_pairs={{0,2},{1,3},{2,0},{3,1},{4,6},{5,7},{6,4},{7,5},{8,10},{9,11},{10,... | collective-permute-start | bytes 110600 | tf_op jit(solution)/shard_map/ppermute | solution.py:489
  57.6 1.3 %collective-permute-done.6 = f32[3,24,128]{2,1,0:T(8,128)S(1)} collective-permute-done((f32[3,24,128]{2,1,0:T(8,128)S(1)}, f32[3,24,128]{2,1,0:T(8,128)S(1)}, u32[]{:S(2)}, u32[]{:S(2)}) %collective-permute-start.6) | collective-permute-done | bytes 36896 | tf_op jit(solution)/shard_map/ppermute | solution.py:489
  59.0 7.3 %collective-permute-start.7 = (f32[3,24,128]{2,1,0:T(8,128)S(1)}, f32[3,24,128]{2,1,0:T(8,128)S(1)}, u32[]{:S(2)}, u32[]{:S(2)}) collective-permute-start(f32[3,24,128]{2,1,0:T(8,128)S(1)} %add.39.refs_8_), channel_id=1, source_target_pairs={{0,4},{1,5},{2,6},{3,7},{4,0},{5,1},{6,2},{7,3},{8,12},{9,13},{10,... | collective-permute-start | bytes 110600 | tf_op jit(solution)/shard_map/ppermute | solution.py:489
  66.3 1.5 %collective-permute-done.7.refs_9_ = f32[3,24,128]{2,1,0:T(8,128)S(1)} collective-permute-done((f32[3,24,128]{2,1,0:T(8,128)S(1)}, f32[3,24,128]{2,1,0:T(8,128)S(1)}, u32[]{:S(2)}, u32[]{:S(2)}) %collective-permute-start.7) | collective-permute-done | bytes 36896 | tf_op jit(solution)/shard_map/ppermute | solution.py:489
  67.8 2.8 %edge_steps.3 = (f32[11,32,128]{2,1,0:T(8,128)S(1)}, f32[11,32,128]{2,1,0:T(8,128)S(1)}, bf16[528,128]{1,0:T(8,128)(2,1)S(1)}, bf16[528,128]{1,0:T(8,128)(2,1)S(...) custom-call(f32[32]{0:T(128)S(1)} %copy-done.10, s32[1]{0:T(128)} %bitcast.refs_1_, f32[2,16,128]{2,1,0:T(8,128)S(1)} %copy-done.6, ...), custom_call_target="tpu_custom_call" | custom-call | tf_op jit(solution)/shard_map/edge_steps/pallas_call | solution.py:433
  70.6 1.9 %collective-permute-start.8 = (bf16[528,128]{1,0:T(8,128)(2,1)S(1)}, bf16[528,128]{1,0:T(8,128)(2,1)S(1)}, u32[]{:S(2)}, u32[]{:S(2)}) collective-permute-start(bf16[528,128]{1,0:T(8,128)(2,1)S(1)} %get-tuple-element.45), channel_id=1, source_target_pairs={{0,8},{8,0},{16,24},{24,16},{32,40},{40,32},{48,56},{56,48},{64,72... | collective-permute-start | bytes 405512 | tf_op jit(solution)/shard_map/ppermute | solution.py:522
  72.5 4.7 %collective-permute-start.11 = (bf16[528,128]{1,0:T(8,128)(2,1)S(1)}, bf16[528,128]{1,0:T(8,128)(2,1)S(1)}, u32[]{:S(2)}, u32[]{:S(2)}) collective-permute-start(bf16[528,128]{1,0:T(8,128)(2,1)S(1)} %get-tuple-element.48), channel_id=1, source_target_pairs={{0,504},{8,16},{16,8},{24,32},{32,24},{40,48},{48,40},{56,64},{64,... | collective-permute-start | bytes 405512 | tf_op jit(solution)/shard_map/ppermute | solution.py:523
  77.3 4.9 %collective-permute-start.9 = (f32[1,128]{1,0:T(1,128)S(1)}, f32[1,128]{1,0:T(1,128)S(1)}, u32[]{:S(2)}, u32[]{:S(2)}) collective-permute-start(f32[1,128]{1,0:T(1,128)S(1)} %fusion), channel_id=1, source_target_pairs={{0,32},{8,40},{16,48},{24,56},{32,0},{40,8},{48,16},{56,24},{64,96... | collective-permute-start | bytes 1544 | tf_op jit(solution)/shard_map/ppermute | solution.py:489
  82.2 3.1 %own_steps.3.refs_4_ = f32[3,32,16,128]{3,2,1,0:T(8,128)S(1)} custom-call(f32[32]{0:T(128)S(1)} %copy-done.10, f32[2,16,128]{2,1,0:T(8,128)S(1)} %get-tuple-element.42.speed_ref.refs_2_, s32[2,16,128]{2,1,0:T(8,128)S(1)} %copy-done.4, f32[3,32,16,128]{3,2,1,0:T(8,128)S(1)} %get-tuple-element.38.refs_5_.fields_ref, bf16[6,3,32,16,128]{4,3,2,1,0:T(8,128)(2,1)S(1)} %copy-done.1), custom_call_target="tpu_custom_call" | custom-call | flops 11796480 | bytes 2359296 | tf_op jit(solution)/shard_map/own_steps/pallas_call | solution.py:450
  85.6 2.1 %collective-permute-start.10 = (f32[1,128]{1,0:T(1,128)S(1)}, f32[1,128]{1,0:T(1,128)S(1)}, u32[]{:S(2)}, u32[]{:S(2)}) collective-permute-start(f32[1,128]{1,0:T(1,128)S(1)} %add.41), channel_id=1, source_target_pairs={{0,16},{8,24},{16,0},{24,8},{32,48},{40,56},{48,32},{56,40},{64,80... | collective-permute-start | bytes 1544 | tf_op jit(solution)/shard_map/ppermute | solution.py:489
  87.8 2.2 %join.6 = (f32[3,32,16,128]{3,2,1,0:T(8,128)S(1)}, f32[3,24,128]{2,1,0:T(8,128)S(1)}, f32[8,128]{1,0:T(8,128)S(1)}) custom-call(f32[32]{0:T(128)S(1)} %copy-done.10, s32[1]{0:T(128)} %bitcast.refs_1_, f32[2,16,128]{2,1,0:T(8,128)S(1)} %get-tuple-element.42.speed_ref.refs_2_, s32[2,16,128]{2,1,0:T(8,128)S(1)} %copy-done.4, ...), custom_call_target="tpu_custom_call" | custom-call | flops 3932160 | bytes 1572864 | tf_op jit(solution)/shard_map/join/pallas_call | solution.py:464
  90.0 1.5 %collective-permute-done.10 = f32[1,128]{1,0:T(1,128)S(1)} collective-permute-done((f32[1,128]{1,0:T(1,128)S(1)}, f32[1,128]{1,0:T(1,128)S(1)}, u32[]{:S(2)}, u32[]{:S(2)}) %collective-permute-start.10) | collective-permute-done | bytes 544 | tf_op jit(solution)/shard_map/ppermute | solution.py:489
  91.4 2.9 %collective-permute-start.12 = (f32[1,128]{1,0:T(1,128)S(1)}, f32[1,128]{1,0:T(1,128)S(1)}, u32[]{:S(2)}, u32[]{:S(2)}) collective-permute-start(f32[1,128]{1,0:T(1,128)S(1)} %add.42), channel_id=1, source_target_pairs={{0,0},{65,1},{130,2},{195,3},{260,4},{325,5},{390,6},{455,7},{8,8}... | collective-permute-start | bytes 1544 | tf_op jit(solution)/shard_map/ppermute | solution.py:508
  94.3 3.0 %join.7 = (f32[3,32,16,128]{3,2,1,0:T(8,128)}, f32[3,24,128]{2,1,0:T(8,128)S(1)}, f32[8,128]{1,0:T(8,128)S(1)}) custom-call(f32[32]{0:T(128)S(1)} %copy-done.10, s32[1]{0:T(128)S(6)} %sub.4.refs_1_, f32[2,16,128]{2,1,0:T(8,128)S(1)} %get-tuple-element.42.speed_ref.refs_2_, s32[2,16,128]{2,1,0:T(8,128)S(1)} %copy-done.4, ...), custom_call_target="tpu_custom_call" | custom-call | flops 3932160 | bytes 1572864 | tf_op jit(solution)/shard_map/join/pallas_call | solution.py:464
  97.3 4.6 %collective-permute-start.13 = (f32[3,24,128]{2,1,0:T(8,128)S(1)}, f32[3,24,128]{2,1,0:T(8,128)S(1)}, u32[]{:S(2)}, u32[]{:S(2)}) collective-permute-start(f32[3,24,128]{2,1,0:T(8,128)S(1)} %dynamic_update_slice.7), channel_id=1, source_target_pairs={{0,1},{1,0},{2,3},{3,2},{4,5},{5,4},{6,7},{7,6},{8,9},{9,8},{10,11... | collective-permute-start | bytes 110600 | tf_op jit(solution)/shard_map/ppermute | solution.py:489
  102.8 5.0 %collective-permute-start.14 = (f32[3,24,128]{2,1,0:T(8,128)S(1)}, f32[3,24,128]{2,1,0:T(8,128)S(1)}, u32[]{:S(2)}, u32[]{:S(2)}) collective-permute-start(f32[3,24,128]{2,1,0:T(8,128)S(1)} %add.43), channel_id=1, source_target_pairs={{0,2},{1,3},{2,0},{3,1},{4,6},{5,7},{6,4},{7,5},{8,10},{9,11},{10,... | collective-permute-start | bytes 110600 | tf_op jit(solution)/shard_map/ppermute | solution.py:489
  107.9 1.3 %collective-permute-done.14 = f32[3,24,128]{2,1,0:T(8,128)S(1)} collective-permute-done((f32[3,24,128]{2,1,0:T(8,128)S(1)}, f32[3,24,128]{2,1,0:T(8,128)S(1)}, u32[]{:S(2)}, u32[]{:S(2)}) %collective-permute-start.14) | collective-permute-done | bytes 36896 | tf_op jit(solution)/shard_map/ppermute | solution.py:489
  109.2 8.5 %collective-permute-start.15 = (f32[3,24,128]{2,1,0:T(8,128)S(1)}, f32[3,24,128]{2,1,0:T(8,128)S(1)}, u32[]{:S(2)}, u32[]{:S(2)}) collective-permute-start(f32[3,24,128]{2,1,0:T(8,128)S(1)} %add.44.stress_ref), channel_id=1, source_target_pairs={{0,4},{1,5},{2,6},{3,7},{4,0},{5,1},{6,2},{7,3},{8,12},{9,13},{10,... | collective-permute-start | bytes 110600 | tf_op jit(solution)/shard_map/ppermute | solution.py:489
  117.7 1.5 %collective-permute-done.15.other_ref = f32[3,24,128]{2,1,0:T(8,128)S(1)} collective-permute-done((f32[3,24,128]{2,1,0:T(8,128)S(1)}, f32[3,24,128]{2,1,0:T(8,128)S(1)}, u32[]{:S(2)}, u32[]{:S(2)}) %collective-permute-start.15) | collective-permute-done | bytes 36896 | tf_op jit(solution)/shard_map/ppermute | solution.py:489
  (43 shorter events, 6.9 us)
Async XLA Ops:
  0.6 1.7 %copy-start = (bf16[6,3,32,16,128]{4,3,2,1,0:T(8,128)(2,1)S(1)}, bf16[6,3,32,16,128]{4,3,2,1,0:T(8,128)(2,1)}, u32[]{:S(2)}) copy-start(bf16[6,3,32,16,128]{4,3,2,1,0:T(8,128)(2,1)} %wiener_ref.3) | copy-start | bytes 7077892
  2.3 1.1 copy-start.2
  3.4 0.7 copy-start.3
  4.2 0.7 copy-start.5
  4.9 0.7 copy-start.7
  5.6 0.7 copy-start.9
  8.9 19.0 %collective-permute-start = (bf16[528,128]{1,0:T(8,128)(2,1)S(1)}, bf16[528,128]{1,0:T(8,128)(2,1)S(1)}, u32[]{:S(2)}, u32[]{:S(2)}) collective-permute-start(bf16[528,128]{1,0:T(8,128)(2,1)S(1)} %get-tuple-element.31), channel_id=1, source_target_pairs={{0,8},{8,0},{16,24},{24,16},{32,40},{40,32},{48,56},{56,48},{64,72... | collective-permute-start | bytes 405512 | tf_op jit(solution)/shard_map/ppermute | solution.py:522
  12.8 29.1 %collective-permute-start.3 = (bf16[528,128]{1,0:T(8,128)(2,1)S(1)}, bf16[528,128]{1,0:T(8,128)(2,1)S(1)}, u32[]{:S(2)}, u32[]{:S(2)}) collective-permute-start(bf16[528,128]{1,0:T(8,128)(2,1)S(1)} %get-tuple-element.34), channel_id=1, source_target_pairs={{0,504},{8,16},{16,8},{24,32},{32,24},{40,48},{48,40},{56,64},{64,... | collective-permute-start | bytes 405512 | tf_op jit(solution)/shard_map/ppermute | solution.py:523
  27.9 8.2 %collective-permute-start.1 = (f32[1,128]{1,0:T(1,128)S(1)}, f32[1,128]{1,0:T(1,128)S(1)}, u32[]{:S(2)}, u32[]{:S(2)}) collective-permute-start(f32[1,128]{1,0:T(1,128)S(1)} %fusion.1), channel_id=1, source_target_pairs={{0,32},{8,40},{16,48},{24,56},{32,0},{40,8},{48,16},{56,24},{64,96... | collective-permute-start | bytes 1544 | tf_op jit(solution)/shard_map/ppermute | solution.py:489
  33.0 34.7 %copy-start.1 = (bf16[6,3,32,16,128]{4,3,2,1,0:T(8,128)(2,1)S(1)}, bf16[6,3,32,16,128]{4,3,2,1,0:T(8,128)(2,1)}, u32[]{:S(2)}) copy-start(bf16[6,3,32,16,128]{4,3,2,1,0:T(8,128)(2,1)} %wiener_ref.3) | copy-start | bytes 7077892
  33.0 34.7 %copy-start.4 = (s32[2,16,128]{2,1,0:T(8,128)S(1)}, s32[2,16,128]{2,1,0:T(8,128)}, u32[]{:S(2)}) copy-start(s32[2,16,128]{2,1,0:T(8,128)} %refs_3_.11) | copy-start | bytes 49156
  33.0 34.7 %copy-start.6 = (f32[2,16,128]{2,1,0:T(8,128)S(1)}, f32[2,16,128]{2,1,0:T(8,128)}, u32[]{:S(2)}) copy-start(f32[2,16,128]{2,1,0:T(8,128)} %refs_2_.7) | copy-start | bytes 49156
  33.1 34.7 %copy-start.8 = (s32[16,128]{1,0:T(8,128)S(1)}, s32[16,128]{1,0:T(8,128)}, u32[]{:S(2)}) copy-start(s32[16,128]{1,0:T(8,128)} %solid_ref.1) | copy-start | bytes 24580
  33.1 34.7 %copy-start.10 = (f32[32]{0:T(128)S(1)}, f32[32]{0:T(128)}, u32[]{:S(2)}) copy-start(f32[32]{0:T(128)} %refs_0_.11) | copy-start | bytes 388
  36.2 5.8 %collective-permute-start.2 = (f32[1,128]{1,0:T(1,128)S(1)}, f32[1,128]{1,0:T(1,128)S(1)}, u32[]{:S(2)}, u32[]{:S(2)}) collective-permute-start(f32[1,128]{1,0:T(1,128)S(1)} %add.36), channel_id=1, source_target_pairs={{0,16},{8,24},{16,0},{24,8},{32,48},{40,56},{48,32},{56,40},{64,80... | collective-permute-start | bytes 1544 | tf_op jit(solution)/shard_map/ppermute | solution.py:489
  42.0 5.1 %collective-permute-start.4 = (f32[1,128]{1,0:T(1,128)S(1)}, f32[1,128]{1,0:T(1,128)S(1)}, u32[]{:S(2)}, u32[]{:S(2)}) collective-permute-start(f32[1,128]{1,0:T(1,128)S(1)} %add.37), channel_id=1, source_target_pairs={{0,0},{65,1},{130,2},{195,3},{260,4},{325,5},{390,6},{455,7},{8,8}... | collective-permute-start | bytes 1544 | tf_op jit(solution)/shard_map/ppermute | solution.py:508
  47.1 3.9 %collective-permute-start.5 = (f32[3,24,128]{2,1,0:T(8,128)S(1)}, f32[3,24,128]{2,1,0:T(8,128)S(1)}, u32[]{:S(2)}, u32[]{:S(2)}) collective-permute-start(f32[3,24,128]{2,1,0:T(8,128)S(1)} %dynamic_update_slice.6), channel_id=1, source_target_pairs={{0,1},{1,0},{2,3},{3,2},{4,5},{5,4},{6,7},{7,6},{8,9},{9,8},{10,11... | collective-permute-start | bytes 110600 | tf_op jit(solution)/shard_map/ppermute | solution.py:489
  51.1 7.9 %collective-permute-start.6 = (f32[3,24,128]{2,1,0:T(8,128)S(1)}, f32[3,24,128]{2,1,0:T(8,128)S(1)}, u32[]{:S(2)}, u32[]{:S(2)}) collective-permute-start(f32[3,24,128]{2,1,0:T(8,128)S(1)} %add.38), channel_id=1, source_target_pairs={{0,2},{1,3},{2,0},{3,1},{4,6},{5,7},{6,4},{7,5},{8,10},{9,11},{10,... | collective-permute-start | bytes 110600 | tf_op jit(solution)/shard_map/ppermute | solution.py:489
  59.0 8.7 %collective-permute-start.7 = (f32[3,24,128]{2,1,0:T(8,128)S(1)}, f32[3,24,128]{2,1,0:T(8,128)S(1)}, u32[]{:S(2)}, u32[]{:S(2)}) collective-permute-start(f32[3,24,128]{2,1,0:T(8,128)S(1)} %add.39.refs_8_), channel_id=1, source_target_pairs={{0,4},{1,5},{2,6},{3,7},{4,0},{5,1},{6,2},{7,3},{8,12},{9,13},{10,... | collective-permute-start | bytes 110600 | tf_op jit(solution)/shard_map/ppermute | solution.py:489
  70.6 6.7 %collective-permute-start.8 = (bf16[528,128]{1,0:T(8,128)(2,1)S(1)}, bf16[528,128]{1,0:T(8,128)(2,1)S(1)}, u32[]{:S(2)}, u32[]{:S(2)}) collective-permute-start(bf16[528,128]{1,0:T(8,128)(2,1)S(1)} %get-tuple-element.45), channel_id=1, source_target_pairs={{0,8},{8,0},{16,24},{24,16},{32,40},{40,32},{48,56},{56,48},{64,72... | collective-permute-start | bytes 405512 | tf_op jit(solution)/shard_map/ppermute | solution.py:522
  72.5 18.9 %collective-permute-start.11 = (bf16[528,128]{1,0:T(8,128)(2,1)S(1)}, bf16[528,128]{1,0:T(8,128)(2,1)S(1)}, u32[]{:S(2)}, u32[]{:S(2)}) collective-permute-start(bf16[528,128]{1,0:T(8,128)(2,1)S(1)} %get-tuple-element.48), channel_id=1, source_target_pairs={{0,504},{8,16},{16,8},{24,32},{32,24},{40,48},{48,40},{56,64},{64,... | collective-permute-start | bytes 405512 | tf_op jit(solution)/shard_map/ppermute | solution.py:523
  77.3 8.4 %collective-permute-start.9 = (f32[1,128]{1,0:T(1,128)S(1)}, f32[1,128]{1,0:T(1,128)S(1)}, u32[]{:S(2)}, u32[]{:S(2)}) collective-permute-start(f32[1,128]{1,0:T(1,128)S(1)} %fusion), channel_id=1, source_target_pairs={{0,32},{8,40},{16,48},{24,56},{32,0},{40,8},{48,16},{56,24},{64,96... | collective-permute-start | bytes 1544 | tf_op jit(solution)/shard_map/ppermute | solution.py:489
  85.6 5.8 %collective-permute-start.10 = (f32[1,128]{1,0:T(1,128)S(1)}, f32[1,128]{1,0:T(1,128)S(1)}, u32[]{:S(2)}, u32[]{:S(2)}) collective-permute-start(f32[1,128]{1,0:T(1,128)S(1)} %add.41), channel_id=1, source_target_pairs={{0,16},{8,24},{16,0},{24,8},{32,48},{40,56},{48,32},{56,40},{64,80... | collective-permute-start | bytes 1544 | tf_op jit(solution)/shard_map/ppermute | solution.py:489
  91.4 5.9 %collective-permute-start.12 = (f32[1,128]{1,0:T(1,128)S(1)}, f32[1,128]{1,0:T(1,128)S(1)}, u32[]{:S(2)}, u32[]{:S(2)}) collective-permute-start(f32[1,128]{1,0:T(1,128)S(1)} %add.42), channel_id=1, source_target_pairs={{0,0},{65,1},{130,2},{195,3},{260,4},{325,5},{390,6},{455,7},{8,8}... | collective-permute-start | bytes 1544 | tf_op jit(solution)/shard_map/ppermute | solution.py:508
  97.3 5.5 %collective-permute-start.13 = (f32[3,24,128]{2,1,0:T(8,128)S(1)}, f32[3,24,128]{2,1,0:T(8,128)S(1)}, u32[]{:S(2)}, u32[]{:S(2)}) collective-permute-start(f32[3,24,128]{2,1,0:T(8,128)S(1)} %dynamic_update_slice.7), channel_id=1, source_target_pairs={{0,1},{1,0},{2,3},{3,2},{4,5},{5,4},{6,7},{7,6},{8,9},{9,8},{10,11... | collective-permute-start | bytes 110600 | tf_op jit(solution)/shard_map/ppermute | solution.py:489
  102.8 6.4 %collective-permute-start.14 = (f32[3,24,128]{2,1,0:T(8,128)S(1)}, f32[3,24,128]{2,1,0:T(8,128)S(1)}, u32[]{:S(2)}, u32[]{:S(2)}) collective-permute-start(f32[3,24,128]{2,1,0:T(8,128)S(1)} %add.43), channel_id=1, source_target_pairs={{0,2},{1,3},{2,0},{3,1},{4,6},{5,7},{6,4},{7,5},{8,10},{9,11},{10,... | collective-permute-start | bytes 110600 | tf_op jit(solution)/shard_map/ppermute | solution.py:489
  109.2 9.9 %collective-permute-start.15 = (f32[3,24,128]{2,1,0:T(8,128)S(1)}, f32[3,24,128]{2,1,0:T(8,128)S(1)}, u32[]{:S(2)}, u32[]{:S(2)}) collective-permute-start(f32[3,24,128]{2,1,0:T(8,128)S(1)} %add.44.stress_ref), channel_id=1, source_target_pairs={{0,4},{1,5},{2,6},{3,7},{4,0},{5,1},{6,2},{7,3},{8,12},{9,13},{10,... | collective-permute-start | bytes 110600 | tf_op jit(solution)/shard_map/ppermute | solution.py:489

commit v4 on v3

--- a/solution.py
+++ b/solution.py
@@ -65,17 +65,23 @@
     return flow[:, which : which + 1] + flow[:, which + 2 : which + 3] + flow[:, which + 4 : which + 5]
 
 
+def pairwise(terms):
+    while len(terms) > 1:
+        terms = [terms[i] + terms[i + 1] for i in range(0, len(terms), 2)]
+    return terms[0]
+
+
 def updated_speed(fields_total, speed, halo_ref, stress_refs, fluid):
     row = row_index(ROWS)
     scale = modulus / fields_total
 
     def stress(c, rows):
-        return scale * (stress_refs[0][c, rows, :] + stress_refs[1][c, rows, :]) - (modulus if c != 1 else 0.0)
+        return scale * pairwise([ref[c, rows, :] for ref in stress_refs]) - (modulus if c != 1 else 0.0)
 
     main = [stress(c, slice(0, ROWS)) for c in range(3)]
     before = [stress(c, slice(TOP_ROW, TOP_ROW + 1)) for c in range(3)]
     after = [stress(c, slice(BOTTOM_ROW, BOTTOM_ROW + 1)) for c in range(3)]
-    flow = sum(ref[0, ROWS : ROWS + 1, :] for ref in stress_refs)
+    flow = pairwise([ref[0, ROWS : ROWS + 1, :] for ref in stress_refs])
     mean_flow = total(flow, 0) / total(flow, 1)
 
     def up(v, edge):
@@ -143,7 +149,7 @@
     return new
 
 
-def edge_kernel(nf, fields_total, first, *refs):
+def edge_kernel(nf, fields_total, terms, *refs):
     refs = list(refs)
 
     def take(count):
@@ -152,8 +158,10 @@
         return taken
 
     relax_ref, odd_ref, speed_ref, solid_ref, upwind_ref, fields_ref, wiener_ref = take(7)
+    first = terms == 0
     if not first:
-        halo_ref, stress_ref, other_ref = take(3)
+        (halo_ref,) = take(1)
+        stress_refs = take(terms)
     top_ref, bottom_ref, send1_ref, send2_ref, sums_ref = take(5)
     if not first:
         (new_speed_ref,) = take(1)
@@ -162,7 +170,7 @@
     fluid = (1 - solid_ref[...]).astype(jnp.float32)
     sx, sy = speed_ref[0], speed_ref[1]
     if not first:
-        sx, sy = updated_speed(fields_total, (sx, sy), halo_ref, (stress_ref, other_ref), fluid)
+        sx, sy = updated_speed(fields_total, (sx, sy), halo_ref, stress_refs, fluid)
         new_speed_ref[0] = sx
         new_speed_ref[1] = sy
     flow = jnp.sum(jnp.sum(fluid * sx, axis=0, keepdims=True), axis=1, keepdims=True)
@@ -380,10 +388,11 @@
         stress_ref[c, ROWS : ROWS + 8, :] = edge
 
 
-def last_kernel(fields_total, speed_ref, solid_ref, halo_ref, stress_ref, other_ref, out_ref):
+def last_kernel(fields_total, speed_ref, solid_ref, halo_ref, *refs):
+    stress_refs, out_ref = refs[:-1], refs[-1]
     fluid = (1 - solid_ref[...]).astype(jnp.float32)
     speed = (speed_ref[0], speed_ref[1])
-    sx, sy = updated_speed(fields_total, speed, halo_ref, (stress_ref, other_ref), fluid)
+    sx, sy = updated_speed(fields_total, speed, halo_ref, stress_refs, fluid)
     out_ref[0] = sx
     out_ref[1] = sy
 
@@ -431,7 +440,7 @@
     if not first:
         outs.append(shaped(speed.shape))
     got = pl.pallas_call(
-        functools.partial(edge_kernel, nf, fields_total, first),
+        functools.partial(edge_kernel, nf, fields_total, max(0, len(extra) - 1)),
         grid=(1,),
         out_shape=outs,
         in_specs=[smem(), smem()]
@@ -473,15 +482,15 @@
     )(relax, side, speed, upwind, own, top, bottom, recv, *before)
 
 
-def last_speed(fields_total, speed, solid, halo, stress, other):
+def last_speed(fields_total, speed, solid, halo, *stresses):
     return pl.pallas_call(
         functools.partial(last_kernel, fields_total),
         out_shape=shaped(speed.shape),
-        in_specs=[vmem()] * 5,
+        in_specs=[vmem()] * (3 + len(stresses)),
         out_specs=vmem(),
         compiler_params=params(),
         name="last_speed",
-    )(speed, solid, halo, stress, other)
+    )(speed, solid, halo, *stresses)
 
 
 def swapped(value, axis, bit):
@@ -490,11 +499,8 @@
 
 
 def field_sum(value):
-    bit = 1
-    while 2 * bit < lax.axis_size("field"):
-        value = value + swapped(value, "field", bit)
-        bit *= 2
-    return value, swapped(value, "field", bit)
+    value = value + swapped(value, "field", 1)
+    return (value,) + tuple(swapped(value, "field", bits) for bits in range(2, lax.axis_size("field"), 2))
 
 
 def flow_sums(sums, recv1, recv2):

time: 121 us -> 120 us (level)
    ppermute x10 -> x12, waiting for transfers between devices: 13.9 us -> 13.2 us  [swapped(): return lax.ppermute(value, axis, [(i, i ^ bit) for i in range(count)])]
    ppermute x10 -> x12, starting transfers between devices: 45.9 us -> 45.7 us  [swapped(): return lax.ppermute(value, axis, [(i, i ^ bit) for i in range(count)])]
  transfers between devices with their start and end apart: 16 -> 18, of which waited for: 10 -> 10; matrix products, arithmetic and copies ran while one was open for 0% -> 0% of each run, Pallas kernels for 13% -> 13%
where the time goes in v4:
time: 120 us; the launch traced here: 119 us
  starting transfers between devices  77.3 us (64%)
  Pallas kernels  22 us (18%)
  waiting for transfers between devices  13.3 us (11%)
  local copies, waits for them, and re-layouts  5.67 us (5%)
    ppermute x12, starting transfers between devices, swapped(): return lax.ppermute(value, axis, [(i, i ^ bit) for i in range(count)])  45.7 us
    ppermute x2, starting transfers between devices, per_device(): recv2 = lax.ppermute(send2, 'slab', far_pairs)  19.8 us
    ppermute x12, waiting for transfers between devices, swapped(): return lax.ppermute(value, axis, [(i, i ^ bit) for i in range(count)])  13.2 us
    pallas_call x4, Pallas kernels, join(): pl.pallas_call(functools.partial(join_kernel, nf, not before), out_shape=...  9.45 us
    pallas_call x2, Pallas kernels, own_steps(): pl.pallas_call(functools.partial(own_kernel, fields.shape[1]), grid=(1,),...  6.29 us
    ppermute x2, starting transfers between devices, flow_sums(): return (lax.ppermute(value, ('slab', 'field'), pairs), recv2)  5.92 us
    ppermute x2, starting transfers between devices, per_device(): recv1 = lax.ppermute(send1, 'slab', near_pairs)  5.87 us
    unnamed x22, local copies, waits for them, and re-layouts  5.61 us
  transfers between devices with their start and end apart: 18, of which 10 were waited for; matrix products, arithmetic and copies ran while one was open for 0% of the time, Pallas kernels for 13%

profile of v4, /device:TPU:1, one launch (start us, length us, event | category | flops | bytes accessed | tf_op | source)
XLA Modules:
  0.0 119.2 jit_solution(15820314679937326909)
XLA Ops:
  0.7 1.7 %copy-done = bf16[6,3,32,16,128]{4,3,2,1,0:T(8,128)(2,1)S(1)} copy-done((bf16[6,3,32,16,128]{4,3,2,1,0:T(8,128)(2,1)S(1)}, bf16[6,3,32,16,128]{4,3,2,1,0:T(8,128)(2,1)}, u32[]{:S(2)}) %copy-start) | copy-done | bytes 2359320
  6.2 2.6 %edge_steps.2 = (f32[11,32,128]{2,1,0:T(8,128)S(1)}, f32[11,32,128]{2,1,0:T(8,128)S(1)}, bf16[528,128]{1,0:T(8,128)(2,1)S(1)}, bf16[528,128]{1,0:T(8,128)(2,1)S(1)}, f32[1,128]{1,0:T(1,128)S(1)}) custom-call(f32[32]{0:T(128)S(1)} %copy-done.9, s32[1]{0:T(128)} %bitcast.refs_1_, f32[2,16,128]{2,1,0:T(8,128)S(1)} %copy-done.5, s32[16,128]{1,0:T(8,128)S(1)} %copy-done.7, ...), custom_call_target="tpu_custom_call" | custom-call | tf_op jit(solution)/shard_map/edge_steps/pallas_call | solution.py:442
  8.9 3.9 %collective-permute-start = (bf16[528,128]{1,0:T(8,128)(2,1)S(1)}, bf16[528,128]{1,0:T(8,128)(2,1)S(1)}, u32[]{:S(2)}, u32[]{:S(2)}) collective-permute-start(bf16[528,128]{1,0:T(8,128)(2,1)S(1)} %get-tuple-element.31), channel_id=1, source_target_pairs={{0,8},{8,0},{16,24},{24,16},{32,40},{40,32},{48,56},{56,48},{64,72... | collective-permute-start | bytes 405512 | tf_op jit(solution)/shard_map/ppermute | solution.py:528
  12.8 15.1 %collective-permute-start.3 = (bf16[528,128]{1,0:T(8,128)(2,1)S(1)}, bf16[528,128]{1,0:T(8,128)(2,1)S(1)}, u32[]{:S(2)}, u32[]{:S(2)}) collective-permute-start(bf16[528,128]{1,0:T(8,128)(2,1)S(1)} %get-tuple-element.34), channel_id=1, source_target_pairs={{0,504},{8,16},{16,8},{24,32},{32,24},{40,48},{48,40},{56,64},{64,... | collective-permute-start | bytes 405512 | tf_op jit(solution)/shard_map/ppermute | solution.py:529
  27.9 1.9 %collective-permute-start.1 = (f32[1,128]{1,0:T(1,128)S(1)}, f32[1,128]{1,0:T(1,128)S(1)}, u32[]{:S(2)}, u32[]{:S(2)}) collective-permute-start(f32[1,128]{1,0:T(1,128)S(1)} %fusion.1), channel_id=1, source_target_pairs={{0,32},{8,40},{16,48},{24,56},{32,0},{40,8},{48,16},{56,24},{64,96... | collective-permute-start | bytes 1544 | tf_op jit(solution)/shard_map/ppermute | solution.py:498
  29.9 3.1 %own_steps.2.refs_4_ = f32[3,32,16,128]{3,2,1,0:T(8,128)S(1)} custom-call(f32[32]{0:T(128)S(1)} %copy-done.9, f32[2,16,128]{2,1,0:T(8,128)S(1)} %copy-done.5, s32[2,16,128]{2,1,0:T(8,128)S(1)} %copy-done.3, f32[3,32,16,128]{3,2,1,0:T(8,128)S(1)} %copy-done.2, bf16[6,3,32,16,128]{4,3,2,1,0:T(8,128)(2,1)S(1)} %copy-done), custom_call_target="tpu_custom_call" | custom-call | flops 11796480 | bytes 2359296 | tf_op jit(solution)/shard_map/own_steps/pallas_call | solution.py:459
  33.1 3.1 %collective-permute-done.1 = f32[1,128]{1,0:T(1,128)S(1)} collective-permute-done((f32[1,128]{1,0:T(1,128)S(1)}, f32[1,128]{1,0:T(1,128)S(1)}, u32[]{:S(2)}, u32[]{:S(2)}) %collective-permute-start.1) | collective-permute-done | bytes 544 | tf_op jit(solution)/shard_map/ppermute | solution.py:498
  36.2 1.9 %collective-permute-start.2 = (f32[1,128]{1,0:T(1,128)S(1)}, f32[1,128]{1,0:T(1,128)S(1)}, u32[]{:S(2)}, u32[]{:S(2)}) collective-permute-start(f32[1,128]{1,0:T(1,128)S(1)} %add.30), channel_id=1, source_target_pairs={{0,16},{8,24},{16,0},{24,8},{32,48},{40,56},{48,32},{56,40},{64,80... | collective-permute-start | bytes 1544 | tf_op jit(solution)/shard_map/ppermute | solution.py:498
  38.1 2.2 %join.4 = (f32[3,32,16,128]{3,2,1,0:T(8,128)S(1)}, f32[3,24,128]{2,1,0:T(8,128)S(1)}, f32[8,128]{1,0:T(8,128)S(1)}) custom-call(f32[32]{0:T(128)S(1)} %copy-done.9, s32[1]{0:T(128)} %bitcast.refs_1_, f32[2,16,128]{2,1,0:T(8,128)S(1)} %copy-done.5, s32[2,16,128]{2,1,0:T(8,128)S(1)} %copy-done.3, f32[3,32,16,128]{3,2,1,0:T(8,128)S(1)} %own_steps.2.refs_4_, ...), custom_call_target="tpu_custom_call" | custom-call | flops 3932160 | bytes 1572864 | tf_op jit(solution)/shard_map/join/pallas_call | solution.py:473
  40.3 1.7 %collective-permute-done.2 = f32[1,128]{1,0:T(1,128)S(1)} collective-permute-done((f32[1,128]{1,0:T(1,128)S(1)}, f32[1,128]{1,0:T(1,128)S(1)}, u32[]{:S(2)}, u32[]{:S(2)}) %collective-permute-start.2) | collective-permute-done | bytes 544 | tf_op jit(solution)/shard_map/ppermute | solution.py:498
  42.0 3.0 %collective-permute-start.4 = (f32[1,128]{1,0:T(1,128)S(1)}, f32[1,128]{1,0:T(1,128)S(1)}, u32[]{:S(2)}, u32[]{:S(2)}) collective-permute-start(f32[1,128]{1,0:T(1,128)S(1)} %add.31), channel_id=1, source_target_pairs={{0,0},{65,1},{130,2},{195,3},{260,4},{325,5},{390,6},{455,7},{8,8}... | collective-permute-start | bytes 1544 | tf_op jit(solution)/shard_map/ppermute | solution.py:514
  44.9 2.1 %join.5 = (f32[3,32,16,128]{3,2,1,0:T(8,128)S(1)}, f32[3,24,128]{2,1,0:T(8,128)S(1)}, f32[8,128]{1,0:T(8,128)S(1)}) custom-call(f32[32]{0:T(128)S(1)} %copy-done.9, s32[1]{0:T(128)S(6)} %sub.4.refs_1_, f32[2,16,128]{2,1,0:T(8,128)S(1)} %copy-done.5, s32[2,16,128]{2,1,0:T(8,128)S(1)} %copy-done.3, f32[3,32,16,128]{3,2,1,0:T(8,128)S(1)} %get-tuple-element.32.refs_4_, ...), custom_call_target="tpu_custom_call" | custom-call | flops 3932160 | bytes 1572864 | tf_op jit(solution)/shard_map/join/pallas_call | solution.py:473
  47.1 3.1 %collective-permute-start.5 = (f32[3,24,128]{2,1,0:T(8,128)S(1)}, f32[3,24,128]{2,1,0:T(8,128)S(1)}, u32[]{:S(2)}, u32[]{:S(2)}) collective-permute-start(f32[3,24,128]{2,1,0:T(8,128)S(1)} %dynamic_update_slice.6), channel_id=1, source_target_pairs={{0,1},{1,0},{2,3},{3,2},{4,5},{5,4},{6,7},{7,6},{8,9},{9,8},{10,11... | collective-permute-start | bytes 110600 | tf_op jit(solution)/shard_map/ppermute | solution.py:498
  51.1 9.6 %collective-permute-start.8 = (f32[3,24,128]{2,1,0:T(8,128)S(1)}, f32[3,24,128]{2,1,0:T(8,128)S(1)}, u32[]{:S(2)}, u32[]{:S(2)}) collective-permute-start(f32[3,24,128]{2,1,0:T(8,128)S(1)} %add.32.refs_8_), channel_id=1, source_target_pairs={{0,6},{1,7},{2,4},{3,5},{4,2},{5,3},{6,0},{7,1},{8,14},{9,15},{10,... | collective-permute-start | bytes 110600 | tf_op jit(solution)/shard_map/ppermute | solution.py:498
  60.7 2.8 %collective-permute-start.7 = (f32[3,24,128]{2,1,0:T(8,128)S(1)}, f32[3,24,128]{2,1,0:T(8,128)S(1)}, u32[]{:S(2)}, u32[]{:S(2)}) collective-permute-start(f32[3,24,128]{2,1,0:T(8,128)S(1)} %add.32.refs_8_), channel_id=1, source_target_pairs={{0,4},{1,5},{2,6},{3,7},{4,0},{5,1},{6,2},{7,3},{8,12},{9,13},{10,... | collective-permute-start | bytes 110600 | tf_op jit(solution)/shard_map/ppermute | solution.py:498
  63.5 2.2 %collective-permute-start.6 = (f32[3,24,128]{2,1,0:T(8,128)S(1)}, f32[3,24,128]{2,1,0:T(8,128)S(1)}, u32[]{:S(2)}, u32[]{:S(2)}) collective-permute-start(f32[3,24,128]{2,1,0:T(8,128)S(1)} %add.32.refs_8_), channel_id=1, source_target_pairs={{0,2},{1,3},{2,0},{3,1},{4,6},{5,7},{6,4},{7,5},{8,10},{9,11},{10,... | collective-permute-start | bytes 110600 | tf_op jit(solution)/shard_map/ppermute | solution.py:498
  66.3 1.9 %collective-permute-done.6.refs_9_ = f32[3,24,128]{2,1,0:T(8,128)S(1)} collective-permute-done((f32[3,24,128]{2,1,0:T(8,128)S(1)}, f32[3,24,128]{2,1,0:T(8,128)S(1)}, u32[]{:S(2)}, u32[]{:S(2)}) %collective-permute-start.6) | collective-permute-done | bytes 36896 | tf_op jit(solution)/shard_map/ppermute | solution.py:498
  68.2 2.8 %edge_steps.3 = (f32[11,32,128]{2,1,0:T(8,128)S(1)}, f32[11,32,128]{2,1,0:T(8,128)S(1)}, bf16[528,128]{1,0:T(8,128)(2,1)S(1)}, bf16[528,128]{1,0:T(8,128)(2,1)S(...) custom-call(f32[32]{0:T(128)S(1)} %copy-done.10, s32[1]{0:T(128)} %bitcast.refs_1_, f32[2,16,128]{2,1,0:T(8,128)S(1)} %copy-done.6, ...), custom_call_target="tpu_custom_call" | custom-call | tf_op jit(solution)/shard_map/edge_steps/pallas_call | solution.py:442
  71.1 1.9 %collective-permute-start.9 = (bf16[528,128]{1,0:T(8,128)(2,1)S(1)}, bf16[528,128]{1,0:T(8,128)(2,1)S(1)}, u32[]{:S(2)}, u32[]{:S(2)}) collective-permute-start(bf16[528,128]{1,0:T(8,128)(2,1)S(1)} %get-tuple-element.45), channel_id=1, source_target_pairs={{0,8},{8,0},{16,24},{24,16},{32,40},{40,32},{48,56},{56,48},{64,72... | collective-permute-start | bytes 405512 | tf_op jit(solution)/shard_map/ppermute | solution.py:528
  73.0 4.7 %collective-permute-start.12 = (bf16[528,128]{1,0:T(8,128)(2,1)S(1)}, bf16[528,128]{1,0:T(8,128)(2,1)S(1)}, u32[]{:S(2)}, u32[]{:S(2)}) collective-permute-start(bf16[528,128]{1,0:T(8,128)(2,1)S(1)} %get-tuple-element.48), channel_id=1, source_target_pairs={{0,504},{8,16},{16,8},{24,32},{32,24},{40,48},{48,40},{56,64},{64,... | collective-permute-start | bytes 405512 | tf_op jit(solution)/shard_map/ppermute | solution.py:529
  77.8 4.9 %collective-permute-start.10 = (f32[1,128]{1,0:T(1,128)S(1)}, f32[1,128]{1,0:T(1,128)S(1)}, u32[]{:S(2)}, u32[]{:S(2)}) collective-permute-start(f32[1,128]{1,0:T(1,128)S(1)} %fusion), channel_id=1, source_target_pairs={{0,32},{8,40},{16,48},{24,56},{32,0},{40,8},{48,16},{56,24},{64,96... | collective-permute-start | bytes 1544 | tf_op jit(solution)/shard_map/ppermute | solution.py:498
  82.7 3.1 %own_steps.3.refs_4_ = f32[3,32,16,128]{3,2,1,0:T(8,128)S(1)} custom-call(f32[32]{0:T(128)S(1)} %copy-done.10, f32[2,16,128]{2,1,0:T(8,128)S(1)} %get-tuple-element.42.speed_ref.refs_2_, s32[2,16,128]{2,1,0:T(8,128)S(1)} %copy-done.4, f32[3,32,16,128]{3,2,1,0:T(8,128)S(1)} %get-tuple-element.38.refs_5_.fields_ref, bf16[6,3,32,16,128]{4,3,2,1,0:T(8,128)(2,1)S(1)} %copy-done.1), custom_call_target="tpu_custom_call" | custom-call | flops 11796480 | bytes 2359296 | tf_op jit(solution)/shard_map/own_steps/pallas_call | solution.py:459
  86.1 2.2 %collective-permute-start.11 = (f32[1,128]{1,0:T(1,128)S(1)}, f32[1,128]{1,0:T(1,128)S(1)}, u32[]{:S(2)}, u32[]{:S(2)}) collective-permute-start(f32[1,128]{1,0:T(1,128)S(1)} %add.34), channel_id=1, source_target_pairs={{0,16},{8,24},{16,0},{24,8},{32,48},{40,56},{48,32},{56,40},{64,80... | collective-permute-start | bytes 1544 | tf_op jit(solution)/shard_map/ppermute | solution.py:498
  88.3 2.2 %join.6 = (f32[3,32,16,128]{3,2,1,0:T(8,128)S(1)}, f32[3,24,128]{2,1,0:T(8,128)S(1)}, f32[8,128]{1,0:T(8,128)S(1)}) custom-call(f32[32]{0:T(128)S(1)} %copy-done.10, s32[1]{0:T(128)} %bitcast.refs_1_, f32[2,16,128]{2,1,0:T(8,128)S(1)} %get-tuple-element.42.speed_ref.refs_2_, s32[2,16,128]{2,1,0:T(8,128)S(1)} %copy-done.4, ...), custom_call_target="tpu_custom_call" | custom-call | flops 3932160 | bytes 1572864 | tf_op jit(solution)/shard_map/join/pallas_call | solution.py:473
  90.5 1.5 %collective-permute-done.11 = f32[1,128]{1,0:T(1,128)S(1)} collective-permute-done((f32[1,128]{1,0:T(1,128)S(1)}, f32[1,128]{1,0:T(1,128)S(1)}, u32[]{:S(2)}, u32[]{:S(2)}) %collective-permute-start.11) | collective-permute-done | bytes 544 | tf_op jit(solution)/shard_map/ppermute | solution.py:498
  91.9 3.0 %collective-permute-start.13 = (f32[1,128]{1,0:T(1,128)S(1)}, f32[1,128]{1,0:T(1,128)S(1)}, u32[]{:S(2)}, u32[]{:S(2)}) collective-permute-start(f32[1,128]{1,0:T(1,128)S(1)} %add.35), channel_id=1, source_target_pairs={{0,0},{65,1},{130,2},{195,3},{260,4},{325,5},{390,6},{455,7},{8,8}... | collective-permute-start | bytes 1544 | tf_op jit(solution)/shard_map/ppermute | solution.py:514
  94.9 3.0 %join.7 = (f32[3,32,16,128]{3,2,1,0:T(8,128)}, f32[3,24,128]{2,1,0:T(8,128)S(1)}, f32[8,128]{1,0:T(8,128)S(1)}) custom-call(f32[32]{0:T(128)S(1)} %copy-done.10, s32[1]{0:T(128)S(6)} %sub.4.refs_1_, f32[2,16,128]{2,1,0:T(8,128)S(1)} %get-tuple-element.42.speed_ref.refs_2_, s32[2,16,128]{2,1,0:T(8,128)S(1)} %copy-done.4, ...), custom_call_target="tpu_custom_call" | custom-call | flops 3932160 | bytes 1572864 | tf_op jit(solution)/shard_map/join/pallas_call | solution.py:473
  97.9 4.1 %collective-permute-start.14 = (f32[3,24,128]{2,1,0:T(8,128)S(1)}, f32[3,24,128]{2,1,0:T(8,128)S(1)}, u32[]{:S(2)}, u32[]{:S(2)}) collective-permute-start(f32[3,24,128]{2,1,0:T(8,128)S(1)} %dynamic_update_slice.7), channel_id=1, source_target_pairs={{0,1},{1,0},{2,3},{3,2},{4,5},{5,4},{6,7},{7,6},{8,9},{9,8},{10,11... | collective-permute-start | bytes 110600 | tf_op jit(solution)/shard_map/ppermute | solution.py:498
  102.8 8.4 %collective-permute-start.17 = (f32[3,24,128]{2,1,0:T(8,128)S(1)}, f32[3,24,128]{2,1,0:T(8,128)S(1)}, u32[]{:S(2)}, u32[]{:S(2)}) collective-permute-start(f32[3,24,128]{2,1,0:T(8,128)S(1)} %add.36.refs_0_), channel_id=1, source_target_pairs={{0,6},{1,7},{2,4},{3,5},{4,2},{5,3},{6,0},{7,1},{8,14},{9,15},{10,... | collective-permute-start | bytes 110600 | tf_op jit(solution)/shard_map/ppermute | solution.py:498
  111.2 2.5 %collective-permute-start.16 = (f32[3,24,128]{2,1,0:T(8,128)S(1)}, f32[3,24,128]{2,1,0:T(8,128)S(1)}, u32[]{:S(2)}, u32[]{:S(2)}) collective-permute-start(f32[3,24,128]{2,1,0:T(8,128)S(1)} %add.36.refs_0_), channel_id=1, source_target_pairs={{0,4},{1,5},{2,6},{3,7},{4,0},{5,1},{6,2},{7,3},{8,12},{9,13},{10,... | collective-permute-start | bytes 110600 | tf_op jit(solution)/shard_map/ppermute | solution.py:498
  113.7 2.2 %collective-permute-start.15 = (f32[3,24,128]{2,1,0:T(8,128)S(1)}, f32[3,24,128]{2,1,0:T(8,128)S(1)}, u32[]{:S(2)}, u32[]{:S(2)}) collective-permute-start(f32[3,24,128]{2,1,0:T(8,128)S(1)} %add.36.refs_0_), channel_id=1, source_target_pairs={{0,2},{1,3},{2,0},{3,1},{4,6},{5,7},{6,4},{7,5},{8,10},{9,11},{10,... | collective-permute-start | bytes 110600 | tf_op jit(solution)/shard_map/ppermute | solution.py:498
  116.8 1.6 %collective-permute-done.15.refs_1_ = f32[3,24,128]{2,1,0:T(8,128)S(1)} collective-permute-done((f32[3,24,128]{2,1,0:T(8,128)S(1)}, f32[3,24,128]{2,1,0:T(8,128)S(1)}, u32[]{:S(2)}, u32[]{:S(2)}) %collective-permute-start.15) | collective-permute-done | bytes 36896 | tf_op jit(solution)/shard_map/ppermute | solution.py:498
  (45 shorter events, 8.3 us)
Async XLA Ops:
  0.6 1.7 %copy-start = (bf16[6,3,32,16,128]{4,3,2,1,0:T(8,128)(2,1)S(1)}, bf16[6,3,32,16,128]{4,3,2,1,0:T(8,128)(2,1)}, u32[]{:S(2)}) copy-start(bf16[6,3,32,16,128]{4,3,2,1,0:T(8,128)(2,1)} %wiener_ref.3) | copy-start | bytes 7077892
  2.3 1.1 copy-start.2
  3.4 0.7 copy-start.3
  4.2 0.7 copy-start.5
  4.9 0.7 copy-start.7
  5.6 0.7 copy-start.9
  8.9 19.0 %collective-permute-start = (bf16[528,128]{1,0:T(8,128)(2,1)S(1)}, bf16[528,128]{1,0:T(8,128)(2,1)S(1)}, u32[]{:S(2)}, u32[]{:S(2)}) collective-permute-start(bf16[528,128]{1,0:T(8,128)(2,1)S(1)} %get-tuple-element.31), channel_id=1, source_target_pairs={{0,8},{8,0},{16,24},{24,16},{32,40},{40,32},{48,56},{56,48},{64,72... | collective-permute-start | bytes 405512 | tf_op jit(solution)/shard_map/ppermute | solution.py:528
  12.8 29.1 %collective-permute-start.3 = (bf16[528,128]{1,0:T(8,128)(2,1)S(1)}, bf16[528,128]{1,0:T(8,128)(2,1)S(1)}, u32[]{:S(2)}, u32[]{:S(2)}) collective-permute-start(bf16[528,128]{1,0:T(8,128)(2,1)S(1)} %get-tuple-element.34), channel_id=1, source_target_pairs={{0,504},{8,16},{16,8},{24,32},{32,24},{40,48},{48,40},{56,64},{64,... | collective-permute-start | bytes 405512 | tf_op jit(solution)/shard_map/ppermute | solution.py:529
  27.9 8.2 %collective-permute-start.1 = (f32[1,128]{1,0:T(1,128)S(1)}, f32[1,128]{1,0:T(1,128)S(1)}, u32[]{:S(2)}, u32[]{:S(2)}) collective-permute-start(f32[1,128]{1,0:T(1,128)S(1)} %fusion.1), channel_id=1, source_target_pairs={{0,32},{8,40},{16,48},{24,56},{32,0},{40,8},{48,16},{56,24},{64,96... | collective-permute-start | bytes 1544 | tf_op jit(solution)/shard_map/ppermute | solution.py:498
  33.0 35.2 %copy-start.1 = (bf16[6,3,32,16,128]{4,3,2,1,0:T(8,128)(2,1)S(1)}, bf16[6,3,32,16,128]{4,3,2,1,0:T(8,128)(2,1)}, u32[]{:S(2)}) copy-start(bf16[6,3,32,16,128]{4,3,2,1,0:T(8,128)(2,1)} %wiener_ref.3) | copy-start | bytes 7077892
  33.0 35.2 %copy-start.4 = (s32[2,16,128]{2,1,0:T(8,128)S(1)}, s32[2,16,128]{2,1,0:T(8,128)}, u32[]{:S(2)}) copy-start(s32[2,16,128]{2,1,0:T(8,128)} %refs_3_.11) | copy-start | bytes 49156
  33.0 35.2 %copy-start.6 = (f32[2,16,128]{2,1,0:T(8,128)S(1)}, f32[2,16,128]{2,1,0:T(8,128)}, u32[]{:S(2)}) copy-start(f32[2,16,128]{2,1,0:T(8,128)} %refs_2_.7) | copy-start | bytes 49156
  33.1 35.2 %copy-start.8 = (s32[16,128]{1,0:T(8,128)S(1)}, s32[16,128]{1,0:T(8,128)}, u32[]{:S(2)}) copy-start(s32[16,128]{1,0:T(8,128)} %solid_ref.1) | copy-start | bytes 24580
  33.1 35.2 %copy-start.10 = (f32[32]{0:T(128)S(1)}, f32[32]{0:T(128)}, u32[]{:S(2)}) copy-start(f32[32]{0:T(128)} %refs_0_.11) | copy-start | bytes 388
  36.2 5.8 %collective-permute-start.2 = (f32[1,128]{1,0:T(1,128)S(1)}, f32[1,128]{1,0:T(1,128)S(1)}, u32[]{:S(2)}, u32[]{:S(2)}) collective-permute-start(f32[1,128]{1,0:T(1,128)S(1)} %add.30), channel_id=1, source_target_pairs={{0,16},{8,24},{16,0},{24,8},{32,48},{40,56},{48,32},{56,40},{64,80... | collective-permute-start | bytes 1544 | tf_op jit(solution)/shard_map/ppermute | solution.py:498
  42.0 5.1 %collective-permute-start.4 = (f32[1,128]{1,0:T(1,128)S(1)}, f32[1,128]{1,0:T(1,128)S(1)}, u32[]{:S(2)}, u32[]{:S(2)}) collective-permute-start(f32[1,128]{1,0:T(1,128)S(1)} %add.31), channel_id=1, source_target_pairs={{0,0},{65,1},{130,2},{195,3},{260,4},{325,5},{390,6},{455,7},{8,8}... | collective-permute-start | bytes 1544 | tf_op jit(solution)/shard_map/ppermute | solution.py:514
  47.1 3.9 %collective-permute-start.5 = (f32[3,24,128]{2,1,0:T(8,128)S(1)}, f32[3,24,128]{2,1,0:T(8,128)S(1)}, u32[]{:S(2)}, u32[]{:S(2)}) collective-permute-start(f32[3,24,128]{2,1,0:T(8,128)S(1)} %dynamic_update_slice.6), channel_id=1, source_target_pairs={{0,1},{1,0},{2,3},{3,2},{4,5},{5,4},{6,7},{7,6},{8,9},{9,8},{10,11... | collective-permute-start | bytes 110600 | tf_op jit(solution)/shard_map/ppermute | solution.py:498
  51.1 14.6 %collective-permute-start.8 = (f32[3,24,128]{2,1,0:T(8,128)S(1)}, f32[3,24,128]{2,1,0:T(8,128)S(1)}, u32[]{:S(2)}, u32[]{:S(2)}) collective-permute-start(f32[3,24,128]{2,1,0:T(8,128)S(1)} %add.32.refs_8_), channel_id=1, source_target_pairs={{0,6},{1,7},{2,4},{3,5},{4,2},{5,3},{6,0},{7,1},{8,14},{9,15},{10,... | collective-permute-start | bytes 110600 | tf_op jit(solution)/shard_map/ppermute | solution.py:498
  60.7 5.6 %collective-permute-start.7 = (f32[3,24,128]{2,1,0:T(8,128)S(1)}, f32[3,24,128]{2,1,0:T(8,128)S(1)}, u32[]{:S(2)}, u32[]{:S(2)}) collective-permute-start(f32[3,24,128]{2,1,0:T(8,128)S(1)} %add.32.refs_8_), channel_id=1, source_target_pairs={{0,4},{1,5},{2,6},{3,7},{4,0},{5,1},{6,2},{7,3},{8,12},{9,13},{10,... | collective-permute-start | bytes 110600 | tf_op jit(solution)/shard_map/ppermute | solution.py:498
  63.5 4.7 %collective-permute-start.6 = (f32[3,24,128]{2,1,0:T(8,128)S(1)}, f32[3,24,128]{2,1,0:T(8,128)S(1)}, u32[]{:S(2)}, u32[]{:S(2)}) collective-permute-start(f32[3,24,128]{2,1,0:T(8,128)S(1)} %add.32.refs_8_), channel_id=1, source_target_pairs={{0,2},{1,3},{2,0},{3,1},{4,6},{5,7},{6,4},{7,5},{8,10},{9,11},{10,... | collective-permute-start | bytes 110600 | tf_op jit(solution)/shard_map/ppermute | solution.py:498
  71.1 6.7 %collective-permute-start.9 = (bf16[528,128]{1,0:T(8,128)(2,1)S(1)}, bf16[528,128]{1,0:T(8,128)(2,1)S(1)}, u32[]{:S(2)}, u32[]{:S(2)}) collective-permute-start(bf16[528,128]{1,0:T(8,128)(2,1)S(1)} %get-tuple-element.45), channel_id=1, source_target_pairs={{0,8},{8,0},{16,24},{24,16},{32,40},{40,32},{48,56},{56,48},{64,72... | collective-permute-start | bytes 405512 | tf_op jit(solution)/shard_map/ppermute | solution.py:528
  73.0 18.9 %collective-permute-start.12 = (bf16[528,128]{1,0:T(8,128)(2,1)S(1)}, bf16[528,128]{1,0:T(8,128)(2,1)S(1)}, u32[]{:S(2)}, u32[]{:S(2)}) collective-permute-start(bf16[528,128]{1,0:T(8,128)(2,1)S(1)} %get-tuple-element.48), channel_id=1, source_target_pairs={{0,504},{8,16},{16,8},{24,32},{32,24},{40,48},{48,40},{56,64},{64,... | collective-permute-start | bytes 405512 | tf_op jit(solution)/shard_map/ppermute | solution.py:529
  77.8 8.4 %collective-permute-start.10 = (f32[1,128]{1,0:T(1,128)S(1)}, f32[1,128]{1,0:T(1,128)S(1)}, u32[]{:S(2)}, u32[]{:S(2)}) collective-permute-start(f32[1,128]{1,0:T(1,128)S(1)} %fusion), channel_id=1, source_target_pairs={{0,32},{8,40},{16,48},{24,56},{32,0},{40,8},{48,16},{56,24},{64,96... | collective-permute-start | bytes 1544 | tf_op jit(solution)/shard_map/ppermute | solution.py:498
  86.1 5.8 %collective-permute-start.11 = (f32[1,128]{1,0:T(1,128)S(1)}, f32[1,128]{1,0:T(1,128)S(1)}, u32[]{:S(2)}, u32[]{:S(2)}) collective-permute-start(f32[1,128]{1,0:T(1,128)S(1)} %add.34), channel_id=1, source_target_pairs={{0,16},{8,24},{16,0},{24,8},{32,48},{40,56},{48,32},{56,40},{64,80... | collective-permute-start | bytes 1544 | tf_op jit(solution)/shard_map/ppermute | solution.py:498
  91.9 6.0 %collective-permute-start.13 = (f32[1,128]{1,0:T(1,128)S(1)}, f32[1,128]{1,0:T(1,128)S(1)}, u32[]{:S(2)}, u32[]{:S(2)}) collective-permute-start(f32[1,128]{1,0:T(1,128)S(1)} %add.35), channel_id=1, source_target_pairs={{0,0},{65,1},{130,2},{195,3},{260,4},{325,5},{390,6},{455,7},{8,8}... | collective-permute-start | bytes 1544 | tf_op jit(solution)/shard_map/ppermute | solution.py:514
  97.9 4.9 %collective-permute-start.14 = (f32[3,24,128]{2,1,0:T(8,128)S(1)}, f32[3,24,128]{2,1,0:T(8,128)S(1)}, u32[]{:S(2)}, u32[]{:S(2)}) collective-permute-start(f32[3,24,128]{2,1,0:T(8,128)S(1)} %dynamic_update_slice.7), channel_id=1, source_target_pairs={{0,1},{1,0},{2,3},{3,2},{4,5},{5,4},{6,7},{7,6},{8,9},{9,8},{10,11... | collective-permute-start | bytes 110600 | tf_op jit(solution)/shard_map/ppermute | solution.py:498
  102.8 13.1 %collective-permute-start.17 = (f32[3,24,128]{2,1,0:T(8,128)S(1)}, f32[3,24,128]{2,1,0:T(8,128)S(1)}, u32[]{:S(2)}, u32[]{:S(2)}) collective-permute-start(f32[3,24,128]{2,1,0:T(8,128)S(1)} %add.36.refs_0_), channel_id=1, source_target_pairs={{0,6},{1,7},{2,4},{3,5},{4,2},{5,3},{6,0},{7,1},{8,14},{9,15},{10,... | collective-permute-start | bytes 110600 | tf_op jit(solution)/shard_map/ppermute | solution.py:498
  111.2 5.6 %collective-permute-start.16 = (f32[3,24,128]{2,1,0:T(8,128)S(1)}, f32[3,24,128]{2,1,0:T(8,128)S(1)}, u32[]{:S(2)}, u32[]{:S(2)}) collective-permute-start(f32[3,24,128]{2,1,0:T(8,128)S(1)} %add.36.refs_0_), channel_id=1, source_target_pairs={{0,4},{1,5},{2,6},{3,7},{4,0},{5,1},{6,2},{7,3},{8,12},{9,13},{10,... | collective-permute-start | bytes 110600 | tf_op jit(solution)/shard_map/ppermute | solution.py:498
  113.7 4.7 %collective-permute-start.15 = (f32[3,24,128]{2,1,0:T(8,128)S(1)}, f32[3,24,128]{2,1,0:T(8,128)S(1)}, u32[]{:S(2)}, u32[]{:S(2)}) collective-permute-start(f32[3,24,128]{2,1,0:T(8,128)S(1)} %add.36.refs_0_), channel_id=1, source_target_pairs={{0,2},{1,3},{2,0},{3,1},{4,6},{5,7},{6,4},{7,5},{8,10},{9,11},{10,... | collective-permute-start | bytes 110600 | tf_op jit(solution)/shard_map/ppermute | solution.py:498
